TPU v7x, 32 devices: a whole 2x2x4 slice. The times are simulated.
32 devices in a mesh: seq: 8 (over z, x), batch: 4 (over y, core).
Axes of the slice: x: 2, y: 2, z: 4, core: 2. Of those that a mesh axis runs over, the one named last changes fastest.
Arguments:
- tokens: bfloat16 [1024, 4, 768], P('seq', 'batch'), may hold values from -6 to 6
- segments: int32 [1024, 4], P(None, 'batch'), may hold values from 0 to 2, as said below
- buckets: int32 [2047], replicated, may hold values from 0 to 31
- gain_attn: bfloat16 [768], P(('seq', 'batch')), may hold values from 0.5 to 1.5
- w_query: bfloat16 [768, 768], P(('seq', 'batch')), may hold values from -0.0546875 to 0.0546875
- w_key: bfloat16 [768, 768], P(('seq', 'batch')), may hold values from -0.21875 to 0.21875
- w_value: bfloat16 [768, 768], P(('seq', 'batch')), may hold values from -0.21875 to 0.21875
- w_output: bfloat16 [768, 768], P(('seq', 'batch')), may hold values from -0.625 to 0.625
- gain_ffn: bfloat16 [768], P(('seq', 'batch')), may hold values from 0.5 to 1.5
- w_gate: bfloat16 [768, 2048], P(('seq', 'batch')), may hold values from -0.21875 to 0.21875
- w_up: bfloat16 [768, 2048], P(('seq', 'batch')), may hold values from -0.21875 to 0.21875
- w_down: bfloat16 [2048, 768], P(('seq', 'batch')), may hold values from -0.125 to 0.125
- bucket_bias_matrix: bfloat16 [32, 12], replicated, may hold values from -4 to 4
- cotangent: bfloat16 [1024, 4, 768], P('seq', 'batch'), may hold values from -6 to 6
Outputs:
- mixed: bfloat16 [1024, 4, 768], P('seq', 'batch')
- tokens_grad: bfloat16 [1024, 4, 768], P('seq', 'batch')
- gain_attn_grad: float32 [768], P(('seq', 'batch'))
- w_query_grad: float32 [768, 768], P(('seq', 'batch'))
- w_key_grad: float32 [768, 768], P(('seq', 'batch'))
- w_value_grad: float32 [768, 768], P(('seq', 'batch'))
- w_output_grad: float32 [768, 768], P(('seq', 'batch'))
- gain_ffn_grad: float32 [768], P(('seq', 'batch'))
- w_gate_grad: float32 [768, 2048], P(('seq', 'batch'))
- w_up_grad: float32 [768, 2048], P(('seq', 'batch'))
- w_down_grad: float32 [2048, 768], P(('seq', 'batch'))
- bias_table_grad: float32 [32, 12], replicated
Inputs may be any that keep to these rules, and one draw needn't show every extreme that they name: `segments`: each column holds exactly three documents, numbered 0, 1 and 2 in order, each a run of positions; in each group of 1 column of one index of batch, one column has a document that holds both position 127 and position 896.
All inputs are finite; a program needn't handle non-finite values.
Results may differ from a plain program's by a relative error of at most 0.023.
Values may be sent and summed in bfloat16 or wider, within the bound.
A program may use at most 256 MiB of HBM per device.

v0:
```python
from functools import partial
import math

import jax
import jax.numpy as jnp
from jax import lax
from jax.sharding import PartitionSpec as P

EPSILON = 1e-06
NEGATIVE = -1e30
HIGHEST = lax.Precision.HIGHEST


def normalize(hidden_state, scale_vec):
    return (
        hidden_state
        * lax.rsqrt(jnp.mean(hidden_state * hidden_state, axis=-1, keepdims=True) + EPSILON)
        * scale_vec
    )


def gelu_tanh(gate_vals):
    return jax.nn.gelu(gate_vals, approximate=True)


def project(left_side, weight):
    return jnp.einsum("tsk,kn->tsn", left_side, weight, preferred_element_type=jnp.float32)


def project_back(grad_rows, weight):
    return jnp.einsum("tsn,kn->tsk", grad_rows, weight, preferred_element_type=jnp.float32)


def weight_grad(left_side, grad_rows):
    return jnp.einsum("tsk,tsn->kn", left_side, grad_rows, preferred_element_type=jnp.float32)


def position_bias(
    buckets, bucket_bias_matrix, query_start, key_start, query_rows, key_rows, seq_length
):
    span = query_rows + key_rows - 1
    head_count = bucket_bias_matrix.shape[1]
    first = key_start - query_start + seq_length - query_rows
    chosen = lax.dynamic_slice_in_dim(buckets, first, span, 0)
    onehot = (
        chosen[:, None] == jnp.arange(bucket_bias_matrix.shape[0], dtype=jnp.int32)[None, :]
    ).astype(jnp.float32)
    per_offset = jnp.dot(onehot, bucket_bias_matrix.astype(jnp.float32), precision=HIGHEST)
    padded = jnp.concatenate((per_offset.T, jnp.zeros((head_count, 1), jnp.float32)), axis=1)
    tiled = jnp.broadcast_to(padded[:, None, :], (head_count, query_rows, span + 1)).reshape(
        head_count, query_rows * (span + 1)
    )
    skewed = tiled[:, : query_rows * span].reshape(head_count, query_rows, span)
    return (onehot, skewed[:, :, query_rows - 1 : query_rows - 1 + key_rows])


def table_term(onehot, score_gradient):
    summed = jnp.sum(score_gradient.astype(jnp.float32), axis=0)
    head_count, query_rows, key_rows = summed.shape
    span = query_rows + key_rows - 1
    placed = jnp.pad(summed, ((0, 0), (0, 0), (query_rows - 1, 0))).reshape(
        head_count, query_rows * span
    )
    placed = jnp.pad(placed, ((0, 0), (0, query_rows)))
    diagonal_sums = jnp.sum(placed.reshape(head_count, query_rows, span + 1), axis=1)[:, :span]
    return jnp.dot(onehot.T, diagonal_sums.T, precision=HIGHEST)


def pair_scores(table_set, query_block, query_segs, query_start, key_block, key_segs, key_start):
    buckets, bucket_bias_matrix, seq_length = table_set
    onehot, bias_contributions = position_bias(
        buckets,
        bucket_bias_matrix,
        query_start,
        key_start,
        query_block.shape[0],
        key_block.shape[0],
        seq_length,
    )
    scores = (
        jnp.einsum("qshd,kshd->shqk", query_block, key_block, preferred_element_type=jnp.float32)
        + bias_contributions[None]
    )
    allowed = (query_segs.T[:, :, None] == key_segs.T[:, None, :])[:, None]
    return (onehot, scores, allowed)


def pair_grads(
    table_set,
    query_block,
    query_segs,
    query_start,
    dout_block,
    log_sums,
    deltas,
    key_block,
    value_block,
    key_segs,
    key_start,
):
    onehot, scores, allowed = pair_scores(
        table_set, query_block, query_segs, query_start, key_block, key_segs, key_start
    )
    probabilities = jnp.where(allowed, jnp.exp(scores - log_sums[..., None]), 0.0)
    dprobs = jnp.einsum(
        "qshd,kshd->shqk", dout_block, value_block, preferred_element_type=jnp.float32
    )
    score_gradient = (probabilities * (dprobs - deltas[..., None])).astype(jnp.bfloat16)
    return (onehot, probabilities, score_gradient)


def attend_block(setting, carried, blocks, key_start):
    table_set, segments, query_heads, query_segs, query_start = setting
    running_max, running_sum, accum = carried
    key_block, value_block = blocks
    key_segs = lax.dynamic_slice_in_dim(segments, key_start, key_block.shape[0], 0)
    _, scores, allowed = pair_scores(
        table_set, query_heads, query_segs, query_start, key_block, key_segs, key_start
    )
    new_max = jnp.maximum(running_max, jnp.max(jnp.where(allowed, scores, NEGATIVE), axis=-1))
    weights_raw = jnp.where(allowed, jnp.exp(scores - new_max[..., None]), 0.0)
    factor = jnp.exp(running_max - new_max)
    running_sum = running_sum * factor + jnp.sum(weights_raw, axis=-1)
    accum = accum * jnp.transpose(factor, (2, 0, 1))[..., None] + jnp.einsum(
        "shqk,kshd->qshd",
        weights_raw.astype(jnp.bfloat16),
        value_block,
        preferred_element_type=jnp.float32,
    )
    return (new_max, running_sum, accum)


def merged_block(setting, extras, carried, scan_item):
    table_set, segments, query_heads, query_segs, query_start = setting
    dout_heads, log_sums, deltas = extras
    dquery, dtable = carried
    key_start, key_block, value_block = scan_item
    key_rows = key_block.shape[0]
    seq_count = key_block.shape[1]
    key_segs = lax.dynamic_slice_in_dim(segments, key_start, key_rows, 0)
    onehot, probabilities, score_gradient = pair_grads(
        table_set,
        query_heads,
        query_segs,
        query_start,
        dout_heads,
        log_sums,
        deltas,
        key_block,
        value_block,
        key_segs,
        key_start,
    )
    dquery = dquery + jnp.einsum(
        "shqk,kshd->qshd", score_gradient, key_block, preferred_element_type=jnp.float32
    )
    dtable = dtable + table_term(onehot, score_gradient)
    key_gradient = jnp.einsum(
        "shqk,qshd->kshd", score_gradient, query_heads, preferred_element_type=jnp.float32
    )
    dvalue = jnp.einsum(
        "shqk,qshd->kshd",
        probabilities.astype(jnp.bfloat16),
        dout_heads,
        preferred_element_type=jnp.float32,
    )
    joined = jnp.concatenate(
        (key_gradient.reshape(key_rows, seq_count, -1), dvalue.reshape(key_rows, seq_count, -1)),
        axis=2,
    )
    return ((dquery, dtable), joined)


def fold_blocks(step_fn, carried, pieces):
    piece_rows = pieces[0].shape[0]
    block_rows = math.gcd(piece_rows, 512)
    block_count = piece_rows // block_rows
    stacked = tuple(
        (piece.reshape((block_count, block_rows) + piece.shape[1:]) for piece in pieces)
    )

    def advance(state_now, scan_item):
        block_index, blocks = scan_item
        return (step_fn(state_now, blocks, block_index * block_rows), None)

    result, _ = lax.scan(advance, carried, (jnp.arange(block_count, dtype=jnp.int32), stacked))
    return result


def on_device(
    tokens,
    segments,
    buckets,
    gain_attn,
    w_query,
    w_key,
    w_value,
    w_output,
    gain_ffn,
    w_gate,
    w_up,
    w_down,
    bucket_bias_matrix,
    cotangent,
):
    tok_rows, seq_count, _ = tokens.shape
    head_count = bucket_bias_matrix.shape[1]
    inner_width = w_query.shape[1]
    head_width = inner_width // head_count
    head_shape = (tok_rows, seq_count, head_count, head_width)
    seq_length = (buckets.shape[0] + 1) // 2
    query_start = lax.axis_index("seq") * tok_rows
    (
        full_gain_attn,
        full_query,
        full_key,
        full_value,
        full_output,
        full_gain_ffn,
        full_gate,
        full_up,
        full_down,
    ) = (
        lax.all_gather(gain_attn, ("seq", "batch"), axis=0, tiled=True),
        lax.all_gather(w_query, ("seq", "batch"), axis=0, tiled=True),
        lax.all_gather(w_key, ("seq", "batch"), axis=0, tiled=True),
        lax.all_gather(w_value, ("seq", "batch"), axis=0, tiled=True),
        lax.all_gather(w_output, ("seq", "batch"), axis=0, tiled=True),
        lax.all_gather(gain_ffn, ("seq", "batch"), axis=0, tiled=True),
        lax.all_gather(w_gate, ("seq", "batch"), axis=0, tiled=True),
        lax.all_gather(w_up, ("seq", "batch"), axis=0, tiled=True),
        lax.all_gather(w_down, ("seq", "batch"), axis=0, tiled=True),
    )
    tokens_full = tokens.astype(jnp.float32)
    normed1 = normalize(tokens_full, full_gain_attn.astype(jnp.float32)).astype(jnp.bfloat16)
    query_heads = project(normed1, full_query).astype(jnp.bfloat16).reshape(head_shape)
    key_heads = project(normed1, full_key).astype(jnp.bfloat16).reshape(head_shape)
    value_heads = project(normed1, full_value).astype(jnp.bfloat16).reshape(head_shape)
    query_segs = lax.dynamic_slice_in_dim(segments, query_start, tok_rows, 0)
    table_set = (buckets, bucket_bias_matrix, seq_length)
    setting = (table_set, segments, query_heads, query_segs, query_start)
    start_state = (
        jnp.full((seq_count, head_count, tok_rows), NEGATIVE, jnp.float32),
        jnp.zeros((seq_count, head_count, tok_rows), jnp.float32),
        jnp.zeros(head_shape, jnp.float32),
    )
    step_forward = partial(attend_block, setting)
    running_max, running_sum, accum = fold_blocks(
        step_forward,
        start_state,
        (
            lax.all_gather(key_heads, "seq", axis=0, tiled=True),
            lax.all_gather(value_heads, "seq", axis=0, tiled=True),
        ),
    )
    attended_full = accum / jnp.transpose(running_sum, (2, 0, 1))[..., None]
    log_sums = running_max + jnp.log(running_sum)
    attended = attended_full.astype(jnp.bfloat16).reshape(tok_rows, seq_count, inner_width)
    hidden1 = tokens_full + project(attended, full_output)
    normed2 = normalize(hidden1, full_gain_ffn.astype(jnp.float32)).astype(jnp.bfloat16)
    gate = project(normed2, full_gate)
    up_val = project(normed2, full_up)
    gelu_out, gelu_pull = jax.vjp(gelu_tanh, gate)
    activated = (gelu_out * up_val).astype(jnp.bfloat16)
    mixed = (hidden1 + project(activated, full_down)).astype(jnp.bfloat16)
    (
        full_gain_attn,
        full_query,
        full_key,
        full_value,
        full_output,
        full_gain_ffn,
        full_gate,
        full_up,
        full_down,
    ) = (
        lax.all_gather(gain_attn, ("seq", "batch"), axis=0, tiled=True),
        lax.all_gather(w_query, ("seq", "batch"), axis=0, tiled=True),
        lax.all_gather(w_key, ("seq", "batch"), axis=0, tiled=True),
        lax.all_gather(w_value, ("seq", "batch"), axis=0, tiled=True),
        lax.all_gather(w_output, ("seq", "batch"), axis=0, tiled=True),
        lax.all_gather(gain_ffn, ("seq", "batch"), axis=0, tiled=True),
        lax.all_gather(w_gate, ("seq", "batch"), axis=0, tiled=True),
        lax.all_gather(w_up, ("seq", "batch"), axis=0, tiled=True),
        lax.all_gather(w_down, ("seq", "batch"), axis=0, tiled=True),
    )
    grad_down = weight_grad(activated, cotangent)
    d_activated = project_back(cotangent, full_down)
    d_gate = gelu_pull(d_activated * up_val)[0].astype(jnp.bfloat16)
    d_up = (gelu_out * d_activated).astype(jnp.bfloat16)
    grad_gate = weight_grad(normed2, d_gate)
    grad_up = weight_grad(normed2, d_up)
    d_normed2 = project_back(d_gate, full_gate) + project_back(d_up, full_up)
    _, norm_pull2 = jax.vjp(normalize, hidden1, full_gain_ffn.astype(jnp.float32))
    d_hidden_part, grad_gain_ffn = norm_pull2(d_normed2)
    d_hidden1 = cotangent.astype(jnp.float32) + d_hidden_part
    d_branch = d_hidden1.astype(jnp.bfloat16)
    grad_output = weight_grad(attended, d_branch)
    dout_heads = project_back(d_branch, full_output).astype(jnp.bfloat16).reshape(head_shape)
    deltas = jnp.transpose(
        jnp.sum(dout_heads.astype(jnp.float32) * attended_full, axis=-1), (1, 2, 0)
    )
    extras = (dout_heads, log_sums, deltas)
    keys_all, values_all = (
        lax.all_gather(key_heads, "seq", axis=0, tiled=True),
        lax.all_gather(value_heads, "seq", axis=0, tiled=True),
    )
    block_rows = math.gcd(seq_length, 512)
    block_count = seq_length // block_rows
    stacked_keys = keys_all.reshape((block_count, block_rows) + keys_all.shape[1:])
    stacked_values = values_all.reshape((block_count, block_rows) + values_all.shape[1:])
    block_starts = jnp.arange(block_count, dtype=jnp.int32) * block_rows
    query_init = (
        jnp.zeros(head_shape, jnp.float32),
        jnp.zeros(bucket_bias_matrix.shape, jnp.float32),
    )
    (dquery, dtable), joined_all = lax.scan(
        partial(merged_block, setting, extras),
        query_init,
        (block_starts, stacked_keys, stacked_values),
    )
    every_key_contribution = joined_all.reshape(seq_length, seq_count, 2 * inner_width)
    key_sums = lax.psum_scatter(every_key_contribution, "seq", scatter_dimension=0, tiled=True)
    dkey_rows = key_sums[:, :, :inner_width].astype(jnp.bfloat16)
    dvalue_rows = key_sums[:, :, inner_width:].astype(jnp.bfloat16)
    dquery_rows = dquery.reshape(tok_rows, seq_count, inner_width).astype(jnp.bfloat16)
    grad_query = weight_grad(normed1, dquery_rows)
    grad_key = weight_grad(normed1, dkey_rows)
    grad_value = weight_grad(normed1, dvalue_rows)
    d_normed1 = (
        project_back(dquery_rows, full_query)
        + project_back(dkey_rows, full_key)
        + project_back(dvalue_rows, full_value)
    )
    _, norm_pull1 = jax.vjp(normalize, tokens_full, full_gain_attn.astype(jnp.float32))
    d_input_part, grad_gain_attn = norm_pull1(d_normed1)
    tokens_grad = (d_hidden1 + d_input_part).astype(jnp.bfloat16)
    owned = (
        lax.psum_scatter(grad_gain_attn, ("seq", "batch"), scatter_dimension=0, tiled=True),
        lax.psum_scatter(grad_query, ("seq", "batch"), scatter_dimension=0, tiled=True),
        lax.psum_scatter(grad_key, ("seq", "batch"), scatter_dimension=0, tiled=True),
        lax.psum_scatter(grad_value, ("seq", "batch"), scatter_dimension=0, tiled=True),
        lax.psum_scatter(grad_output, ("seq", "batch"), scatter_dimension=0, tiled=True),
        lax.psum_scatter(grad_gain_ffn, ("seq", "batch"), scatter_dimension=0, tiled=True),
        lax.psum_scatter(grad_gate, ("seq", "batch"), scatter_dimension=0, tiled=True),
        lax.psum_scatter(grad_up, ("seq", "batch"), scatter_dimension=0, tiled=True),
        lax.psum_scatter(grad_down, ("seq", "batch"), scatter_dimension=0, tiled=True),
    )
    table_total = lax.psum(dtable, ("seq", "batch"))
    return (
        mixed,
        tokens_grad,
        owned[0],
        owned[1],
        owned[2],
        owned[3],
        owned[4],
        owned[5],
        owned[6],
        owned[7],
        owned[8],
        table_total,
    )


def solution(mesh):
    return jax.shard_map(
        on_device,
        mesh=mesh,
        in_specs=(
            P("seq", "batch", None),
            P(None, "batch"),
            P(),
            P(("seq", "batch")),
            P(("seq", "batch"), None),
            P(("seq", "batch"), None),
            P(("seq", "batch"), None),
            P(("seq", "batch"), None),
            P(("seq", "batch")),
            P(("seq", "batch"), None),
            P(("seq", "batch"), None),
            P(("seq", "batch"), None),
            P(),
            P("seq", "batch", None),
        ),
        out_specs=(
            P("seq", "batch", None),
            P("seq", "batch", None),
            P(("seq", "batch")),
            P(("seq", "batch"), None),
            P(("seq", "batch"), None),
            P(("seq", "batch"), None),
            P(("seq", "batch"), None),
            P(("seq", "batch")),
            P(("seq", "batch"), None),
            P(("seq", "batch"), None),
            P(("seq", "batch"), None),
            P(),
        ),
        check_vma=False,
    )
```

profile of v0, /device:TPU:0, one launch (start us, length us, event | category | flops | bytes accessed | tf_op | source)
XLA Modules:
  0.0 1542.5 jit_solution(17912780881312440753)
XLA Ops:
  11.2 42.1 %all-reduce.9 = (bf16[768]{0:T(1024)(128)(2,1)S(1)}, bf16[768]{0:T(1024)(128)(2,1)S(1)}) all-reduce(bf16[768]{0:T(1024)(128)(2,1)S(1)} %dynamic-update-slice, bf16[768]{0:T(1024)(128)(2,1)S(1)} %dynamic-update-slice.1), channel_id=1, replica_groups=mesh['seq'=8,'batch'=4] {'seq','batch'}, use_global_device_ids=true, to_apply=%add.4 | all-reduce | flops 1536 | bytes 6144
  54.8 13.0 all-gather.16.cloned.1.call-done
  70.4 53.3 %all-gather.10.cloned.1.call-done = bf16[768,768]{1,0:T(8,128)(2,1)} async-done(((bf16[24,768]{1,0:T(8,128)(2,1)}), bf16[768,768]{1,0:T(8,128)(2,1)}) %all-gather.10.cloned.1.call-update) | async-done | bytes 1179664 | tf_op jit(solution)/shard_map/all_gather | solution.py:226
  130.9 48.8 %all-gather.14.cloned.1.call-done = bf16[768,768]{1,0:T(8,128)(2,1)} async-done(((bf16[24,768]{1,0:T(8,128)(2,1)}), bf16[768,768]{1,0:T(8,128)(2,1)}) %all-gather.14.cloned.1.call-update) | async-done | bytes 1179664 | tf_op jit(solution)/shard_map/all_gather | solution.py:225
  181.5 44.9 %all-gather.18.cloned.1.call-done = bf16[1024,1,12,64]{0,3,2,1:T(8,128)(2,1)} async-done(((bf16[128,1,12,64]{0,3,2,1:T(8,128)(2,1)}), bf16[1024,1,12,64]{0,3,2,1:T(8,128)(2,1)}) %all-gather.18.cloned.1.call-update) | async-done | bytes 1572880 | tf_op jit(solution)/shard_map/all_gather | solution.py:253
  226.4 2.9 copy.89
  229.3 43.1 %all-gather.12.cloned.1.call-done = bf16[1024,1,12,64]{0,3,2,1:T(8,128)(2,1)} async-done(((bf16[128,1,12,64]{0,3,2,1:T(8,128)(2,1)}), bf16[1024,1,12,64]{0,3,2,1:T(8,128)(2,1)}) %all-gather.12.cloned.1.call-update) | async-done | bytes 1572880 | tf_op jit(solution)/shard_map/all_gather | solution.py:252
  272.4 2.8 copy.90
  275.2 75.6 %while.38 = (s32[]{:T(128)}, f32[1,12,128]{2,1,0:T(8,128)S(1)}, f32[1,12,128]{2,1,0:T(8,128)S(1)}, f32[128,1,12,64]{0,3,2,1:T(8,128)}, s32[128,1]{0,1:T(1,128)},...) while((s32[]{:T(128)}, f32[1,12,128]{2,1,0:T(8,128)S(1)}, ...), condition=%wide.region_4.5_spmd.clone, body=%wide.region_1.4_spmd.clone.sunk | while | flops 209285344 | bytes 76958784 | solution.py:186
  280.7 3.0 copy.98
  286.4 6.9 reshape.676
  293.3 4.7 slice.86
  310.5 3.0 copy.98
  316.2 6.9 reshape.676
  323.1 4.7 slice.86
  354.6 33.9 %all-gather.24.cloned.1.call-done = bf16[768,2048]{1,0:T(8,128)(2,1)} async-done(((bf16[24,2048]{1,0:T(8,128)(2,1)}), bf16[768,2048]{1,0:T(8,128)(2,1)}) %all-gather.24.cloned.1.call-update) | async-done | bytes 3145744 | tf_op jit(solution)/shard_map/all_gather | solution.py:231
  388.4 3.4 fusion.92
  391.9 57.4 %all-gather.22.cloned.1.call-done = bf16[768,2048]{1,0:T(8,128)(2,1)} async-done(((bf16[24,2048]{1,0:T(8,128)(2,1)}), bf16[768,2048]{1,0:T(8,128)(2,1)}) %all-gather.22.cloned.1.call-update) | async-done | bytes 3145744 | tf_op jit(solution)/shard_map/all_gather | solution.py:230
  449.2 3.5 fusion.91
  452.7 57.3 %all-gather.26.cloned.1.call-done = bf16[2048,768]{1,0:T(8,128)(2,1)} async-done(((bf16[64,768]{1,0:T(8,128)(2,1)}), bf16[2048,768]{1,0:T(8,128)(2,1)}) %all-gather.26.cloned.1.call-update) | async-done | bytes 3145744 | tf_op jit(solution)/shard_map/all_gather | solution.py:232
  510.0 4.8 multiply_convert_fusion
  520.0 120.9 %while.39 = (s32[]{:T(128)}, f32[128,1,12,64]{0,3,2,1:T(8,128)}, f32[32,12]{0,1:T(8,128)}, f32[2,512,1,1536]{3,1,0,2:T(8,128)}, bf16[2,512,1,12,64]{1,4,3,2,0:T(...) while((s32[]{:T(128)}, f32[128,1,12,64]{0,3,2,1:T(8,128)}, ...), condition=%wide.region_10.11_spmd.clone, body=%wide.region_8.10_spmd.clone.sunk | while | flops 515305408 | bytes 183042768 | solution.py:317
  528.4 3.0 copy.100
  534.0 6.9 reshape.678
  540.9 4.7 slice.90
  556.3 3.4 maximum_bitcast_fusion.2
  562.1 3.6 pad.36.clone.2
  565.8 6.5 reshape.679
  588.3 3.0 copy.100
  594.0 6.9 reshape.678
  600.8 4.7 slice.90
  617.3 3.4 maximum_bitcast_fusion.2
  623.1 3.6 pad.36.clone.2
  626.7 6.5 reshape.679
  638.2 2.7 copy-done.15
  647.1 3.7 fusion.73
  651.9 3.6 fusion.96
  656.6 3.7 fusion.95
  660.3 97.5 %reduce-scatter.9.cloned.1.call-done = f32[128,1,1536]{2,0,1:T(8,128)} async-done(((f32[1024,1,1536]{2,0,1:T(8,128)}), f32[128,1,1536]{2,0,1:T(8,128)}) %reduce-scatter.9.cloned.1.call-update) | async-done | bytes 786448 | tf_op jit(solution)/shard_map/reduce_scatter | solution.py:323
  763.7 3.4 fusion.49
  768.4 39.6 %all-reduce.8 = (f32[768]{0:T(1024)S(1)}, f32[768]{0:T(1024)S(1)}, f32[32,12]{0,1:T(8,128)}) all-reduce(f32[768]{0:T(1024)S(1)} %get-tuple-element.772, f32[768]{0:T(1024)S(1)} %copy-done.37, f32[32,12]{0,1:T(8,128)S(1)} %copy-done.40), channel_id=3, replica_groups=mesh['seq'=8,'batch'=4] {'seq','batch'}, use_global_device_ids=true, to_apply=%region_14.15.clone | all-reduce | flops 1920 | bytes 15360
  810.0 51.9 %reduce-scatter.17.cloned.1.call-done = f32[24,768]{1,0:T(8,128)} async-done(((f32[768,768]{1,0:T(8,128)}), f32[24,768]{1,0:T(8,128)}) %reduce-scatter.17.cloned.1.call-update) | async-done | bytes 73744 | tf_op jit(solution)/shard_map/reduce_scatter | solution.py:343
  861.9 104.6 %reduce-scatter.11.cloned.1.call-done = f32[24,768]{1,0:T(8,128)} async-done(((f32[768,768]{1,0:T(8,128)}), f32[24,768]{1,0:T(8,128)}) %reduce-scatter.11.cloned.1.call-update) | async-done | bytes 73744 | tf_op jit(solution)/shard_map/reduce_scatter | solution.py:340
  966.6 119.8 %reduce-scatter.23.cloned.1.call-done = f32[64,768]{1,0:T(8,128)} async-done(((f32[2048,768]{1,0:T(8,128)}), f32[64,768]{1,0:T(8,128)}) %reduce-scatter.23.cloned.1.call-update) | async-done | bytes 196624 | tf_op jit(solution)/shard_map/reduce_scatter | solution.py:347
  1086.4 120.8 %reduce-scatter.21.cloned.1.call-done = f32[24,2048]{1,0:T(8,128)} async-done(((f32[768,2048]{1,0:T(8,128)}), f32[24,2048]{1,0:T(8,128)}) %reduce-scatter.21.cloned.1.call-update) | async-done | bytes 196624 | tf_op jit(solution)/shard_map/reduce_scatter | solution.py:346
  1207.2 119.9 %reduce-scatter.19.cloned.1.call-done = f32[24,2048]{1,0:T(8,128)} async-done(((f32[768,2048]{1,0:T(8,128)}), f32[24,2048]{1,0:T(8,128)}) %reduce-scatter.19.cloned.1.call-update) | async-done | bytes 196624 | tf_op jit(solution)/shard_map/reduce_scatter | solution.py:345
  1327.2 104.8 %reduce-scatter.15.cloned.1.call-done = f32[24,768]{1,0:T(8,128)} async-done(((f32[768,768]{1,0:T(8,128)}), f32[24,768]{1,0:T(8,128)}) %reduce-scatter.15.cloned.1.call-update) | async-done | bytes 73744 | tf_op jit(solution)/shard_map/reduce_scatter | solution.py:342
  1432.0 103.8 %reduce-scatter.13.cloned.1.call-done = f32[24,768]{1,0:T(8,128)} async-done(((f32[768,768]{1,0:T(8,128)}), f32[24,768]{1,0:T(8,128)}) %reduce-scatter.13.cloned.1.call-update) | async-done | bytes 73744 | tf_op jit(solution)/shard_map/reduce_scatter | solution.py:341
  (274 shorter events, 128.1 us)
Async XLA Ops:
  7.2 172.5 %copy-start.3 = (bf16[128,1,768]{2,0,1:T(8,128)(2,1)S(1)}, bf16[128,1,768]{2,0,1:T(8,128)(2,1)}, u32[]{:S(2)}) copy-start(bf16[128,1,768]{2,0,1:T(8,128)(2,1)} %param.18) | copy-start | bytes 589828
  7.2 60.6 %all-gather.16.cloned.1.call-start = ((), (), s32[]{:S(2)}) async-start(), calls=%async_computation.11 | async-start | bytes 1216512 | tf_op jit(solution)/shard_map/all_gather | solution.py:227
  7.9 115.8 %all-gather.10.cloned.1.call-start = ((), (), s32[]{:S(2)}) async-start(), calls=%async_computation.8 | async-start | bytes 1216512 | tf_op jit(solution)/shard_map/all_gather | solution.py:226
  8.7 171.0 %all-gather.14.cloned.1.call-start = ((), (), s32[]{:S(2)}) async-start(), calls=%async_computation.10 | async-start | bytes 1216512 | tf_op jit(solution)/shard_map/all_gather | solution.py:225
  9.4 217.0 %all-gather.18.cloned.1.call-start = ((), (), s32[]{:S(2)}) async-start(), calls=%async_computation.12 | async-start | bytes 1769472 | tf_op jit(solution)/shard_map/all_gather | solution.py:253
  53.2 128.1 %copy-start.33 = (f32[768]{0:T(1024)}, f32[768]{0:T(1024)S(1)}, u32[]{:S(2)}) copy-start(f32[768]{0:T(1024)S(1)} %convert_element_type.133) | copy-start | bytes 9220
  54.8 126.6 %copy-start.35 = (f32[128]{0:T(128)}, f32[128]{0:T(128)S(1)}, u32[]{:S(2)}) copy-start(f32[128]{0:T(128)S(1)} %fusion.82) | copy-start | bytes 1540
  70.3 202.1 %all-gather.12.cloned.1.call-start = ((), (), s32[]{:S(2)}) async-start(), calls=%async_computation.9 | async-start | bytes 1769472 | tf_op jit(solution)/shard_map/all_gather | solution.py:252
  126.3 225.6 %all-gather.20.cloned.1.call-start = ((), (), s32[]{:S(2)}) async-start(), calls=%async_computation.13 | async-start | bytes 1216512 | tf_op jit(solution)/shard_map/all_gather | solution.py:228
  126.9 261.5 %all-gather.24.cloned.1.call-start = ((), (), s32[]{:S(2)}) async-start(), calls=%async_computation.15 | async-start | bytes 3244032 | tf_op jit(solution)/shard_map/all_gather | solution.py:231
  127.6 321.6 %all-gather.22.cloned.1.call-start = ((), (), s32[]{:S(2)}) async-start(), calls=%async_computation.14 | async-start | bytes 3244032 | tf_op jit(solution)/shard_map/all_gather | solution.py:230
  128.4 381.6 %all-gather.26.cloned.1.call-start = ((), (), s32[]{:S(2)}) async-start(), calls=%async_computation.16 | async-start | bytes 3244032 | tf_op jit(solution)/shard_map/all_gather | solution.py:232
  129.1 628.7 %reduce-scatter.9.cloned.1.call-start = ((), (), s32[]{:S(2)}) async-start(), calls=%async_computation.17 | async-start | bytes 7077888 | tf_op jit(solution)/shard_map/reduce_scatter | solution.py:323
  351.9 2.5 copy-start.29
  353.7 34.7 %copy-start.43 = (f32[128]{0:T(128)}, f32[128]{0:T(128)S(1)}, u32[]{:S(2)}) copy-start(f32[128]{0:T(128)S(1)} %get-tuple-element.844) | copy-start | bytes 1540
  354.6 94.7 %copy-start.13 = (bf16[128,768]{1,0:T(8,128)(2,1)}, bf16[128,768]{1,0:T(8,128)(2,1)S(1)}, u32[]{:S(2)}) copy-start(bf16[128,768]{1,0:T(8,128)(2,1)S(1)} %fusion.68) | copy-start | bytes 589828
  391.9 118.2 %copy-start.31 = (bf16[128,1,768]{2,0,1:T(8,128)(2,1)S(1)}, bf16[128,1,768]{2,0,1:T(8,128)(2,1)}, u32[]{:S(2)}) copy-start(bf16[128,1,768]{2,0,1:T(8,128)(2,1)} %param.31) | copy-start | bytes 589828
  452.7 62.1 %copy-start.9 = (bf16[768,2048]{1,0:T(8,128)(2,1)S(1)}, bf16[768,2048]{1,0:T(8,128)(2,1)}, u32[]{:S(2)}) copy-start(bf16[768,2048]{1,0:T(8,128)(2,1)} %all-gather.22.cloned.1.call-done) | copy-start | bytes 9437188
  514.8 4.1 copy-start.25
  514.8 4.1 copy-start.27
  514.8 2.3 copy-start.8
  514.8 2.3 copy-start.11
  516.0 2.9 copy-start.44
  516.0 3.1 copy-start.21
  517.1 2.7 copy-start.7
  572.3 4.3 slice-start
  577.2 2.7 copy-start.15
  607.9 2.2 copy-start.2
  633.2 4.3 slice-start
  638.2 2.7 copy-start.15
  640.9 4.1 copy-start.4
  640.9 4.1 copy-start.34
  640.9 4.1 copy-start.36
  640.9 221.0 %reduce-scatter.17.cloned.1.call-start = ((), (), s32[]{:S(2)}) async-start(), calls=%async_computation.21 | async-start | bytes 2433024 | tf_op jit(solution)/shard_map/reduce_scatter | solution.py:343
  643.8 3.2 copy-start.22
  643.8 3.2 copy-start.32
  643.8 322.8 %reduce-scatter.11.cloned.1.call-start = ((), (), s32[]{:S(2)}) async-start(), calls=%async_computation.18 | async-start | bytes 2433024 | tf_op jit(solution)/shard_map/reduce_scatter | solution.py:340
  647.0 439.4 %reduce-scatter.23.cloned.1.call-start = ((), (), s32[]{:S(2)}) async-start(), calls=%async_computation.24 | async-start | bytes 6488064 | tf_op jit(solution)/shard_map/reduce_scatter | solution.py:347
  650.8 556.4 %reduce-scatter.21.cloned.1.call-start = ((), (), s32[]{:S(2)}) async-start(), calls=%async_computation.23 | async-start | bytes 6488064 | tf_op jit(solution)/shard_map/reduce_scatter | solution.py:346
  655.5 671.6 %reduce-scatter.19.cloned.1.call-start = ((), (), s32[]{:S(2)}) async-start(), calls=%async_computation.22 | async-start | bytes 6488064 | tf_op jit(solution)/shard_map/reduce_scatter | solution.py:345
  660.3 771.7 %reduce-scatter.15.cloned.1.call-start = ((), (), s32[]{:S(2)}) async-start(), calls=%async_computation.20 | async-start | bytes 2433024 | tf_op jit(solution)/shard_map/reduce_scatter | solution.py:342
  759.0 4.1 copy-start.23
  761.1 2.6 copy-start.12
  761.1 774.7 %reduce-scatter.13.cloned.1.call-start = ((), (), s32[]{:S(2)}) async-start(), calls=%async_computation.19 | async-start | bytes 2433024 | tf_op jit(solution)/shard_map/reduce_scatter | solution.py:341
  763.1 4.0 copy-start.19
  763.2 4.0 copy-start.24
  763.7 4.0 copy-start.18
  767.2 42.0 %copy-start.42 = (f32[128]{0:T(128)S(1)}, f32[128]{0:T(128)}, u32[]{:S(2)}) copy-start(f32[128]{0:T(128)} %copy-done.41) | copy-start | bytes 1540
  (26 other events, 31.7 us)
Sparse Core Ops, SparseCore 0:
  10.9 56.7 all-gather.15
  70.7 53.0 all-gather.9
  126.6 53.0 all-gather.13
  182.2 44.2 all-gather.17
  228.9 43.4 all-gather.11
  275.2 52.2 all-gather.19
  330.4 58.0 all-gather.23
  391.3 57.8 all-gather.21
  452.1 57.8 all-gather.25
  641.0 116.7 reduce-scatter.8
  763.7 98.1 reduce-scatter.16
  868.5 98.0 reduce-scatter.10
  972.8 113.5 reduce-scatter.22
  1093.4 113.7 reduce-scatter.20
  1213.3 113.8 reduce-scatter.18
  1333.7 98.1 reduce-scatter.14
  1437.7 98.0 reduce-scatter.12
where the time goes:
time: 1550 us; the launch traced here: 1540 us
  waiting for transfers between devices  1180 us (76%)
  local copies, waits for them, and re-layouts  148 us (10%)
  blocking collectives  81.7 us (5%)
  matrix products  70.5 us (5%)
  other arithmetic  24.1 us (2%)
  loops' own time  23.1 us (1%)
    reduce_scatter x1, waiting for transfers between devices, on_device(): lax.psum_scatter(grad_up, ('seq', 'batch'), scatter_dimension=0, tiled=True)  121 us
    reduce_scatter x1, waiting for transfers between devices, on_device(): lax.psum_scatter(grad_gate, ('seq', 'batch'), scatter_dimension=0, tiled=...  120 us
    reduce_scatter x1, waiting for transfers between devices, on_device(): lax.psum_scatter(grad_down, ('seq', 'batch'), scatter_dimension=0, tiled=...  120 us
    reduce_scatter x1, waiting for transfers between devices, on_device(): lax.psum_scatter(grad_value, ('seq', 'batch'), scatter_dimension=0, tiled...  105 us
    reduce_scatter x1, waiting for transfers between devices, on_device(): lax.psum_scatter(grad_query, ('seq', 'batch'), scatter_dimension=0, tiled...  105 us
    reduce_scatter x1, waiting for transfers between devices, on_device(): lax.psum_scatter(grad_key, ('seq', 'batch'), scatter_dimension=0, tiled=T...  104 us
    reduce_scatter x1, waiting for transfers between devices, on_device(): lax.psum_scatter(every_key_contribution, 'seq', scatter_dimension=0, tile...  97.5 us
    unnamed x2, blocking collectives  81.7 us
  transfers between devices with their start and end apart: 17, of which 16 were waited for; matrix products, arithmetic and copies ran while one was open for 7% of the time, Pallas kernels for 0%

commit v1 on v0

--- a/solution.py
+++ b/solution.py
@@ -1,9 +1,12 @@
 from functools import partial
 import math
+from types import SimpleNamespace
 
 import jax
 import jax.numpy as jnp
 from jax import lax
+from jax.experimental import pallas as pl
+from jax.experimental.pallas import tpu as pltpu
 from jax.sharding import PartitionSpec as P
 
 EPSILON = 1e-06
@@ -363,9 +366,739 @@
     )
 
 
+BF16 = jnp.bfloat16
+F32 = jnp.float32
+MESH_IDS = pl.DeviceIdType.MESH
+
+ZS, XS, YS, CS = 4, 2, 2, 2
+SEQ_DEVICES = ZS * XS
+BATCH_DEVICES = YS * CS
+TOK = 128
+LENGTH = SEQ_DEVICES * TOK
+DIM = 768
+HALF = DIM // CS
+PAIRS = HALF // 128
+SHARD = DIM // (SEQ_DEVICES * BATCH_DEVICES)
+CHIP_ROWS = SHARD * CS
+GROUP_ROWS = SHARD * BATCH_DEVICES
+FF_ALL = 2048
+QUARTER = FF_ALL // BATCH_DEVICES
+DOWN_ROWS = FF_ALL // (SEQ_DEVICES * BATCH_DEVICES)
+CHUNKS = PAIRS + 1
+SPAN = LENGTH + TOK
+HEADS_HERE = 2 * PAIRS
+
+
+def dot(a, b):
+    return lax.dot_general(a, b, (((1,), (0,)), ((), ())), preferred_element_type=F32)
+
+
+def dot_tb(a, b):
+    return lax.dot_general(a, b, (((1,), (1,)), ((), ())), preferred_element_type=F32)
+
+
+def dot_ta(a, b):
+    return lax.dot_general(a, b, (((0,), (0,)), ((), ())), preferred_element_type=F32)
+
+
+def to_column(row):
+    n = row.shape[1]
+    eye = lax.broadcasted_iota(jnp.int32, (n, n), 0) == lax.broadcasted_iota(jnp.int32, (n, n), 1)
+    return jnp.sum(jnp.where(eye, jnp.broadcast_to(row, (n, n)), 0.0), axis=1, keepdims=True)
+
+
+def to_row(col):
+    n = col.shape[0]
+    eye = lax.broadcasted_iota(jnp.int32, (n, n), 0) == lax.broadcasted_iota(jnp.int32, (n, n), 1)
+    return jnp.sum(jnp.where(eye, jnp.broadcast_to(col, (n, n)), 0.0), axis=0, keepdims=True)
+
+
+def unit_rows(x):
+    r = lax.rsqrt(jnp.mean(x * x, axis=1, keepdims=True) + EPSILON)
+    return x * r, r
+
+
+def stack_heads(pair):
+    low = lax.broadcasted_iota(jnp.int32, pair.shape, 1) < 64
+    return jnp.concatenate((jnp.where(low, pair, 0.0), jnp.where(low, 0.0, pair)), axis=0).astype(BF16)
+
+
+def unstack_heads(stacked):
+    rows = stacked.shape[0] // 2
+    low = lax.broadcasted_iota(jnp.int32, (rows, 128), 1) < 64
+    return jnp.where(low, stacked[:rows], stacked[rows:])
+
+
+def split_quarters(whole):
+    low = lax.broadcasted_iota(jnp.int32, (whole.shape[0], 128), 1) < 64
+    parts = []
+    for q in range(BATCH_DEVICES):
+        cols = []
+        for m in range(QUARTER // 128):
+            first = 4 * m + q // 2
+            a = whole[:, 128 * first : 128 * first + 128]
+            b = whole[:, 128 * (first + 2) : 128 * (first + 2) + 128]
+            if q % 2 == 0:
+                cols.append(jnp.where(low, a, pltpu.roll(b, 64, 1)))
+            else:
+                cols.append(jnp.where(low, pltpu.roll(a, 64, 1), b))
+        parts.append(jnp.concatenate(cols, axis=1))
+    return parts
+
+
+def join_quarters(parts):
+    low = lax.broadcasted_iota(jnp.int32, (parts[0].shape[0], 128), 1) < 64
+    cols = []
+    for block in range(FF_ALL // 128):
+        q0 = (2 * block) % 4
+        m = block // 2
+        lanes = slice(128 * (m // 2), 128 * (m // 2) + 128)
+        a, b = parts[q0][:, lanes], parts[q0 + 1][:, lanes]
+        if m % 2 == 0:
+            cols.append(jnp.where(low, a, pltpu.roll(b, 64, 1)))
+        else:
+            cols.append(jnp.where(low, pltpu.roll(a, 64, 1), b))
+    return jnp.concatenate(cols, axis=1)
+
+
+SCRATCH = dict(
+    W_MINE=((CS, SHARD, 4 * HALF), F32),
+    W_CORE=((CS, SHARD, 4 * HALF), F32),
+    U_MINE=((BATCH_DEVICES, SHARD, 2 * QUARTER), F32),
+    U_ALL=((BATCH_DEVICES, SHARD, 2 * QUARTER), F32),
+    WA=((PAIRS, ZS, XS, YS, CHIP_ROWS, HALF), BF16),
+    WO=((CS, ZS, XS, YS, CHIP_ROWS, HALF), BF16),
+    WG=((ZS, XS, GROUP_ROWS, 2 * QUARTER), BF16),
+    WD=((ZS, XS, DOWN_ROWS, DIM), BF16),
+    X=((CS, ZS, XS, TOK, DIM), BF16),
+    N1=((CS, ZS, XS, TOK, DIM), BF16),
+    N1O=((CS, TOK, DIM), BF16),
+    COT=((YS, CS, TOK, DIM), BF16),
+    SEG=((CS, 8, LENGTH), F32),
+    BK=((1, 2 * LENGTH), jnp.int32),
+    PH=((2 * CS * PAIRS, SPAN), F32),
+    BIAS=((PAIRS, 2 * TOK, LENGTH), F32),
+    MASK=((CS, TOK, LENGTH), F32),
+    KV=((PAIRS, CS, LENGTH, 256), BF16),
+    QS=((PAIRS, CS, 2 * TOK, 128), BF16),
+    PS=((PAIRS, CS, 2 * TOK, LENGTH), BF16),
+    ATT=((CS, CS, TOK, HALF), BF16),
+    H=((TOK, DIM), F32),
+    N2=((YS, CS, TOK, DIM), BF16),
+    ACT=((YS, 2 * TOK, QUARTER), BF16),
+    DGU=((YS, 2 * TOK, 2 * QUARTER), BF16),
+    MX=((YS, CS, TOK, DIM), BF16),
+    MXC=((YS, TOK, DIM), BF16),
+    MXS=((TOK, DIM), BF16),
+    MXY=((TOK, DIM), BF16),
+    E2=((YS, CS, TOK, DIM), BF16),
+    E2C=((YS, TOK, DIM), BF16),
+    E2S=((TOK, DIM), BF16),
+    E2Y=((TOK, DIM), BF16),
+    GG=((ZS, XS, GROUP_ROWS, 2 * QUARTER), BF16),
+    GGX=((ZS, GROUP_ROWS, 2 * QUARTER), BF16),
+    GGZ=((ZS, GROUP_ROWS, 2 * QUARTER), BF16),
+    GD=((ZS, XS, DOWN_ROWS, DIM), BF16),
+    GDX=((ZS, DOWN_ROWS, DIM), BF16),
+    GDZ=((ZS, DOWN_ROWS, DIM), BF16),
+    F4S=((BATCH_DEVICES, SHARD, 2 * QUARTER), F32),
+    F4=((BATCH_DEVICES, SHARD, 2 * QUARTER), F32),
+    DH=((TOK, DIM), F32),
+    DB=((CS, TOK, DIM), BF16),
+    DO=((CS, TOK, HALF), BF16),
+    DS=((CS, 2 * TOK, LENGTH), BF16),
+    DQ=((PAIRS, CS, TOK, 128), BF16),
+    DKV=((PAIRS, CS, 256, LENGTH), BF16),
+    DG=((8, SPAN), F32),
+    GA=((CHUNKS, ZS, XS, YS, CHIP_ROWS, HALF), BF16),
+    GAY=((CHUNKS, ZS, XS, CHIP_ROWS, HALF), BF16),
+    GAX=((CHUNKS, ZS, CHIP_ROWS, HALF), BF16),
+    GAZ=((CHUNKS, ZS, CHIP_ROWS, HALF), BF16),
+    FA=((CS, SHARD, 4 * HALF), F32),
+    F2=((CS, SHARD, 4 * HALF), F32),
+    DN=((CS, ZS, XS, DIM, TOK), BF16),
+    DNC=((ZS, XS, DIM, TOK), BF16),
+    DNX=((ZS, DIM, TOK), BF16),
+    DNZ=((ZS, DIM, TOK), BF16),
+    T1=((8, 128), F32),
+    TY=((8, 128), F32),
+    T2=((8, 128), F32),
+    TX=((8, 128), F32),
+    T3=((8, 128), F32),
+    TZ=((ZS, 8, 128), F32),
+    TO=((CS, 8, 128), F32),
+)
+SEND_COUNT = 224
+SLOTS = dict(
+    segc=1, wc=1, u=4, xz=4, xx=4, xc=8, wz=4 * CHUNKS, wx=CHUNKS, wy=2 * CHUNKS, woc=1,
+    gz=4, gx=4, dz=4, dx=1, coty=1, cotc=2, att=1, n2y=1, n2c=2, mxc=2, mxy=1, e2c=2, e2y=1,
+    rdx=4, rdz=4, rgx=4, rgz=4, f4=4, db=1, ray=CHUNKS, rax=CHUNKS, raz=4 * CHUNKS, f2=1,
+    dnc=4, dnx=4, dnz=4, ty=1, tx=1, tz=4, tc=1,
+)
+RECV_COUNT = sum(SLOTS.values())
+
+
+def slot_bases():
+    bases, used = {}, 0
+    for name, count in SLOTS.items():
+        bases[name] = used
+        used += count
+    return SimpleNamespace(**bases)
+
+
+INPUTS = dict(
+    tok=0, cot=0, seg=0, buckets=0, table=0, ga=0, gf=0, wq=0, wk=0, wv=0, wo=0, wg=0, wu=0, wd=0
+)
+OUTPUTS = dict(
+    mixed=((TOK, DIM), BF16), tg=((TOK, DIM), BF16), gga=((1, SHARD), F32),
+    gwq=((SHARD, DIM), F32), gwk=((SHARD, DIM), F32), gwv=((SHARD, DIM), F32), gwo=((SHARD, DIM), F32),
+    ggf=((1, SHARD), F32), gwg=((SHARD, FF_ALL), F32), gwu=((SHARD, FF_ALL), F32),
+    gwd=((DOWN_ROWS, DIM), F32), gtab=((2 * CS * PAIRS, 32), F32),
+)
+
+
+def layer_kernel(*refs):
+    names = (*INPUTS, *OUTPUTS, *SCRATCH)
+    r = SimpleNamespace(**dict(zip(names, refs[:-2], strict=True)))
+    ssem, rsem = refs[-2:]
+    k = slot_bases()
+    s, b = lax.axis_index("seq"), lax.axis_index("batch")
+    z, x = s // XS, s % XS
+    y, c = b // CS, b % CS
+    xo, yo, co = 1 - x, 1 - y, 1 - c
+    zo = [(z + j) % ZS for j in range(1, ZS)]
+
+    def at(zz, xx, yy, cc):
+        return (XS * zz + xx, CS * yy + cc)
+
+    to_core, to_y, to_diag, to_x = at(z, x, y, co), at(z, x, yo, c), at(z, x, yo, co), at(z, xo, y, c)
+    to_z = [at(zz, x, y, c) for zz in zo]
+
+    barrier = pltpu.get_barrier_semaphore()
+    friends = [to_core, to_y, to_diag, to_x] + to_z
+    for who in friends:
+        pl.semaphore_signal(barrier, inc=1, device_id=who, device_id_type=MESH_IDS)
+
+    sent = []
+
+    def put(src, dst, who, slot):
+        copy = pltpu.make_async_remote_copy(
+            src_ref=src, dst_ref=dst, send_sem=ssem.at[len(sent)], recv_sem=rsem.at[slot],
+            device_id=who, device_id_type=MESH_IDS,
+        )
+        copy.start()
+        sent.append(copy)
+
+    def take(dst, slot):
+        pltpu.make_async_remote_copy(
+            src_ref=dst, dst_ref=dst, send_sem=ssem.at[0], recv_sem=rsem.at[slot],
+            device_id=to_core, device_id_type=MESH_IDS,
+        ).wait_recv()
+
+    gain_a = to_column(r.ga[...].astype(F32))
+    gain_f = to_column(r.gf[...].astype(F32))
+    tok = r.tok
+    r.SEG[c] = jnp.broadcast_to(r.seg[...].astype(F32), (8, LENGTH))
+    r.BK[...] = jnp.zeros(r.BK.shape, jnp.int32)
+    r.BK[:, : 2 * LENGTH - 1] = r.buckets[...]
+    for h in range(CS):
+        for p in range(PAIRS):
+            for j, w_ref in enumerate((r.wq, r.wk, r.wv)):
+                lanes = slice(HALF * h + 128 * p, HALF * h + 128 * p + 128)
+                r.W_MINE[h, :, HALF * p + 128 * j : HALF * p + 128 * j + 128] = (
+                    w_ref[:, lanes].astype(F32) * gain_a
+                )
+        r.W_MINE[h, :, 3 * HALF :] = r.wo[:, HALF * h : HALF * h + HALF].astype(F32)
+
+    pl.semaphore_wait(barrier, len(friends))
+
+    put(r.W_MINE.at[co], r.W_CORE.at[c], to_core, k.wc)
+    for j, who in enumerate(to_z):
+        put(tok, r.X.at[c, z, x], who, k.xz + z)
+    put(tok, r.X.at[c, z, x], to_x, k.xx + z)
+    put(r.SEG.at[c], r.SEG.at[c], to_core, k.segc)
+    put(tok, r.X.at[c, z, x], to_core, k.xc + s)
+    r.X[c, z, x] = tok[...]
+
+    parts = split_quarters(r.wg[...].astype(F32) * gain_f)
+    for q in range(BATCH_DEVICES):
+        r.U_MINE[q, :, :QUARTER] = parts[q]
+    parts = split_quarters(r.wu[...].astype(F32) * gain_f)
+    for q in range(BATCH_DEVICES):
+        r.U_MINE[q, :, QUARTER:] = parts[q]
+
+    take(r.W_CORE.at[co], k.wc)
+    r.W_CORE[c] = r.W_MINE[c]
+    block = r.W_CORE[...].reshape(CHIP_ROWS, 4 * HALF).astype(BF16)
+    for ch in range(PAIRS):
+        r.WA[ch, z, x, y] = block[:, HALF * ch : HALF * ch + HALF]
+    r.WO[c, z, x, y] = block[:, 3 * HALF :]
+
+    def weight(ch):
+        return r.WA.at[ch] if ch < PAIRS else r.WO.at[c]
+
+    for ch in range(CHUNKS):
+        for who in to_z:
+            put(weight(ch).at[z, x, y], weight(ch).at[z, x, y], who, k.wz + 4 * ch + z)
+    for q_y, q_c, who in ((y, co, to_core), (yo, c, to_y), (yo, co, to_diag)):
+        put(r.U_MINE.at[CS * q_y + q_c], r.U_ALL.at[b], who, k.u + b)
+    r.U_ALL[b] = r.U_MINE[b]
+
+    onehot = (
+        lax.broadcasted_iota(jnp.int32, (32, SPAN), 0)
+        == r.BK[:, pl.ds(pl.multiple_of(LENGTH - TOK - TOK * s, 128), SPAN)]
+    )
+    r.PH[...] = dot(r.table[...], onehot.astype(BF16))
+    for p in range(PAIRS):
+        for hh in range(2):
+            line = r.PH[pl.ds(HEADS_HERE * c + 2 * p + hh, 1), :]
+            skewed = pltpu.roll(
+                jnp.broadcast_to(line, (TOK, SPAN)), SPAN - TOK + 1, 1, stride=1, stride_axis=0
+            )
+            r.BIAS[p, TOK * hh : TOK * hh + TOK, :] = skewed[:, :LENGTH]
+    take(r.SEG.at[co], k.segc)
+    for q in range(CS):
+        col = to_column(r.SEG[q, 0:1, pl.ds(pl.multiple_of(TOK * s, 128), TOK)])
+        r.MASK[q] = jnp.where(col == r.SEG[q, 0:1, :], 0.0, NEGATIVE)
+
+    for q_y, q_c in ((y, co), (yo, c), (yo, co)):
+        src = CS * q_y + q_c
+        take(r.U_ALL.at[src], k.u + src)
+    r.WG[z, x] = r.U_ALL[...].reshape(GROUP_ROWS, 2 * QUARTER).astype(BF16)
+    r.WD[z, x] = r.wd[...]
+    for who in to_z:
+        put(r.WG.at[z, x], r.WG.at[z, x], who, k.gz + z)
+    for who in to_z:
+        put(r.WD.at[z, x], r.WD.at[z, x], who, k.dz + z)
+
+    def norm_block(q, zz, xx, own=False):
+        value = unit_rows(r.X[q, zz, xx].astype(F32))[0].astype(BF16)
+        r.N1[q, zz, xx] = value
+        if own:
+            r.N1O[q] = value
+
+    norm_block(c, z, x, own=True)
+    for zz in zo:
+        take(r.X.at[c, zz, x], k.xz + zz)
+        put(r.X.at[c, zz, x], r.X.at[c, zz, x], to_x, k.xx + zz)
+        put(r.X.at[c, zz, x], r.X.at[c, zz, x], to_core, k.xc + XS * zz + x)
+        norm_block(c, zz, x)
+
+    def weight_from_z(ch):
+        for zz in zo:
+            take(weight(ch).at[zz, x, y], k.wz + 4 * ch + zz)
+        put(weight(ch).at[:, x, y], weight(ch).at[:, x, y], to_x, k.wx + ch)
+        put(weight(ch).at[:, x, y], weight(ch).at[:, x, y], to_y, k.wy + 2 * ch)
+
+    def weight_from_x(ch):
+        take(weight(ch).at[:, xo, y], k.wx + ch)
+        put(weight(ch).at[:, xo, y], weight(ch).at[:, xo, y], to_y, k.wy + 2 * ch + 1)
+
+    def weight_from_y(ch):
+        take(weight(ch).at[:, x, yo], k.wy + 2 * ch)
+        take(weight(ch).at[:, xo, yo], k.wy + 2 * ch + 1)
+
+    weight_from_z(0)
+    for zz in [z] + zo:
+        take(r.X.at[c, zz, xo], k.xx + zz)
+        put(r.X.at[c, zz, xo], r.X.at[c, zz, xo], to_core, k.xc + XS * zz + xo)
+        norm_block(c, zz, xo)
+    weight_from_x(0)
+    weight_from_z(1)
+    weight_from_x(1)
+    weight_from_z(2)
+    for zz in [z] + zo:
+        for xx in (x, xo):
+            take(r.X.at[co, zz, xx], k.xc + XS * zz + xx)
+            norm_block(co, zz, xx, own=zz is z and xx is x)
+    weight_from_x(2)
+    put(r.cot, r.COT.at[y, c], to_core, k.cotc + 0)
+    put(r.cot, r.COT.at[y, c], to_y, k.coty)
+    r.COT[y, c] = r.cot[...]
+
+    def attention_pair(p):
+        w_pair = r.WA.at[p]
+
+        def one_sequence(q, carry):
+            w = w_pair[...].reshape(DIM, HALF)
+            n1 = r.N1[q].reshape(LENGTH, DIM)
+            kv = dot(n1, w[:, 128:]).astype(BF16)
+            r.KV[p, q] = kv
+            stacked = stack_heads(dot(r.N1O[q], w[:, :128]))
+            r.QS[p, q] = stacked
+            mask = r.MASK[q]
+            scores = dot_tb(stacked, kv[:, :128]) + r.BIAS[p] + jnp.concatenate((mask, mask), axis=0)
+            weights = jnp.exp(scores - jnp.max(scores, axis=1, keepdims=True))
+            probs = (weights * (1.0 / jnp.sum(weights, axis=1, keepdims=True))).astype(BF16)
+            r.PS[p, q] = probs
+            r.ATT[c, q, :, 128 * p : 128 * p + 128] = unstack_heads(dot(probs, kv[:, 128:])).astype(BF16)
+            return carry
+
+        lax.fori_loop(0, CS, one_sequence, 0)
+
+    def gate_from_z():
+        for zz in zo:
+            take(r.WG.at[zz, x], k.gz + zz)
+            put(r.WG.at[zz, x], r.WG.at[zz, x], to_x, k.gx + zz)
+
+    weight_from_y(0)
+    attention_pair(0)
+    weight_from_z(PAIRS)
+    put(r.WG.at[z, x], r.WG.at[z, x], to_x, k.gx + z)
+    weight_from_y(1)
+    attention_pair(1)
+    weight_from_x(PAIRS)
+    gate_from_z()
+    take(r.COT.at[yo, c], k.coty)
+    put(r.COT.at[yo, c], r.COT.at[yo, c], to_core, k.cotc + 1)
+    weight_from_y(2)
+    attention_pair(2)
+    for zz in zo:
+        take(r.WD.at[zz, x], k.dz + zz)
+    put(r.WD.at[:, x], r.WD.at[:, x], to_x, k.dx)
+    weight_from_y(PAIRS)
+    put(r.WO.at[c], r.WO.at[c], to_core, k.woc)
+    put(r.ATT.at[c], r.ATT.at[c], to_core, k.att)
+    take(r.WO.at[co], k.woc)
+    take(r.ATT.at[co], k.att)
+
+    att_own = jnp.concatenate((r.ATT[0, c], r.ATT[1, c]), axis=1)
+    tokens_f = tok[...].astype(F32)
+    r.H[...] = tokens_f + jnp.concatenate(
+        (dot(att_own, r.WO[0].reshape(DIM, HALF)), dot(att_own, r.WO[1].reshape(DIM, HALF))), axis=1
+    )
+    r.N2[y, c] = unit_rows(r.H[...])[0].astype(BF16)
+    put(r.N2.at[y, c], r.N2.at[y, c], to_core, k.n2c + 0)
+    put(r.N2.at[y, c], r.N2.at[y, c], to_y, k.n2y)
+
+    for zz in [z] + zo:
+        take(r.WG.at[zz, xo], k.gx + zz)
+    take(r.WD.at[:, xo], k.dx)
+    take(r.COT.at[y, co], k.cotc + 0)
+    take(r.COT.at[yo, co], k.cotc + 1)
+    take(r.N2.at[y, co], k.n2c + 0)
+
+    def feed_forward(yy):
+        w_gu = r.WG[...].reshape(DIM, 2 * QUARTER)
+        w_d = r.WD[...].reshape(QUARTER, DIM)
+        n2 = r.N2[yy].reshape(2 * TOK, DIM)
+        g = r.COT[yy].reshape(2 * TOK, DIM)
+        gate = dot(n2, w_gu[:, :QUARTER])
+        up = dot(n2, w_gu[:, QUARTER:])
+        d_act = dot_tb(g, w_d)
+        square = gate * gate
+        inner = math.sqrt(2 / math.pi) * gate * (1.0 + 0.044715 * square)
+        tanh = jnp.tanh(inner)
+        half_open = 0.5 * (1.0 + tanh)
+        gelu = gate * half_open
+        slope = half_open + 0.5 * gate * (1.0 - tanh * tanh) * (
+            math.sqrt(2 / math.pi) * (1.0 + 3 * 0.044715 * square)
+        )
+        act = (gelu * up).astype(BF16)
+        r.ACT[yy] = act
+        d_gu = jnp.concatenate(
+            ((slope * (up * d_act)).astype(BF16), (gelu * d_act).astype(BF16)), axis=1
+        )
+        r.DGU[yy] = d_gu
+        r.E2[yy] = dot_tb(d_gu, w_gu).astype(BF16).reshape(CS, TOK, DIM)
+        put(r.E2.at[yy, co], r.E2C.at[yy], to_core, k.e2c + yy)
+        r.MX[yy] = dot(act, w_d).astype(BF16).reshape(CS, TOK, DIM)
+        put(r.MX.at[yy, co], r.MXC.at[yy], to_core, k.mxc + yy)
+
+    feed_forward(y)
+    take(r.N2.at[yo, c], k.n2y)
+    put(r.N2.at[yo, c], r.N2.at[yo, c], to_core, k.n2c + 1)
+    take(r.N2.at[yo, co], k.n2c + 1)
+    feed_forward(yo)
+    take(r.E2C.at[yo], k.e2c + yo)
+    r.E2S[...] = (r.E2[yo, c].astype(F32) + r.E2C[yo].astype(F32)).astype(BF16)
+    put(r.E2S, r.E2Y, to_y, k.e2y)
+    take(r.MXC.at[yo], k.mxc + yo)
+    r.MXS[...] = (r.MX[yo, c].astype(F32) + r.MXC[yo].astype(F32)).astype(BF16)
+    put(r.MXS, r.MXY, to_y, k.mxy)
+
+    cot_all = r.COT[...].reshape(4 * TOK, DIM)
+    r.GD[...] = dot_ta(r.ACT[...].reshape(4 * TOK, QUARTER), cot_all).astype(BF16).reshape(
+        ZS, XS, DOWN_ROWS, DIM
+    )
+    for zz in zo + [z]:
+        put(r.GD.at[zz, xo], r.GDX.at[zz], to_x, k.rdx + zz)
+    n2_all = r.N2[...].reshape(4 * TOK, DIM)
+    d_gu_all = r.DGU[...].reshape(4 * TOK, 2 * QUARTER)
+    r.GG[...] = dot_ta(n2_all, d_gu_all).astype(BF16).reshape(ZS, XS, GROUP_ROWS, 2 * QUARTER)
+    for zz in zo + [z]:
+        put(r.GG.at[zz, xo], r.GGX.at[zz], to_x, k.rgx + zz)
+
+    def grad_from_x(full, part, got, slot, back):
+        for j, zz in enumerate(zo + [z]):
+            take(part.at[zz], slot + zz)
+            total = full[zz, x].astype(F32) + part[zz].astype(F32)
+            full[zz, x] = total.astype(BF16)
+            if j < ZS - 1:
+                put(full.at[zz, x], got.at[z], to_z[j], back + z)
+
+    def sum_z(own, got, slot):
+        total = own.astype(F32)
+        for zz in zo:
+            take(got.at[zz], slot + zz)
+            total = total + got[zz].astype(F32)
+        return total
+
+    take(r.E2C.at[y], k.e2c + y)
+    take(r.E2Y, k.e2y)
+    e2 = r.E2[y, c].astype(F32) + r.E2C[y].astype(F32) + r.E2Y[...].astype(F32)
+    n2_own, r2 = unit_rows(r.H[...])
+    r.DH[...] = r.cot[...].astype(F32) + r2 * (e2 - n2_own * jnp.mean(e2 * n2_own, axis=1, keepdims=True))
+    r.DB[c] = r.DH[...].astype(BF16)
+    put(r.DB.at[c], r.DB.at[c], to_core, k.db)
+    take(r.MXC.at[y], k.mxc + y)
+    take(r.MXY, k.mxy)
+    r.mixed[...] = (
+        r.H[...] + r.MX[y, c].astype(F32) + r.MXC[y].astype(F32) + r.MXY[...].astype(F32)
+    ).astype(BF16)
+    take(r.DB.at[co], k.db)
+    db_all = r.DB[...].reshape(CS * TOK, DIM)
+    rows = [r.WO[h, pl.ds(2 * c, 2)].reshape(HALF, HALF) for h in range(CS)]
+    d_att = dot_tb(db_all[:, :HALF], rows[0]) + dot_tb(db_all[:, HALF:], rows[1])
+    r.DO[...] = d_att.astype(BF16).reshape(CS, TOK, HALF)
+    att_all = jnp.concatenate(
+        [jnp.concatenate((r.ATT[0, q], r.ATT[1, q]), axis=1) for q in range(CS)], axis=0
+    )
+    db_cols = r.DB[:, :, pl.ds(pl.multiple_of(HALF * c, 128), HALF)].reshape(CS * TOK, HALF)
+
+    def chip_grad(ch, value):
+        r.GA[ch] = value.astype(BF16).reshape(ZS, XS, YS, CHIP_ROWS, HALF)
+        put(r.GA.at[ch, :, :, yo], r.GAY.at[ch], to_y, k.ray + ch)
+
+    chip_grad(PAIRS, dot_ta(att_all, db_cols))
+
+    def chip_from_y(ch):
+        take(r.GAY.at[ch], k.ray + ch)
+        r.GA[ch, :, :, y] = (r.GA[ch, :, :, y].astype(F32) + r.GAY[ch].astype(F32)).astype(BF16)
+        put(r.GA.at[ch, :, xo, y], r.GAX.at[ch], to_x, k.rax + ch)
+
+    def chip_from_x(ch):
+        take(r.GAX.at[ch], k.rax + ch)
+        r.GA[ch, :, x, y] = (r.GA[ch, :, x, y].astype(F32) + r.GAX[ch].astype(F32)).astype(BF16)
+        for j, zz in enumerate(zo):
+            put(r.GA.at[ch, zz, x, y], r.GAZ.at[ch, z], to_z[j], k.raz + 4 * ch + z)
+
+    def chip_from_z(ch):
+        total = r.GA[ch, z, x, y].astype(F32)
+        for zz in zo:
+            take(r.GAZ.at[ch, zz], k.raz + 4 * ch + zz)
+            total = total + r.GAZ[ch, zz].astype(F32)
+        r.FA[:, :, HALF * ch : HALF * ch + HALF] = total.reshape(CS, SHARD, HALF)
+
+    reverse = (
+        lax.broadcasted_iota(jnp.int32, (TOK, TOK), 0) + lax.broadcasted_iota(jnp.int32, (TOK, TOK), 1)
+        == TOK - 1
+    ).astype(BF16)
+    reverse2 = jnp.concatenate((reverse, reverse), axis=1)
+
+    def attention_pair_back(p):
+        def one_sequence(q, carry):
+            d_out = stack_heads(r.DO[q, :, 128 * p : 128 * p + 128].astype(F32))
+            kv = r.KV.at[p, q]
+            probs = r.PS[p, q]
+            weighted = probs.astype(F32) * dot_tb(d_out, kv[:, 128:])
+            delta = jnp.sum(weighted, axis=1, keepdims=True)
+            d_scores = (weighted - probs.astype(F32) * delta).astype(BF16)
+            r.DS[q] = d_scores
+            r.DQ[p, q] = unstack_heads(dot(d_scores, kv[:, :128])).astype(BF16)
+            r.DKV[p, q, :128] = dot_ta(r.QS[p, q], d_scores).astype(BF16)
+            r.DKV[p, q, 128:] = dot_ta(d_out, probs).astype(BF16)
+            return carry
+
+        lax.fori_loop(0, CS, one_sequence, 0)
+        for hh in range(2):
+            both = r.DS[:, TOK * hh : TOK * hh + TOK, :].reshape(CS * TOK, LENGTH)
+            padded = jnp.concatenate((dot(reverse2, both), jnp.zeros((TOK, TOK), F32)), axis=1)
+            placed = pltpu.roll(padded, 0, 1, stride=1, stride_axis=0)
+            r.DG[2 * p + hh : 2 * p + hh + 1, :] = jnp.sum(placed, axis=0, keepdims=True)
+        kv_grad = dot(r.DKV[p, 0], r.N1[0].reshape(LENGTH, DIM)) + dot(
+            r.DKV[p, 1], r.N1[1].reshape(LENGTH, DIM)
+        )
+        own_rows = r.N1O[...].reshape(CS * TOK, DIM)
+        q_grad = dot_ta(r.DQ[p].reshape(CS * TOK, 128), own_rows)
+        chip_grad(p, jnp.concatenate((q_grad, kv_grad), axis=0).astype(BF16).T)
+
+    attention_pair_back(0)
+    grad_from_x(r.GD, r.GDX, r.GDZ, k.rdx, k.rdz)
+    chip_from_y(PAIRS)
+    attention_pair_back(1)
+    grad_from_x(r.GG, r.GGX, r.GGZ, k.rgx, k.rgz)
+    chip_from_x(PAIRS)
+    chip_from_y(0)
+    attention_pair_back(2)
+    chip_from_x(0)
+    chip_from_y(1)
+
+    r.DG[HEADS_HERE:, :] = jnp.zeros((8 - HEADS_HERE, SPAN), F32)
+    onehot_back = (
+        lax.broadcasted_iota(jnp.int32, (128, SPAN), 0)
+        == r.BK[:, pl.ds(pl.multiple_of(LENGTH - TOK - TOK * s, 128), SPAN)]
+    ).astype(F32)
+    r.T1[...] = lax.dot_general(
+        r.DG[...], onehot_back, (((1,), (1,)), ((), ())), precision=HIGHEST, preferred_element_type=F32
+    )
+    put(r.T1, r.TY, to_y, k.ty)
+
+    w_kv = jnp.concatenate([r.WA[p].reshape(DIM, HALF)[:, 128:] for p in range(PAIRS)], axis=1)
+
+    def token_grad(q, zz):
+        lanes = pl.ds(pl.multiple_of(XS * TOK * zz, 128), XS * TOK)
+        d_kv = r.DKV[:, q, :, lanes].reshape(PAIRS * 256, XS * TOK)
+        out = dot(w_kv, d_kv)
+        return [out[:, :TOK], out[:, TOK:]]
+
+    def query_part(q):
+        total = dot_tb(r.WA[0].reshape(DIM, HALF)[:, :128], r.DQ[0, q])
+        for p in range(1, PAIRS):
+            total = total + dot_tb(r.WA[p].reshape(DIM, HALF)[:, :128], r.DQ[p, q])
+        return total
+
+    for zz in zo + [z]:
+        both = token_grad(co, zz)
+        for xx in range(XS):
+            r.DN[co, zz, xx] = both[xx].astype(BF16)
+        if zz is z:
+            r.DN[co, z, x] = (r.DN[co, z, x].astype(F32) + query_part(co)).astype(BF16)
+        put(r.DN.at[co, zz], r.DNC.at[zz], to_core, k.dnc + zz)
+    for zz in zo + [z]:
+        both = token_grad(c, zz)
+        for xx in range(XS):
+            r.DN[c, zz, xx] = both[xx].astype(BF16)
+        if zz is z:
+            r.DN[c, z, x] = (r.DN[c, z, x].astype(F32) + query_part(c)).astype(BF16)
+        take(r.DNC.at[zz], k.dnc + zz)
+        r.DN[c, zz] = (r.DN[c, zz].astype(F32) + r.DNC[zz].astype(F32)).astype(BF16)
+        put(r.DN.at[c, zz, xo], r.DNX.at[zz], to_x, k.dnx + zz)
+
+    chip_from_x(1)
+    chip_from_y(2)
+    take(r.TY, k.ty)
+    r.T2[...] = r.T1[...] + r.TY[...]
+    put(r.T2, r.TX, to_x, k.tx)
+    for j, zz in enumerate(zo + [z]):
+        take(r.DNX.at[zz], k.dnx + zz)
+        r.DN[c, zz, x] = (r.DN[c, zz, x].astype(F32) + r.DNX[zz].astype(F32)).astype(BF16)
+        if j < ZS - 1:
+            put(r.DN.at[c, zz, x], r.DNZ.at[z], to_z[j], k.dnz + z)
+    chip_from_x(2)
+    take(r.TX, k.tx)
+    r.T3[...] = r.T2[...] + r.TX[...]
+    for who in to_z:
+        put(r.T3, r.TZ.at[z], who, k.tz + z)
+    r.TZ[z] = r.T3[...]
+
+    r.gwd[...] = sum_z(r.GD[z, x], r.GDZ, k.rdz)
+    r.F4S[...] = sum_z(r.GG[z, x], r.GGZ, k.rgz).reshape(BATCH_DEVICES, SHARD, 2 * QUARTER)
+    for q_y, q_c, who in ((y, co, to_core), (yo, c, to_y), (yo, co, to_diag)):
+        put(r.F4S.at[CS * q_y + q_c], r.F4.at[b], who, k.f4 + b)
+    r.F4[b] = r.F4S[b]
+    chip_from_z(PAIRS)
+    chip_from_z(0)
+    chip_from_z(1)
+    for q_y, q_c in ((y, co), (yo, c), (yo, co)):
+        src = CS * q_y + q_c
+        take(r.F4.at[src], k.f4 + src)
+    gate_grad = join_quarters([r.F4[q, :, :QUARTER] for q in range(BATCH_DEVICES)])
+    up_grad = join_quarters([r.F4[q, :, QUARTER:] for q in range(BATCH_DEVICES)])
+    r.gwg[...] = gate_grad * gain_f
+    r.gwu[...] = up_grad * gain_f
+    r.ggf[...] = to_row(
+        jnp.sum(gate_grad * r.wg[...].astype(F32) + up_grad * r.wu[...].astype(F32), axis=1, keepdims=True)
+    )
+    chip_from_z(2)
+    put(r.FA.at[co], r.F2.at[c], to_core, k.f2)
+    r.F2[c] = r.FA[c]
+
+    for zz in zo:
+        take(r.TZ.at[zz], k.tz + zz)
+    r.TO[c] = (r.TZ[0] + r.TZ[1]) + (r.TZ[2] + r.TZ[3])
+    put(r.TO.at[c], r.TO.at[c], to_core, k.tc)
+
+    e1 = sum_z(r.DN[c, z, x], r.DNZ, k.dnz).T
+    n1_own, r1 = unit_rows(tokens_f)
+    r.tg[...] = (
+        r.DH[...] + r1 * (e1 - n1_own * jnp.mean(e1 * n1_own, axis=1, keepdims=True))
+    ).astype(BF16)
+
+    take(r.F2.at[co], k.f2)
+    gain_total = jnp.zeros((SHARD, 1), F32)
+    for j, (w_ref, out_ref) in enumerate(((r.wq, r.gwq), (r.wk, r.gwk), (r.wv, r.gwv))):
+        for h in range(CS):
+            for p in range(PAIRS):
+                lanes = slice(HALF * h + 128 * p, HALF * h + 128 * p + 128)
+                grad = r.F2[h, :, HALF * p + 128 * j : HALF * p + 128 * j + 128]
+                gain_total = gain_total + jnp.sum(grad * w_ref[:, lanes].astype(F32), axis=1, keepdims=True)
+                out_ref[:, lanes] = grad * gain_a
+    r.gga[...] = to_row(gain_total)
+    for h in range(CS):
+        r.gwo[:, HALF * h : HALF * h + HALF] = r.F2[h, :, 3 * HALF :]
+    take(r.TO.at[co], k.tc)
+    for q in range(CS):
+        r.gtab[HEADS_HERE * q : HEADS_HERE * q + HEADS_HERE, :] = r.TO[q, :HEADS_HERE, :32]
+    for copy in sent:
+        copy.wait_send()
+
+
+def finish_kernel(*refs):
+    count = len(refs) // 2
+    for src, dst in zip(refs[:count], refs[count:]):
+        dst[...] = src[...]
+
+
+def fused_device(
+    tokens, segments, buckets, gain_attn, w_query, w_key, w_value, w_output,
+    gain_ffn, w_gate, w_up, w_down, bucket_bias_matrix, cotangent,
+):
+    operands = (
+        tokens.reshape(TOK, DIM),
+        cotangent.reshape(TOK, DIM),
+        segments.reshape(1, LENGTH),
+        buckets.reshape(1, 2 * LENGTH - 1),
+        bucket_bias_matrix.T,
+        gain_attn.reshape(1, SHARD),
+        gain_ffn.reshape(1, SHARD),
+        w_query, w_key, w_value, w_output, w_gate, w_up, w_down,
+    )
+    out_shape = [jax.ShapeDtypeStruct(shape, dtype) for shape, dtype in OUTPUTS.values()]
+    in_vmem = pl.BlockSpec(memory_space=pltpu.VMEM)
+    outs = pl.pallas_call(
+        layer_kernel,
+        out_shape=out_shape,
+        in_specs=[in_vmem] * len(operands),
+        out_specs=[in_vmem] * len(out_shape),
+        scratch_shapes=[pltpu.VMEM(shape, dtype) for shape, dtype in SCRATCH.values()]
+        + [pltpu.SemaphoreType.DMA((SEND_COUNT,)), pltpu.SemaphoreType.DMA((RECV_COUNT,))],
+        compiler_params=pltpu.CompilerParams(
+            collective_id=0, has_side_effects=True, vmem_limit_bytes=63 * 2**20
+        ),
+        name="layer",
+    )(*operands)
+    outs = pl.pallas_call(
+        finish_kernel,
+        out_shape=out_shape,
+        in_specs=[in_vmem] * len(out_shape),
+        out_specs=[in_vmem] * len(out_shape),
+        name="finish",
+    )(*outs)
+    mixed, tokens_grad, gga, gwq, gwk, gwv, gwo, ggf, gwg, gwu, gwd, table_grad = outs
+    return (
+        mixed.reshape(tokens.shape), tokens_grad.reshape(tokens.shape), gga.reshape(SHARD),
+        gwq, gwk, gwv, gwo, ggf.reshape(SHARD), gwg, gwu, gwd, table_grad.T,
+    )
+
+
+def fits_fused(mesh):
+    return mesh.shape["seq"] == SEQ_DEVICES and mesh.shape["batch"] == BATCH_DEVICES
+
+
 def solution(mesh):
     return jax.shard_map(
-        on_device,
+        fused_device if fits_fused(mesh) else on_device,
         mesh=mesh,
         in_specs=(
             P("seq", "batch", None),

time: 1550 us -> 170 us (0.11)
  waiting for transfers between devices: 1180 us -> 0 us
  Pallas kernels: 0 us -> 168 us
  local copies, waits for them, and re-layouts: 148 us -> 0 us
  blocking collectives: 81.7 us -> 0 us
  matrix products: 70.5 us -> 0 us
  other arithmetic: 24.1 us -> 0 us
  loops' own time: 23.1 us -> 0 us
    reduce_scatter x8 -> x0, waiting for transfers between devices: 823 us -> none  [the longest x1 121 us: on_device(): lax.psum_scatter(grad_up, ('seq', 'batch'), scatter_dimension=0, tiled=True)]
    all_gather x9 -> x0, waiting for transfers between devices: 352 us -> none  [the longest x1 57.4 us: on_device(): lax.all_gather(w_gate, ('seq', 'batch'), axis=0, tiled=True)]
    pallas_call x0 -> x2, Pallas kernels: none -> 168 us  [the longest x1 166 us: fused_device(): pl.pallas_call(layer_kernel, out_shape=out_shape, in_specs=[in_vmem] * le...]
    unnamed x2 -> x0, blocking collectives: 81.7 us -> none
    dot_general x41 -> x0, matrix products: 70.5 us -> none  [the longest x7 18.9 us: weight_grad(): jnp.einsum('tsk,tsn->kn', left_side, grad_rows, preferred_element_type=jn...]
    reshape x8 -> x0, local copies, waits for them, and re-layouts: 46.2 us -> none  [the longest x4 27.5 us: position_bias(): skewed = tiled[:, :query_rows * span].reshape(head_count, query_rows, span)]
    while x58 -> x0, local copies, waits for them, and re-layouts: 38.5 us -> none
    slice x8 -> x0, local copies, waits for them, and re-layouts: 29.4 us -> none  [the longest x4 18.8 us: position_bias(): return (onehot, skewed[:, :, query_rows - 1:query_rows - 1 + key_rows])]
  transfers between devices with their start and end apart: 17 -> 0, of which waited for: 16 -> 0; matrix products, arithmetic and copies ran while one was open for 7% -> 0% of each run, Pallas kernels for 0% -> 0%
where the time goes in v1:
time: 170 us; the launch traced here: 169 us
  Pallas kernels  168 us (99%)
    pallas_call x1, Pallas kernels, fused_device(): pl.pallas_call(layer_kernel, out_shape=out_shape, in_specs=[in_vmem] * le...  166 us

profile of v1, /device:TPU:0, one launch (start us, length us, event | category | flops | bytes accessed | tf_op | source)
XLA Modules:
  0.0 169.1 jit_solution(3143152368083087801)
XLA Ops:
  0.6 165.8 %layer.1 = (bf16[128,768]{1,0:T(8,128)(2,1)}, bf16[128,768]{1,0:T(8,128)(2,1)}, f32[1,24]{1,0:T(1,128)}, f32[24,768]{1,0:T(8,128)}, f32[24,768]{1,0:T(8,128)}, /...) custom-call(bf16[128,768]{1,0:T(8,128)(2,1)} %bitcast.12, ...), custom_call_target="tpu_custom_call" | custom-call | tf_op jit(solution)/shard_map/layer/pallas_call | solution.py:1069
  166.5 2.4 %finish.1 = (bf16[128,768]{1,0:T(8,128)(2,1)}, bf16[128,768]{1,0:T(8,128)(2,1)}, f32[1,24]{1,0:T(1,128)}, f32[24,768]{1,0:T(8,128)}, f32[24,768]{1,0:T(8,128)}, ...) custom-call(bf16[128,768]{1,0:T(8,128)(2,1)} %get-tuple-element.36.r, ...), custom_call_target="tpu_custom_call" | custom-call | tf_op jit(solution)/shard_map/finish/pallas_call | solution.py:1081

commit v2 on v0

--- a/solution.py
+++ b/solution.py
@@ -1,9 +1,12 @@
 from functools import partial
 import math
+from types import SimpleNamespace
 
 import jax
 import jax.numpy as jnp
 from jax import lax
+from jax.experimental import pallas as pl
+from jax.experimental.pallas import tpu as pltpu
 from jax.sharding import PartitionSpec as P
 
 EPSILON = 1e-06
@@ -363,9 +366,998 @@
     )
 
 
+BF16 = jnp.bfloat16
+F32 = jnp.float32
+MESH_IDS = pl.DeviceIdType.MESH
+
+ZS, XS, YS, CS = 4, 2, 2, 2
+SEQ_DEVICES = ZS * XS
+BATCH_DEVICES = YS * CS
+TOK = 128
+LENGTH = SEQ_DEVICES * TOK
+DIM = 768
+HALF = DIM // CS
+PAIRS = HALF // 128
+SHARD = DIM // (SEQ_DEVICES * BATCH_DEVICES)
+CHIP_ROWS = SHARD * CS
+GROUP_ROWS = SHARD * BATCH_DEVICES
+FF_ALL = 2048
+QUARTER = FF_ALL // BATCH_DEVICES
+DOWN_ROWS = FF_ALL // (SEQ_DEVICES * BATCH_DEVICES)
+CHUNKS = PAIRS + 1
+SPAN = LENGTH + TOK
+HEADS_HERE = 2 * PAIRS
+
+
+def dot(a, b):
+    return lax.dot_general(a, b, (((1,), (0,)), ((), ())), preferred_element_type=F32)
+
+
+def dot_tb(a, b):
+    return lax.dot_general(a, b, (((1,), (1,)), ((), ())), preferred_element_type=F32)
+
+
+def dot_ta(a, b):
+    return lax.dot_general(a, b, (((0,), (0,)), ((), ())), preferred_element_type=F32)
+
+
+def to_column(row):
+    n = row.shape[1]
+    eye = lax.broadcasted_iota(jnp.int32, (n, n), 0) == lax.broadcasted_iota(jnp.int32, (n, n), 1)
+    return jnp.sum(jnp.where(eye, jnp.broadcast_to(row, (n, n)), 0.0), axis=1, keepdims=True)
+
+
+def to_row(col):
+    n = col.shape[0]
+    eye = lax.broadcasted_iota(jnp.int32, (n, n), 0) == lax.broadcasted_iota(jnp.int32, (n, n), 1)
+    return jnp.sum(jnp.where(eye, jnp.broadcast_to(col, (n, n)), 0.0), axis=0, keepdims=True)
+
+
+def unit_rows(x):
+    r = lax.rsqrt(jnp.mean(x * x, axis=1, keepdims=True) + EPSILON)
+    return x * r, r
+
+
+def stack_heads(pair):
+    low = lax.broadcasted_iota(jnp.int32, pair.shape, 1) < 64
+    return jnp.concatenate((jnp.where(low, pair, 0.0), jnp.where(low, 0.0, pair)), axis=0).astype(BF16)
+
+
+def unstack_heads(stacked):
+    rows = stacked.shape[0] // 2
+    low = lax.broadcasted_iota(jnp.int32, (rows, 128), 1) < 64
+    return jnp.where(low, stacked[:rows], stacked[rows:])
+
+
+def split_quarters(whole):
+    low = lax.broadcasted_iota(jnp.int32, (whole.shape[0], 128), 1) < 64
+    parts = []
+    for q in range(BATCH_DEVICES):
+        cols = []
+        for m in range(ZS):
+            first = 4 * m + 2 * (q // 2)
+            a = whole[:, 128 * first : 128 * first + 128]
+            b = whole[:, 128 * (first + 1) : 128 * (first + 1) + 128]
+            if q % 2 == 0:
+                cols.append(jnp.where(low, a, pltpu.roll(b, 64, 1)))
+            else:
+                cols.append(jnp.where(low, pltpu.roll(a, 64, 1), b))
+        parts.append(jnp.concatenate(cols, axis=1))
+    return parts
+
+
+def join_quarters(parts):
+    low = lax.broadcasted_iota(jnp.int32, (parts[0].shape[0], 128), 1) < 64
+    cols = []
+    for block in range(FF_ALL // 128):
+        m, xx, yy = block // 4, block // 2 % 2, block % 2
+        lanes = slice(128 * m, 128 * m + 128)
+        a, b = parts[2 * xx][:, lanes], parts[2 * xx + 1][:, lanes]
+        if yy == 0:
+            cols.append(jnp.where(low, a, pltpu.roll(b, 64, 1)))
+        else:
+            cols.append(jnp.where(low, pltpu.roll(a, 64, 1), b))
+    return jnp.concatenate(cols, axis=1)
+
+
+SCRATCH = dict(
+    W_MINE=((CS, SHARD, 4 * HALF + 4 * QUARTER), F32),
+    W_CORE=((CS, SHARD, 4 * HALF + 4 * QUARTER), F32),
+    UB=((XS, CHIP_ROWS, 2 * QUARTER), BF16),
+    WA=((PAIRS, ZS, XS, YS, CHIP_ROWS, HALF), BF16),
+    WO=((CS, ZS, XS, YS, CHIP_ROWS, HALF), BF16),
+    WG=((ZS, XS, YS, CHIP_ROWS, 2 * QUARTER), BF16),
+    WD=((ZS, YS, DOWN_ROWS, DIM), BF16),
+    X=((CS, ZS, XS, TOK, DIM), BF16),
+    N1=((CS, ZS, XS, TOK, DIM), BF16),
+    N1O=((CS, TOK, DIM), BF16),
+    COT=((XS, CS, TOK, DIM), BF16),
+    SEG=((CS, 8, LENGTH), F32),
+    BK=((1, 2 * LENGTH), jnp.int32),
+    PH=((2 * CS * PAIRS, SPAN), F32),
+    BIAS=((PAIRS, 2 * TOK, LENGTH), F32),
+    MASK=((CS, TOK, LENGTH), F32),
+    KV=((PAIRS, CS, LENGTH, 256), BF16),
+    QS=((PAIRS, CS, 2 * TOK, 128), BF16),
+    PS=((PAIRS, CS, 2 * TOK, LENGTH), BF16),
+    ATT=((CS, CS, TOK, HALF), BF16),
+    H=((TOK, DIM), F32),
+    N2=((XS, CS, TOK, DIM), BF16),
+    ACT=((XS, 2 * TOK, QUARTER), BF16),
+    DGU=((XS, 2 * TOK, 2 * QUARTER), BF16),
+    MX=((XS, CS, TOK, DIM), BF16),
+    MXC=((XS, TOK, DIM), BF16),
+    MXS=((TOK, DIM), BF16),
+    MXX=((TOK, DIM), BF16),
+    E2=((XS, CS, TOK, DIM), BF16),
+    E2C=((XS, TOK, DIM), BF16),
+    E2S=((TOK, DIM), BF16),
+    E2X=((TOK, DIM), BF16),
+    GG=((ZS, XS, YS, CHIP_ROWS, 2 * QUARTER), BF16),
+    GGY=((ZS, XS, CHIP_ROWS, 2 * QUARTER), BF16),
+    GGZ=((ZS, XS, CHIP_ROWS, 2 * QUARTER), BF16),
+    GGC=((XS, CHIP_ROWS, 2 * QUARTER), BF16),
+    GD=((ZS, YS, DOWN_ROWS, DIM), BF16),
+    GDY=((ZS, DOWN_ROWS, DIM), BF16),
+    GDZ=((ZS, DOWN_ROWS, DIM), BF16),
+    GDC=((DOWN_ROWS, DIM), BF16),
+    F4S=((XS, CHIP_ROWS, 2 * QUARTER), BF16),
+    F4X=((CHIP_ROWS, 2 * QUARTER), BF16),
+    F4S2=((CS, XS, SHARD, 2 * QUARTER), F32),
+    F4=((CS, XS, SHARD, 2 * QUARTER), F32),
+    DH=((TOK, DIM), F32),
+    DB=((CS, TOK, DIM), BF16),
+    DO=((CS, TOK, HALF), BF16),
+    DS=((CS, 2 * TOK, LENGTH), BF16),
+    DQ=((PAIRS, CS, TOK, 128), BF16),
+    DKV=((PAIRS, CS, 256, LENGTH), BF16),
+    DG=((8, SPAN), F32),
+    GA=((CHUNKS, ZS, XS, YS, CHIP_ROWS, HALF), BF16),
+    GA1=((CHUNKS, ZS, 2, CHIP_ROWS, HALF), BF16),
+    GA2=((CHUNKS, ZS, CHIP_ROWS, HALF), BF16),
+    GAZ=((CHUNKS, ZS, CHIP_ROWS, HALF), BF16),
+    GAC=((CHUNKS, CHIP_ROWS, HALF), BF16),
+    FA=((CS, SHARD, 4 * HALF), F32),
+    F2=((CS, SHARD, 4 * HALF), F32),
+    DN=((CS, ZS, XS, DIM, TOK), BF16),
+    DNC=((ZS, XS, DIM, TOK), BF16),
+    DNX=((ZS, DIM, TOK), BF16),
+    DNZ=((ZS, DIM, TOK), BF16),
+    DNT=((DIM, TOK), BF16),
+    T1=((8, 128), F32),
+    TY=((8, 128), F32),
+    T2=((8, 128), F32),
+    TX=((8, 128), F32),
+    T3=((8, 128), F32),
+    TZ=((ZS, 8, 128), F32),
+    TO=((CS, 8, 128), F32),
+)
+SEND_COUNT = 224
+SLOTS = dict(
+    segc=1, wc=1, u=1, xz=4, xx=4, xc=8, wz=4 * CHUNKS, wx=4 * CHUNKS, wy=4 * CHUNKS, wr=CHUNKS, woc=1,
+    gz=8, gy=8, dz=4, dy=4, cotx=1, cotc=2, att=1, n2x=1, n2c=2, mxc=2, mxx=1, e2c=2, e2x=1,
+    rdy=4, rdz=4, rdc=1, rgy=4, rgz=4, rgc=1, f4x=1, f4=1, db=1,
+    ra1=CHUNKS, ra2=CHUNKS, raz=4 * CHUNKS, rac=CHUNKS, f2=1,
+    dnc=4, dnx=4, dnz=4, dnt=1, ty=1, tx=1, tz=4, tc=1,
+)
+RECV_COUNT = sum(SLOTS.values())
+
+
+def slot_bases():
+    bases, used = {}, 0
+    for name, count in SLOTS.items():
+        bases[name] = used
+        used += count
+    return SimpleNamespace(**bases)
+
+
+INPUTS = dict(
+    tok=0, cot=0, seg=0, buckets=0, table=0, ga=0, gf=0, wq=0, wk=0, wv=0, wo=0, wg=0, wu=0, wd=0
+)
+OUTPUTS = dict(
+    mixed=((TOK, DIM), BF16), tg=((TOK, DIM), BF16), gga=((1, SHARD), F32),
+    gwq=((SHARD, DIM), F32), gwk=((SHARD, DIM), F32), gwv=((SHARD, DIM), F32), gwo=((SHARD, DIM), F32),
+    ggf=((1, SHARD), F32), gwg=((SHARD, FF_ALL), F32), gwu=((SHARD, FF_ALL), F32),
+    gwd=((DOWN_ROWS, DIM), F32), gtab=((2 * CS * PAIRS, 32), F32),
+)
+
+
+RELAY_TO_Y = (True, True, True, True)
+HEAVY_X = (True, True, True, True)
+
+
+def layer_kernel(*refs):
+    names = (*INPUTS, *OUTPUTS, *SCRATCH)
+    r = SimpleNamespace(**dict(zip(names, refs[:-2], strict=True)))
+    ssem, rsem = refs[-2:]
+    k = slot_bases()
+    s, b = lax.axis_index("seq"), lax.axis_index("batch")
+    z, x = s // XS, s % XS
+    y, c = b // CS, b % CS
+    xo, yo, co = 1 - x, 1 - y, 1 - c
+    side = z // 2
+    m = z + side * (3 - 2 * z)
+    at_end, beside = m == 0, m == 1
+    zord = [near + side * (3 - 2 * near) for near in (1 - m, 2, 3)]
+
+    def at(zz, xx, yy, cc):
+        return (XS * zz + xx, CS * yy + cc)
+
+    to_core, to_x, to_y = at(z, x, y, co), at(z, xo, y, c), at(z, x, yo, c)
+    to_z = [at(zz, x, y, c) for zz in zord]
+
+    barrier = pltpu.get_barrier_semaphore()
+    friends = [to_core, to_x, to_y] + to_z
+    for who in friends:
+        pl.semaphore_signal(barrier, inc=1, device_id=who, device_id_type=MESH_IDS)
+
+    sent = []
+
+    def put(src, dst, who, slot, when=None):
+        copy = pltpu.make_async_remote_copy(
+            src_ref=src, dst_ref=dst, send_sem=ssem.at[len(sent)], recv_sem=rsem.at[slot],
+            device_id=who, device_id_type=MESH_IDS,
+        )
+        if when is None:
+            copy.start()
+        else:
+            pl.when(when)(copy.start)
+        sent.append((copy, when))
+
+    def take(dst, slot, when=None):
+        wait = pltpu.make_async_remote_copy(
+            src_ref=dst, dst_ref=dst, send_sem=ssem.at[0], recv_sem=rsem.at[slot],
+            device_id=to_core, device_id_type=MESH_IDS,
+        ).wait_recv
+        if when is None:
+            wait()
+        else:
+            pl.when(when)(wait)
+
+    def z_send(src, dst, slot):
+        put(src, dst, to_z[0], slot + z)
+        put(src, dst, to_z[1], slot + z)
+        put(src, dst, to_z[2], slot + z, when=beside)
+
+    def z_take(block, slot, i):
+        zz = zord[i]
+        take(block(zz), slot + zz)
+        if i == 2:
+            put(block(zz), block(zz), to_z[0], slot + zz, when=beside)
+
+    def z_scatter(part, land, chain, slot, chain_slot, i):
+        if i == 2:
+            put(part(zord[2]), chain, to_z[0], chain_slot, when=at_end)
+        else:
+            put(part(zord[i]), land.at[z], to_z[i], slot + z)
+
+    def z_chain(part, land, chain, slot, chain_slot):
+        @pl.when(beside)
+        def _():
+            take(chain, chain_slot)
+            mine = part(zord[2])
+            mine[...] = (mine[...].astype(F32) + chain[...].astype(F32)).astype(BF16)
+
+        put(part(zord[2]), land.at[z], to_z[2], slot + z, when=beside)
+
+    def z_zero(land):
+        @pl.when(at_end)
+        def _():
+            land[zord[2]] = jnp.zeros(land.shape[1:], land.dtype)
+
+    def z_sum(own, land, slot):
+        take(land.at[zord[0]], slot + zord[0])
+        take(land.at[zord[1]], slot + zord[1])
+        take(land.at[zord[2]], slot + zord[2], when=beside)
+        total = own.astype(F32)
+        for zz in zord:
+            total = total + land[zz].astype(F32)
+        return total
+
+    gain_a = to_column(r.ga[...].astype(F32))
+    gain_f = to_column(r.gf[...].astype(F32))
+    tok = r.tok
+    r.SEG[c] = jnp.broadcast_to(r.seg[...].astype(F32), (8, LENGTH))
+    for h in range(CS):
+        for p in range(PAIRS):
+            for j, w_ref in enumerate((r.wq, r.wk, r.wv)):
+                lanes = slice(HALF * h + 128 * p, HALF * h + 128 * p + 128)
+                r.W_MINE[h, :, HALF * p + 128 * j : HALF * p + 128 * j + 128] = (
+                    w_ref[:, lanes].astype(F32) * gain_a
+                )
+        r.W_MINE[h, :, 3 * HALF : 4 * HALF] = r.wo[:, HALF * h : HALF * h + HALF].astype(F32)
+    for j, w_ref in enumerate((r.wg, r.wu)):
+        for q, part in enumerate(split_quarters(w_ref[...].astype(F32) * gain_f)):
+            first = 4 * HALF + 2 * QUARTER * (q // CS) + QUARTER * j
+            r.W_MINE[q % CS, :, first : first + QUARTER] = part
+
+    pl.semaphore_wait(barrier, len(friends))
+
+    put(r.W_MINE.at[co], r.W_CORE.at[c], to_core, k.wc)
+    put(tok, r.X.at[c, z, x], to_x, k.xx + z)
+    put(r.SEG.at[c], r.SEG.at[c], to_core, k.segc)
+    put(tok, r.X.at[c, z, x], to_core, k.xc + s)
+    put(r.wd, r.WD.at[z, y], to_y, k.dy + z)
+    r.X[c, z, x] = tok[...]
+    r.WD[z, y] = r.wd[...]
+    r.W_CORE[c] = r.W_MINE[c]
+    z_send(r.wd, r.WD.at[z, y], k.dz)
+
+    def weight(ch):
+        return r.WA.at[ch] if ch < PAIRS else r.WO.at[c]
+
+    def weight_start(ch):
+        own = weight(ch).at[z, x, y]
+        z_send(own, own, k.wz + 4 * ch)
+        put(own, own, to_y, k.wy + 4 * ch + z)
+        put(own, own, to_x, k.wx + 4 * ch + z)
+
+    def norm_block(q, zz, xx, own=False):
+        value = unit_rows(r.X[q, zz, xx].astype(F32))[0].astype(BF16)
+        r.N1[q, zz, xx] = value
+        if own:
+            r.N1O[q] = value
+
+    def token_from_z(i):
+        z_take(lambda zz: r.X.at[c, zz, x], k.xz, i)
+        zz = zord[i]
+        put(r.X.at[c, zz, x], r.X.at[c, zz, x], to_x, k.xx + zz)
+        put(r.X.at[c, zz, x], r.X.at[c, zz, x], to_core, k.xc + XS * zz + x)
+        norm_block(c, zz, x)
+
+    def token_from_x(zz):
+        take(r.X.at[c, zz, xo], k.xx + zz)
+        put(r.X.at[c, zz, xo], r.X.at[c, zz, xo], to_core, k.xc + XS * zz + xo)
+        norm_block(c, zz, xo)
+
+    def token_from_core(zz, xx):
+        take(r.X.at[co, zz, xx], k.xc + XS * zz + xx)
+        norm_block(co, zz, xx, own=zz is z and xx is x)
+
+    def bias_lines():
+        r.BK[...] = jnp.zeros(r.BK.shape, jnp.int32)
+        r.BK[:, : 2 * LENGTH - 1] = r.buckets[...]
+        onehot = (
+            lax.broadcasted_iota(jnp.int32, (32, SPAN), 0)
+            == r.BK[:, pl.ds(pl.multiple_of(LENGTH - TOK - TOK * s, 128), SPAN)]
+        )
+        r.PH[...] = dot(r.table[...], onehot.astype(BF16))
+
+    def bias_pair(p):
+        for hh in range(2):
+            line = r.PH[pl.ds(HEADS_HERE * c + 2 * p + hh, 1), :]
+            skewed = pltpu.roll(
+                jnp.broadcast_to(line, (TOK, SPAN)), SPAN - TOK + 1, 1, stride=1, stride_axis=0
+            )
+            r.BIAS[p, TOK * hh : TOK * hh + TOK, :] = skewed[:, :LENGTH]
+
+    def masks():
+        take(r.SEG.at[co], k.segc)
+        for q in range(CS):
+            col = to_column(r.SEG[q, 0:1, pl.ds(pl.multiple_of(TOK * s, 128), TOK)])
+            r.MASK[q] = jnp.where(col == r.SEG[q, 0:1, :], 0.0, NEGATIVE)
+
+    def weight_from_z(ch, i):
+        w = weight(ch)
+        z_take(lambda zz: w.at[zz, x, y], k.wz + 4 * ch, i)
+        arrived = w.at[zord[i], x, y]
+        put(arrived, arrived, to_y, k.wy + 4 * ch + zord[i])
+        put(arrived, arrived, to_x, k.wx + 4 * ch + zord[i])
+
+    def weight_relay(ch):
+        w = weight(ch)
+        for zz in [z] + zord:
+            if RELAY_TO_Y[ch]:
+                take(w.at[zz, xo, y], k.wx + 4 * ch + zz)
+            else:
+                take(w.at[zz, x, yo], k.wy + 4 * ch + zz)
+        if RELAY_TO_Y[ch]:
+            put(w.at[:, xo, y], w.at[:, xo, y], to_y, k.wr + ch)
+        else:
+            put(w.at[:, x, yo], w.at[:, x, yo], to_x, k.wr + ch)
+
+    def weight_end(ch):
+        w = weight(ch)
+        for zz in [z] + zord:
+            if RELAY_TO_Y[ch]:
+                take(w.at[zz, x, yo], k.wy + 4 * ch + zz)
+            else:
+                take(w.at[zz, xo, y], k.wx + 4 * ch + zz)
+        take(w.at[:, xo, yo], k.wr + ch)
+
+    def gate_send(xx):
+        own = r.WG.at[z, xx, y]
+        z_send(own, own, k.gz + 4 * xx)
+        put(own, own, to_y, k.gy + 4 * xx + z)
+
+    def gate_from_z(xx, i):
+        z_take(lambda zz: r.WG.at[zz, xx, y], k.gz + 4 * xx, i)
+        arrived = r.WG.at[zord[i], xx, y]
+        put(arrived, arrived, to_y, k.gy + 4 * xx + zord[i])
+
+    def down_from_z(i):
+        z_take(lambda zz: r.WD.at[zz, y], k.dz, i)
+        put(r.WD.at[zord[i], y], r.WD.at[zord[i], y], to_y, k.dy + zord[i])
+
+    take(r.W_CORE.at[co], k.wc)
+    shard = r.W_CORE[...].reshape(CHIP_ROWS, 4 * HALF + 4 * QUARTER).astype(BF16)
+    for ch in range(PAIRS):
+        r.WA[ch, z, x, y] = shard[:, HALF * ch : HALF * ch + HALF]
+    r.WO[c, z, x, y] = shard[:, 3 * HALF : 4 * HALF]
+    for xx in range(XS):
+        first = 4 * HALF + 2 * QUARTER * xx
+        r.UB[xx] = shard[:, first : first + 2 * QUARTER]
+    weight_start(0)
+    put(r.UB.at[xo], r.WG.at[z, x, y], to_x, k.u)
+    weight_start(1)
+    weight_start(2)
+    r.WG[z, x, y] = r.UB[x]
+    z_send(tok, r.X.at[c, z, x], k.xz)
+    weight_start(PAIRS)
+    gate_send(x)
+
+    def gate_other():
+        take(r.WG.at[z, xo, y], k.u)
+        gate_send(xo)
+
+    def cot_send():
+        put(r.cot, r.COT.at[x, c], to_core, k.cotc + 0)
+        put(r.cot, r.COT.at[x, c], to_x, k.cotx)
+        r.COT[x, c] = r.cot[...]
+
+    def cot_from_x():
+        take(r.COT.at[xo, c], k.cotx)
+        put(r.COT.at[xo, c], r.COT.at[xo, c], to_core, k.cotc + 1)
+
+    def output_send():
+        put(r.WO.at[c], r.WO.at[c], to_core, k.woc)
+
+    zall = [z] + zord
+
+    def attention_pair(p):
+        w_pair = r.WA.at[p]
+
+        def one_sequence(q, carry):
+            w = w_pair[...].reshape(DIM, HALF)
+            n1 = r.N1[q].reshape(LENGTH, DIM)
+            kv = dot(n1, w[:, 128:]).astype(BF16)
+            r.KV[p, q] = kv
+            stacked = stack_heads(dot(r.N1O[q], w[:, :128]))
+            r.QS[p, q] = stacked
+            mask = r.MASK[q]
+            scores = dot_tb(stacked, kv[:, :128]) + r.BIAS[p] + jnp.concatenate((mask, mask), axis=0)
+            weights = jnp.exp(scores - jnp.max(scores, axis=1, keepdims=True))
+            probs = (weights * (1.0 / jnp.sum(weights, axis=1, keepdims=True))).astype(BF16)
+            r.PS[p, q] = probs
+            r.ATT[c, q, :, 128 * p : 128 * p + 128] = unstack_heads(dot(probs, kv[:, 128:])).astype(BF16)
+            return carry
+
+        lax.fori_loop(0, CS, one_sequence, 0)
+
+    def attended_send():
+        put(r.ATT.at[c], r.ATT.at[c], to_core, k.att)
+
+    token_from_core(z, x)
+    bias_lines()
+    gate_other()
+    weight_from_z(0, 1)
+    masks()
+    cot_send()
+    weight_from_z(1, 0)
+    bias_pair(2)
+    bias_pair(1)
+    down_from_z(1)
+    token_from_z(0)
+    weight_from_z(2, 0)
+    token_from_x(z)
+    weight_from_z(0, 0)
+    bias_pair(0)
+    weight_from_z(1, 1)
+    weight_from_z(2, 1)
+    token_from_core(zord[0], x)
+    down_from_z(0)
+    weight_from_z(1, 2)
+    token_from_core(z, xo)
+    down_from_z(2)
+    weight_from_z(0, 2)
+    token_from_x(zord[0])
+    weight_from_z(2, 2)
+    norm_block(c, z, x, own=True)
+    token_from_z(1)
+    weight_relay(0)
+    weight_relay(1)
+    weight_relay(2)
+    token_from_core(zord[0], xo)
+    token_from_z(2)
+    token_from_x(zord[1])
+    token_from_core(zord[2], x)
+    weight_end(0)
+    token_from_x(zord[2])
+    weight_from_z(PAIRS, 2)
+    token_from_core(zord[1], x)
+    weight_end(1)
+    gate_from_z(x, 0)
+    weight_from_z(PAIRS, 0)
+    weight_from_z(PAIRS, 1)
+    weight_end(2)
+    token_from_core(zord[2], xo)
+    token_from_core(zord[1], xo)
+    gate_from_z(xo, 0)
+    attention_pair(2)
+    weight_relay(PAIRS)
+    attention_pair(0)
+    gate_from_z(xo, 2)
+    cot_from_x()
+    gate_from_z(xo, 1)
+    weight_end(PAIRS)
+    attention_pair(1)
+    output_send()
+    gate_from_z(x, 2)
+    attended_send()
+    gate_from_z(x, 1)
+    take(r.WO.at[co], k.woc)
+    take(r.ATT.at[co], k.att)
+
+    att_own = jnp.concatenate((r.ATT[0, c], r.ATT[1, c]), axis=1)
+    tokens_f = tok[...].astype(F32)
+    r.H[...] = tokens_f + jnp.concatenate(
+        (dot(att_own, r.WO[0].reshape(DIM, HALF)), dot(att_own, r.WO[1].reshape(DIM, HALF))), axis=1
+    )
+    r.N2[x, c] = unit_rows(r.H[...])[0].astype(BF16)
+    put(r.N2.at[x, c], r.N2.at[x, c], to_core, k.n2c + 0)
+    put(r.N2.at[x, c], r.N2.at[x, c], to_x, k.n2x)
+
+    for zz in [z] + zord:
+        for xx in range(XS):
+            take(r.WG.at[zz, xx, yo], k.gy + 4 * xx + zz)
+        take(r.WD.at[zz, yo], k.dy + zz)
+    take(r.COT.at[x, co], k.cotc + 0)
+    take(r.COT.at[xo, co], k.cotc + 1)
+    take(r.N2.at[x, co], k.n2c + 0)
+
+    def feed_forward(xx):
+        w_gu = r.WG[...].reshape(DIM, 2 * QUARTER)
+        w_d = r.WD[...].reshape(QUARTER, DIM)
+        n2 = r.N2[xx].reshape(2 * TOK, DIM)
+        g = r.COT[xx].reshape(2 * TOK, DIM)
+        gate = dot(n2, w_gu[:, :QUARTER])
+        up = dot(n2, w_gu[:, QUARTER:])
+        d_act = dot_tb(g, w_d)
+        square = gate * gate
+        inner = math.sqrt(2 / math.pi) * gate * (1.0 + 0.044715 * square)
+        tanh = jnp.tanh(inner)
+        half_open = 0.5 * (1.0 + tanh)
+        gelu = gate * half_open
+        slope = half_open + 0.5 * gate * (1.0 - tanh * tanh) * (
+            math.sqrt(2 / math.pi) * (1.0 + 3 * 0.044715 * square)
+        )
+        act = (gelu * up).astype(BF16)
+        r.ACT[xx] = act
+        d_gu = jnp.concatenate(
+            ((slope * (up * d_act)).astype(BF16), (gelu * d_act).astype(BF16)), axis=1
+        )
+        r.DGU[xx] = d_gu
+        r.E2[xx] = dot_tb(d_gu, w_gu).astype(BF16).reshape(CS, TOK, DIM)
+        put(r.E2.at[xx, co], r.E2C.at[xx], to_core, k.e2c + xx)
+        r.MX[xx] = dot(act, w_d).astype(BF16).reshape(CS, TOK, DIM)
+        put(r.MX.at[xx, co], r.MXC.at[xx], to_core, k.mxc + xx)
+
+    feed_forward(x)
+    take(r.N2.at[xo, c], k.n2x)
+    put(r.N2.at[xo, c], r.N2.at[xo, c], to_core, k.n2c + 1)
+    take(r.N2.at[xo, co], k.n2c + 1)
+    feed_forward(xo)
+    take(r.E2C.at[xo], k.e2c + xo)
+    r.E2S[...] = (r.E2[xo, c].astype(F32) + r.E2C[xo].astype(F32)).astype(BF16)
+    put(r.E2S, r.E2X, to_x, k.e2x)
+
+    far_first = [zord[2], zord[1], zord[0], z]
+
+    def down_grad(zz):
+        return r.GD.at[zz, y]
+
+    def gate_grad(zz):
+        return r.GG.at[zz, :, y]
+
+    def grad_from_y(part, got, slot, scatter, i):
+        zz = far_first[i]
+        take(got.at[zz], slot + zz)
+        mine = part(zz)
+        mine[...] = (mine[...].astype(F32) + got[zz].astype(F32)).astype(BF16)
+        if i < 3:
+            z_scatter(part, *scatter, 2 - i)
+
+    down_scatter = (r.GDZ, r.GDC, k.rdz, k.rdc)
+    gate_scatter = (r.GGZ, r.GGC, k.rgz, k.rgc)
+
+    def down_from_y(i):
+        grad_from_y(down_grad, r.GDY, k.rdy, down_scatter, i)
+
+    def gate_from_y(i):
+        grad_from_y(gate_grad, r.GGY, k.rgy, gate_scatter, i)
+
+    def down_chain():
+        z_chain(down_grad, *down_scatter)
+
+    def gate_chain():
+        z_chain(gate_grad, *gate_scatter)
+
+    def chip_grad(ch, value):
+        r.GA[ch] = value.astype(BF16).reshape(ZS, XS, YS, CHIP_ROWS, HALF)
+        if HEAVY_X[ch]:
+            put(r.GA.at[ch, :, xo], r.GA1.at[ch], to_x, k.ra1 + ch)
+        else:
+            put(r.GA.at[ch, :, :, yo], r.GA1.at[ch], to_y, k.ra1 + ch)
+
+    def chip_step1(ch):
+        take(r.GA1.at[ch], k.ra1 + ch)
+        if HEAVY_X[ch]:
+            r.GA[ch, :, x] = (r.GA[ch, :, x].astype(F32) + r.GA1[ch].astype(F32)).astype(BF16)
+            put(r.GA.at[ch, :, x, yo], r.GA2.at[ch], to_y, k.ra2 + ch)
+        else:
+            r.GA[ch, :, :, y] = (r.GA[ch, :, :, y].astype(F32) + r.GA1[ch].astype(F32)).astype(BF16)
+            put(r.GA.at[ch, :, xo, y], r.GA2.at[ch], to_x, k.ra2 + ch)
+
+    def chip_scatter(ch):
+        return (lambda zz: r.GA.at[ch, zz, x, y]), r.GAZ.at[ch], r.GAC.at[ch], k.raz + 4 * ch, k.rac + ch
+
+    def chip_step2(ch):
+        take(r.GA2.at[ch], k.ra2 + ch)
+        r.GA[ch, :, x, y] = (r.GA[ch, :, x, y].astype(F32) + r.GA2[ch].astype(F32)).astype(BF16)
+        for i in (2, 1, 0):
+            z_scatter(*chip_scatter(ch), i)
+
+    def chip_chain(ch):
+        z_chain(*chip_scatter(ch))
+
+    def chip_end(ch):
+        total = z_sum(r.GA[ch, z, x, y], r.GAZ.at[ch], k.raz + 4 * ch)
+        r.FA[:, :, HALF * ch : HALF * ch + HALF] = total.reshape(CS, SHARD, HALF)
+
+    reverse = (
+        lax.broadcasted_iota(jnp.int32, (TOK, TOK), 0) + lax.broadcasted_iota(jnp.int32, (TOK, TOK), 1)
+        == TOK - 1
+    ).astype(BF16)
+    reverse2 = jnp.concatenate((reverse, reverse), axis=1)
+
+    def attention_pair_back(p):
+        def one_sequence(q, carry):
+            d_out = stack_heads(r.DO[q, :, 128 * p : 128 * p + 128].astype(F32))
+            kv = r.KV.at[p, q]
+            probs = r.PS[p, q]
+            weighted = probs.astype(F32) * dot_tb(d_out, kv[:, 128:])
+            delta = jnp.sum(weighted, axis=1, keepdims=True)
+            d_scores = (weighted - probs.astype(F32) * delta).astype(BF16)
+            r.DS[q] = d_scores
+            r.DQ[p, q] = unstack_heads(dot(d_scores, kv[:, :128])).astype(BF16)
+            r.DKV[p, q, :128] = dot_ta(r.QS[p, q], d_scores).astype(BF16)
+            r.DKV[p, q, 128:] = dot_ta(d_out, probs).astype(BF16)
+            return carry
+
+        lax.fori_loop(0, CS, one_sequence, 0)
+        kv_grad = dot(r.DKV[p, 0], r.N1[0].reshape(LENGTH, DIM)) + dot(
+            r.DKV[p, 1], r.N1[1].reshape(LENGTH, DIM)
+        )
+        own_rows = r.N1O[...].reshape(CS * TOK, DIM)
+        q_grad = dot_ta(r.DQ[p].reshape(CS * TOK, 128), own_rows)
+        chip_grad(p, jnp.concatenate((q_grad, kv_grad), axis=0).astype(BF16).T)
+        for hh in range(2):
+            both = r.DS[:, TOK * hh : TOK * hh + TOK, :].reshape(CS * TOK, LENGTH)
+            padded = jnp.concatenate((dot(reverse2, both), jnp.zeros((TOK, TOK), F32)), axis=1)
+            placed = pltpu.roll(padded, 0, 1, stride=1, stride_axis=0)
+            r.DG[2 * p + hh : 2 * p + hh + 1, :] = jnp.sum(placed, axis=0, keepdims=True)
+
+    w_kv = jnp.concatenate([r.WA[p].reshape(DIM, HALF)[:, 128:] for p in range(PAIRS)], axis=1)
+
+    def token_grad(q, zz):
+        lanes = pl.ds(pl.multiple_of(XS * TOK * zz, 128), XS * TOK)
+        d_kv = r.DKV[:, q, :, lanes].reshape(PAIRS * 256, XS * TOK)
+        out = dot(w_kv, d_kv)
+        for xx in range(XS):
+            r.DN[q, zz, xx] = out[:, TOK * xx : TOK * xx + TOK].astype(BF16)
+        if zz is z:
+            total = r.DN[q, z, x].astype(F32)
+            for p in range(PAIRS):
+                total = total + dot_tb(r.WA[p].reshape(DIM, HALF)[:, :128], r.DQ[p, q])
+            r.DN[q, z, x] = total.astype(BF16)
+
+    def token_exchange(zz):
+        token_grad(co, zz)
+        put(r.DN.at[co, zz], r.DNC.at[zz], to_core, k.dnc + zz)
+        token_grad(c, zz)
+
+    def token_to_x(zz):
+        take(r.DNC.at[zz], k.dnc + zz)
+        r.DN[c, zz] = (r.DN[c, zz].astype(F32) + r.DNC[zz].astype(F32)).astype(BF16)
+        put(r.DN.at[c, zz, xo], r.DNX.at[zz], to_x, k.dnx + zz)
+
+    def token_part(zz):
+        return r.DN.at[c, zz, x]
+
+    token_scatter = (r.DNZ, r.DNT, k.dnz, k.dnt)
+
+    def token_chain():
+        z_chain(token_part, *token_scatter)
+
+    def token_to_z(i):
+        zz = far_first[i]
+        take(r.DNX.at[zz], k.dnx + zz)
+        r.DN[c, zz, x] = (r.DN[c, zz, x].astype(F32) + r.DNX[zz].astype(F32)).astype(BF16)
+        if i < 3:
+            z_scatter(token_part, *token_scatter, 2 - i)
+
+    def grads_down():
+        cot_all = r.COT[...].reshape(4 * TOK, DIM)
+        r.GD[...] = dot_ta(r.ACT[...].reshape(4 * TOK, QUARTER), cot_all).astype(BF16).reshape(
+            ZS, YS, DOWN_ROWS, DIM
+        )
+        for zz in far_first:
+            put(r.GD.at[zz, yo], r.GDY.at[zz], to_y, k.rdy + zz)
+
+    def grads_gate():
+        n2_all = r.N2[...].reshape(4 * TOK, DIM)
+        d_gu_all = r.DGU[...].reshape(4 * TOK, 2 * QUARTER)
+        r.GG[...] = dot_ta(n2_all, d_gu_all).astype(BF16).reshape(ZS, XS, YS, CHIP_ROWS, 2 * QUARTER)
+        for zz in far_first:
+            put(r.GG.at[zz, :, yo], r.GGY.at[zz], to_y, k.rgy + zz)
+
+    def zeros():
+        z_zero(r.GDZ)
+        z_zero(r.GGZ)
+        z_zero(r.DNZ)
+        for ch in range(CHUNKS):
+            z_zero(r.GAZ.at[ch])
+
+    def hidden_back():
+        take(r.E2C.at[x], k.e2c + x)
+        take(r.E2X, k.e2x)
+        e2 = r.E2[x, c].astype(F32) + r.E2C[x].astype(F32) + r.E2X[...].astype(F32)
+        n2_own, r2 = unit_rows(r.H[...])
+        r.DH[...] = r.cot[...].astype(F32) + r2 * (
+            e2 - n2_own * jnp.mean(e2 * n2_own, axis=1, keepdims=True)
+        )
+        r.DB[c] = r.DH[...].astype(BF16)
+        put(r.DB.at[c], r.DB.at[c], to_core, k.db)
+
+    def mixed_send():
+        take(r.MXC.at[xo], k.mxc + xo)
+        r.MXS[...] = (r.MX[xo, c].astype(F32) + r.MXC[xo].astype(F32)).astype(BF16)
+        put(r.MXS, r.MXX, to_x, k.mxx)
+
+    def mixed_end():
+        take(r.MXC.at[x], k.mxc + x)
+        take(r.MXX, k.mxx)
+        r.mixed[...] = (
+            r.H[...] + r.MX[x, c].astype(F32) + r.MXC[x].astype(F32) + r.MXX[...].astype(F32)
+        ).astype(BF16)
+
+    def attended_back():
+        take(r.DB.at[co], k.db)
+        db_all = r.DB[...].reshape(CS * TOK, DIM)
+        rows = [r.WO[h, pl.ds(2 * c, 2)].reshape(HALF, HALF) for h in range(CS)]
+        d_att = dot_tb(db_all[:, :HALF], rows[0]) + dot_tb(db_all[:, HALF:], rows[1])
+        r.DO[...] = d_att.astype(BF16).reshape(CS, TOK, HALF)
+
+    def grads_output():
+        att_all = jnp.concatenate(
+            [jnp.concatenate((r.ATT[0, q], r.ATT[1, q]), axis=1) for q in range(CS)], axis=0
+        )
+        db_cols = r.DB[:, :, pl.ds(pl.multiple_of(HALF * c, 128), HALF)].reshape(CS * TOK, HALF)
+        chip_grad(PAIRS, dot_ta(att_all, db_cols))
+
+    def table_start():
+        r.DG[HEADS_HERE:, :] = jnp.zeros((8 - HEADS_HERE, SPAN), F32)
+        onehot_back = (
+            lax.broadcasted_iota(jnp.int32, (128, SPAN), 0)
+            == r.BK[:, pl.ds(pl.multiple_of(LENGTH - TOK - TOK * s, 128), SPAN)]
+        ).astype(F32)
+        r.T1[...] = lax.dot_general(
+            r.DG[...], onehot_back, (((1,), (1,)), ((), ())), precision=HIGHEST, preferred_element_type=F32
+        )
+        put(r.T1, r.TY, to_y, k.ty)
+
+    def table_to_x():
+        take(r.TY, k.ty)
+        r.T2[...] = r.T1[...] + r.TY[...]
+        put(r.T2, r.TX, to_x, k.tx)
+
+    def table_to_z():
+        take(r.TX, k.tx)
+        r.T3[...] = r.T2[...] + r.TX[...]
+        for who in to_z:
+            put(r.T3, r.TZ.at[z], who, k.tz + z)
+        r.TZ[z] = r.T3[...]
+
+    def table_to_core():
+        for zz in zord:
+            take(r.TZ.at[zz], k.tz + zz)
+        r.TO[c] = (r.TZ[0] + r.TZ[1]) + (r.TZ[2] + r.TZ[3])
+        put(r.TO.at[c], r.TO.at[c], to_core, k.tc)
+
+    def table_end():
+        take(r.TO.at[co], k.tc)
+        for q in range(CS):
+            r.gtab[HEADS_HERE * q : HEADS_HERE * q + HEADS_HERE, :] = r.TO[q, :HEADS_HERE, :32]
+
+    def down_end():
+        r.gwd[...] = z_sum(r.GD[z, y], r.GDZ, k.rdz)
+
+    def gate_to_x():
+        total = z_sum(r.GG[z, :, y], r.GGZ, k.rgz)
+        r.F4S[...] = total.astype(BF16)
+        put(r.F4S.at[xo], r.F4X, to_x, k.f4x)
+
+    def gate_to_core():
+        take(r.F4X, k.f4x)
+        r.F4S2[:, x] = r.F4S[x].astype(F32).reshape(CS, SHARD, 2 * QUARTER)
+        r.F4S2[:, xo] = r.F4X[...].astype(F32).reshape(CS, SHARD, 2 * QUARTER)
+        put(r.F4S2.at[co], r.F4.at[c], to_core, k.f4)
+        r.F4[c] = r.F4S2[c]
+
+    def gate_end():
+        take(r.F4.at[co], k.f4)
+        quarters = [r.F4[q % CS, q // CS] for q in range(BATCH_DEVICES)]
+        gate_total = join_quarters([quarter[:, :QUARTER] for quarter in quarters])
+        up_total = join_quarters([quarter[:, QUARTER:] for quarter in quarters])
+        r.gwg[...] = gate_total * gain_f
+        r.gwu[...] = up_total * gain_f
+        r.ggf[...] = to_row(
+            jnp.sum(
+                gate_total * r.wg[...].astype(F32) + up_total * r.wu[...].astype(F32), axis=1, keepdims=True
+            )
+        )
+
+    def token_end():
+        e1 = z_sum(r.DN[c, z, x], r.DNZ, k.dnz).T
+        n1_own, r1 = unit_rows(tok[...].astype(F32))
+        r.tg[...] = (
+            r.DH[...] + r1 * (e1 - n1_own * jnp.mean(e1 * n1_own, axis=1, keepdims=True))
+        ).astype(BF16)
+
+    def chips_to_core():
+        put(r.FA.at[co], r.F2.at[c], to_core, k.f2)
+        r.F2[c] = r.FA[c]
+
+    def chips_end():
+        take(r.F2.at[co], k.f2)
+        gain_total = jnp.zeros((SHARD, 1), F32)
+        for j, (w_ref, out_ref) in enumerate(((r.wq, r.gwq), (r.wk, r.gwk), (r.wv, r.gwv))):
+            for h in range(CS):
+                for p in range(PAIRS):
+                    lanes = slice(HALF * h + 128 * p, HALF * h + 128 * p + 128)
+                    grad = r.F2[h, :, HALF * p + 128 * j : HALF * p + 128 * j + 128]
+                    gain_total = gain_total + jnp.sum(
+                        grad * w_ref[:, lanes].astype(F32), axis=1, keepdims=True
+                    )
+                    out_ref[:, lanes] = grad * gain_a
+        r.gga[...] = to_row(gain_total)
+        for h in range(CS):
+            r.gwo[:, HALF * h : HALF * h + HALF] = r.F2[h, :, 3 * HALF :]
+
+    grads_down()
+    grads_gate()
+    mixed_send()
+    hidden_back()
+    down_from_y(1)
+    attended_back()
+    down_from_y(0)
+    grads_output()
+    attention_pair_back(2)
+    chip_step1(PAIRS)
+    zeros()
+    gate_from_y(0)
+    gate_from_y(1)
+    down_chain()
+    attention_pair_back(0)
+    gate_from_y(2)
+    down_from_y(2)
+    attention_pair_back(1)
+    token_exchange(far_first[3])
+    token_exchange(far_first[0])
+    table_start()
+    chip_step1(2)
+    chip_step2(PAIRS)
+    chip_step1(0)
+    gate_chain()
+    token_to_x(far_first[0])
+    token_exchange(far_first[1])
+    token_exchange(far_first[2])
+    table_to_x()
+    chip_step2(2)
+    chip_chain(PAIRS)
+    token_to_x(far_first[1])
+    chip_step2(0)
+    chip_step1(1)
+    down_from_y(3)
+    gate_from_y(3)
+    chip_step2(1)
+    mixed_end()
+    token_to_z(0)
+    down_end()
+    chip_chain(2)
+    chip_chain(0)
+    chip_end(PAIRS)
+    table_to_z()
+    token_to_x(far_first[2])
+    gate_to_x()
+    token_to_z(1)
+    token_to_x(far_first[3])
+    chip_chain(1)
+    chip_end(0)
+    token_to_z(2)
+    chip_end(2)
+    token_chain()
+    gate_to_core()
+    chip_end(1)
+    table_to_core()
+    chips_to_core()
+    gate_end()
+    table_end()
+    token_to_z(3)
+    chips_end()
+    token_end()
+    for copy, when in sent:
+        if when is None:
+            copy.wait_send()
+        else:
+            pl.when(when)(copy.wait_send)
+
+
+def finish_kernel(*refs):
+    count = len(refs) // 2
+    for src, dst in zip(refs[:count], refs[count:]):
+        dst[...] = src[...]
+
+
+def fused_device(
+    tokens, segments, buckets, gain_attn, w_query, w_key, w_value, w_output,
+    gain_ffn, w_gate, w_up, w_down, bucket_bias_matrix, cotangent,
+):
+    operands = (
+        tokens.reshape(TOK, DIM),
+        cotangent.reshape(TOK, DIM),
+        segments.reshape(1, LENGTH),
+        buckets.reshape(1, 2 * LENGTH - 1),
+        bucket_bias_matrix.T,
+        gain_attn.reshape(1, SHARD),
+        gain_ffn.reshape(1, SHARD),
+        w_query, w_key, w_value, w_output, w_gate, w_up, w_down,
+    )
+    out_shape = [jax.ShapeDtypeStruct(shape, dtype) for shape, dtype in OUTPUTS.values()]
+    in_vmem = pl.BlockSpec(memory_space=pltpu.VMEM)
+    outs = pl.pallas_call(
+        layer_kernel,
+        out_shape=out_shape,
+        in_specs=[in_vmem] * len(operands),
+        out_specs=[in_vmem] * len(out_shape),
+        scratch_shapes=[pltpu.VMEM(shape, dtype) for shape, dtype in SCRATCH.values()]
+        + [pltpu.SemaphoreType.DMA((SEND_COUNT,)), pltpu.SemaphoreType.DMA((RECV_COUNT,))],
+        compiler_params=pltpu.CompilerParams(
+            collective_id=0, has_side_effects=True, vmem_limit_bytes=63 * 2**20
+        ),
+        name="layer",
+    )(*operands)
+    outs = pl.pallas_call(
+        finish_kernel,
+        out_shape=out_shape,
+        in_specs=[in_vmem] * len(out_shape),
+        out_specs=[in_vmem] * len(out_shape),
+        name="finish",
+    )(*outs)
+    mixed, tokens_grad, gga, gwq, gwk, gwv, gwo, ggf, gwg, gwu, gwd, table_grad = outs
+    return (
+        mixed.reshape(tokens.shape), tokens_grad.reshape(tokens.shape), gga.reshape(SHARD),
+        gwq, gwk, gwv, gwo, ggf.reshape(SHARD), gwg, gwu, gwd, table_grad.T,
+    )
+
+
+def fits_fused(mesh):
+    return mesh.shape["seq"] == SEQ_DEVICES and mesh.shape["batch"] == BATCH_DEVICES
+
+
 def solution(mesh):
     return jax.shard_map(
-        on_device,
+        fused_device if fits_fused(mesh) else on_device,
         mesh=mesh,
         in_specs=(
             P("seq", "batch", None),

time: 1550 us -> 144 us (0.09)
  waiting for transfers between devices: 1180 us -> 0 us
  local copies, waits for them, and re-layouts: 148 us -> 0 us
  Pallas kernels: 0 us -> 143 us
  blocking collectives: 81.7 us -> 0 us
  matrix products: 70.5 us -> 0 us
  other arithmetic: 24.1 us -> 0 us
  loops' own time: 23.1 us -> 0 us
    reduce_scatter x8 -> x0, waiting for transfers between devices: 823 us -> none  [the longest x1 121 us: on_device(): lax.psum_scatter(grad_up, ('seq', 'batch'), scatter_dimension=0, tiled=True)]
    all_gather x9 -> x0, waiting for transfers between devices: 352 us -> none  [the longest x1 57.4 us: on_device(): lax.all_gather(w_gate, ('seq', 'batch'), axis=0, tiled=True)]
    pallas_call x0 -> x2, Pallas kernels: none -> 143 us  [the longest x1 140 us: fused_device(): pl.pallas_call(layer_kernel, out_shape=out_shape, in_specs=[in_vmem] * le...]
    unnamed x2 -> x0, blocking collectives: 81.7 us -> none
    dot_general x41 -> x0, matrix products: 70.5 us -> none  [the longest x7 18.9 us: weight_grad(): jnp.einsum('tsk,tsn->kn', left_side, grad_rows, preferred_element_type=jn...]
    reshape x8 -> x0, local copies, waits for them, and re-layouts: 46.2 us -> none  [the longest x4 27.5 us: position_bias(): skewed = tiled[:, :query_rows * span].reshape(head_count, query_rows, span)]
    while x58 -> x0, local copies, waits for them, and re-layouts: 38.5 us -> none
    slice x8 -> x0, local copies, waits for them, and re-layouts: 29.4 us -> none  [the longest x4 18.8 us: position_bias(): return (onehot, skewed[:, :, query_rows - 1:query_rows - 1 + key_rows])]
  transfers between devices with their start and end apart: 17 -> 0, of which waited for: 16 -> 0; matrix products, arithmetic and copies ran while one was open for 7% -> 0% of each run, Pallas kernels for 0% -> 0%
where the time goes in v2:
time: 144 us; the launch traced here: 143 us
  Pallas kernels  143 us (99%)
    pallas_call x1, Pallas kernels, fused_device(): pl.pallas_call(layer_kernel, out_shape=out_shape, in_specs=[in_vmem] * le...  140 us

profile of v2, /device:TPU:0, one launch (start us, length us, event | category | flops | bytes accessed | tf_op | source)
XLA Modules:
  0.0 143.4 jit_solution(12133769866198728719)
XLA Ops:
  0.6 140.2 %layer.1 = (bf16[128,768]{1,0:T(8,128)(2,1)}, bf16[128,768]{1,0:T(8,128)(2,1)}, f32[1,24]{1,0:T(1,128)}, f32[24,768]{1,0:T(8,128)}, f32[24,768]{1,0:T(8,128)}, /...) custom-call(bf16[128,768]{1,0:T(8,128)(2,1)} %bitcast.12, ...), custom_call_target="tpu_custom_call" | custom-call | tf_op jit(solution)/shard_map/layer/pallas_call | solution.py:1328
  140.8 2.4 %finish.1 = (bf16[128,768]{1,0:T(8,128)(2,1)}, bf16[128,768]{1,0:T(8,128)(2,1)}, f32[1,24]{1,0:T(1,128)}, f32[24,768]{1,0:T(8,128)}, f32[24,768]{1,0:T(8,128)}, ...) custom-call(bf16[128,768]{1,0:T(8,128)(2,1)} %get-tuple-element.36.r, ...), custom_call_target="tpu_custom_call" | custom-call | tf_op jit(solution)/shard_map/finish/pallas_call | solution.py:1340

commit v3 on v2

--- a/solution.py
+++ b/solution.py
@@ -508,7 +508,7 @@
     DH=((TOK, DIM), F32),
     DB=((CS, TOK, DIM), BF16),
     DO=((CS, TOK, HALF), BF16),
-    DS=((CS, 2 * TOK, LENGTH), BF16),
+    DS=((PAIRS, CS, 2 * TOK, LENGTH), BF16),
     DQ=((PAIRS, CS, TOK, 128), BF16),
     DKV=((PAIRS, CS, 256, LENGTH), BF16),
     DG=((8, SPAN), F32),
@@ -532,7 +532,7 @@
     TZ=((ZS, 8, 128), F32),
     TO=((CS, 8, 128), F32),
 )
-SEND_COUNT = 224
+SEND_RING = 72
 SLOTS = dict(
     segc=1, wc=1, u=1, xz=4, xx=4, xc=8, wz=4 * CHUNKS, wx=4 * CHUNKS, wy=4 * CHUNKS, wr=CHUNKS, woc=1,
     gz=8, gy=8, dz=4, dy=4, cotx=1, cotc=2, att=1, n2x=1, n2c=2, mxc=2, mxx=1, e2c=2, e2x=1,
@@ -562,8 +562,14 @@
 )
 
 
-RELAY_TO_Y = (True, True, True, True)
-HEAVY_X = (True, True, True, True)
+RELAY_TO_Y = (True, True, False, False)
+HEAVY_X = (False, False, True, True)
+FAR_DIRECT_CHIP = (False, False, False, False)
+FAR_DIRECT_TOKEN = False
+SPREAD_TOKEN = False
+SPREAD_CHIP = (False, False, False, False)
+SPREAD_GATE = False
+SPREAD_DOWN = False
 
 
 def layer_kernel(*refs):
@@ -593,9 +599,18 @@
 
     sent = []
 
+    def sent_wait(i):
+        copy, when = sent[i]
+        if when is None:
+            copy.wait_send()
+        else:
+            pl.when(when)(copy.wait_send)
+
     def put(src, dst, who, slot, when=None):
+        if len(sent) >= SEND_RING:
+            sent_wait(len(sent) - SEND_RING)
         copy = pltpu.make_async_remote_copy(
-            src_ref=src, dst_ref=dst, send_sem=ssem.at[len(sent)], recv_sem=rsem.at[slot],
+            src_ref=src, dst_ref=dst, send_sem=ssem.at[len(sent) % SEND_RING], recv_sem=rsem.at[slot],
             device_id=who, device_id_type=MESH_IDS,
         )
         if when is None:
@@ -614,19 +629,21 @@
         else:
             pl.when(when)(wait)
 
-    def z_send(src, dst, slot):
+    def z_send(src, dst, slot, direct):
         put(src, dst, to_z[0], slot + z)
         put(src, dst, to_z[1], slot + z)
-        put(src, dst, to_z[2], slot + z, when=beside)
-
-    def z_take(block, slot, i):
+        put(src, dst, to_z[2], slot + z, when=None if direct else beside)
+
+    def z_take(block, slot, i, direct):
         zz = zord[i]
         take(block(zz), slot + zz)
-        if i == 2:
+        if i == 2 and not direct:
             put(block(zz), block(zz), to_z[0], slot + zz, when=beside)
 
     def z_scatter(part, land, chain, slot, chain_slot, i):
-        if i == 2:
+        if i == 2 and chain is None:
+            put(part(zord[2]), land.at[z], to_z[2], slot + z)
+        elif i == 2:
             put(part(zord[2]), chain, to_z[0], chain_slot, when=at_end)
         else:
             put(part(zord[i]), land.at[z], to_z[i], slot + z)
@@ -645,10 +662,10 @@
         def _():
             land[zord[2]] = jnp.zeros(land.shape[1:], land.dtype)
 
-    def z_sum(own, land, slot):
+    def z_sum(own, land, slot, direct=False):
         take(land.at[zord[0]], slot + zord[0])
         take(land.at[zord[1]], slot + zord[1])
-        take(land.at[zord[2]], slot + zord[2], when=beside)
+        take(land.at[zord[2]], slot + zord[2], when=None if direct else beside)
         total = own.astype(F32)
         for zz in zord:
             total = total + land[zz].astype(F32)
@@ -677,18 +694,16 @@
     put(tok, r.X.at[c, z, x], to_x, k.xx + z)
     put(r.SEG.at[c], r.SEG.at[c], to_core, k.segc)
     put(tok, r.X.at[c, z, x], to_core, k.xc + s)
-    put(r.wd, r.WD.at[z, y], to_y, k.dy + z)
     r.X[c, z, x] = tok[...]
     r.WD[z, y] = r.wd[...]
     r.W_CORE[c] = r.W_MINE[c]
-    z_send(r.wd, r.WD.at[z, y], k.dz)
 
     def weight(ch):
         return r.WA.at[ch] if ch < PAIRS else r.WO.at[c]
 
     def weight_start(ch):
         own = weight(ch).at[z, x, y]
-        z_send(own, own, k.wz + 4 * ch)
+        z_send(own, own, k.wz + 4 * ch, SPREAD_CHIP[ch])
         put(own, own, to_y, k.wy + 4 * ch + z)
         put(own, own, to_x, k.wx + 4 * ch + z)
 
@@ -699,7 +714,7 @@
             r.N1O[q] = value
 
     def token_from_z(i):
-        z_take(lambda zz: r.X.at[c, zz, x], k.xz, i)
+        z_take(lambda zz: r.X.at[c, zz, x], k.xz, i, SPREAD_TOKEN)
         zz = zord[i]
         put(r.X.at[c, zz, x], r.X.at[c, zz, x], to_x, k.xx + zz)
         put(r.X.at[c, zz, x], r.X.at[c, zz, x], to_core, k.xc + XS * zz + x)
@@ -739,7 +754,7 @@
 
     def weight_from_z(ch, i):
         w = weight(ch)
-        z_take(lambda zz: w.at[zz, x, y], k.wz + 4 * ch, i)
+        z_take(lambda zz: w.at[zz, x, y], k.wz + 4 * ch, i, SPREAD_CHIP[ch])
         arrived = w.at[zord[i], x, y]
         put(arrived, arrived, to_y, k.wy + 4 * ch + zord[i])
         put(arrived, arrived, to_x, k.wx + 4 * ch + zord[i])
@@ -767,34 +782,38 @@
 
     def gate_send(xx):
         own = r.WG.at[z, xx, y]
-        z_send(own, own, k.gz + 4 * xx)
+        z_send(own, own, k.gz + 4 * xx, SPREAD_GATE)
         put(own, own, to_y, k.gy + 4 * xx + z)
 
     def gate_from_z(xx, i):
-        z_take(lambda zz: r.WG.at[zz, xx, y], k.gz + 4 * xx, i)
+        z_take(lambda zz: r.WG.at[zz, xx, y], k.gz + 4 * xx, i, SPREAD_GATE)
         arrived = r.WG.at[zord[i], xx, y]
         put(arrived, arrived, to_y, k.gy + 4 * xx + zord[i])
 
     def down_from_z(i):
-        z_take(lambda zz: r.WD.at[zz, y], k.dz, i)
+        z_take(lambda zz: r.WD.at[zz, y], k.dz, i, SPREAD_DOWN)
         put(r.WD.at[zord[i], y], r.WD.at[zord[i], y], to_y, k.dy + zord[i])
 
-    take(r.W_CORE.at[co], k.wc)
-    shard = r.W_CORE[...].reshape(CHIP_ROWS, 4 * HALF + 4 * QUARTER).astype(BF16)
-    for ch in range(PAIRS):
-        r.WA[ch, z, x, y] = shard[:, HALF * ch : HALF * ch + HALF]
-    r.WO[c, z, x, y] = shard[:, 3 * HALF : 4 * HALF]
-    for xx in range(XS):
-        first = 4 * HALF + 2 * QUARTER * xx
-        r.UB[xx] = shard[:, first : first + 2 * QUARTER]
-    weight_start(0)
-    put(r.UB.at[xo], r.WG.at[z, x, y], to_x, k.u)
-    weight_start(1)
-    weight_start(2)
-    r.WG[z, x, y] = r.UB[x]
-    z_send(tok, r.X.at[c, z, x], k.xz)
-    weight_start(PAIRS)
-    gate_send(x)
+    def tokens_send():
+        z_send(tok, r.X.at[c, z, x], k.xz, SPREAD_TOKEN)
+
+    def down_send():
+        put(r.wd, r.WD.at[z, y], to_y, k.dy + z)
+        z_send(r.wd, r.WD.at[z, y], k.dz, SPREAD_DOWN)
+
+    def shards():
+        take(r.W_CORE.at[co], k.wc)
+        shard = r.W_CORE[...].reshape(CHIP_ROWS, 4 * HALF + 4 * QUARTER).astype(BF16)
+        for ch in range(PAIRS):
+            r.WA[ch, z, x, y] = shard[:, HALF * ch : HALF * ch + HALF]
+        r.WO[c, z, x, y] = shard[:, 3 * HALF : 4 * HALF]
+        for xx in range(XS):
+            first = 4 * HALF + 2 * QUARTER * xx
+            r.UB[xx] = shard[:, first : first + 2 * QUARTER]
+        r.WG[z, x, y] = r.UB[x]
+
+    def gate_exchange():
+        put(r.UB.at[xo], r.WG.at[z, x, y], to_x, k.u)
 
     def gate_other():
         take(r.WG.at[z, xo, y], k.u)
@@ -814,87 +833,109 @@
 
     zall = [z] + zord
 
-    def attention_pair(p):
-        w_pair = r.WA.at[p]
-
-        def one_sequence(q, carry):
-            w = w_pair[...].reshape(DIM, HALF)
-            n1 = r.N1[q].reshape(LENGTH, DIM)
-            kv = dot(n1, w[:, 128:]).astype(BF16)
-            r.KV[p, q] = kv
-            stacked = stack_heads(dot(r.N1O[q], w[:, :128]))
-            r.QS[p, q] = stacked
-            mask = r.MASK[q]
-            scores = dot_tb(stacked, kv[:, :128]) + r.BIAS[p] + jnp.concatenate((mask, mask), axis=0)
-            weights = jnp.exp(scores - jnp.max(scores, axis=1, keepdims=True))
-            probs = (weights * (1.0 / jnp.sum(weights, axis=1, keepdims=True))).astype(BF16)
-            r.PS[p, q] = probs
-            r.ATT[c, q, :, 128 * p : 128 * p + 128] = unstack_heads(dot(probs, kv[:, 128:])).astype(BF16)
-            return carry
-
-        lax.fori_loop(0, CS, one_sequence, 0)
+    def keys_values(q, zz):
+        w = jnp.concatenate([r.WA[p].reshape(DIM, HALF)[:, 128:] for p in range(PAIRS)], axis=1)
+        kv = dot(r.N1[q, zz].reshape(XS * TOK, DIM), w).astype(BF16)
+        for p in range(PAIRS):
+            r.KV[p, q, pl.ds(pl.multiple_of(XS * TOK * zz, 128), XS * TOK), :] = kv[:, 256 * p : 256 * p + 256]
+
+    def queries(q):
+        for p in range(PAIRS):
+            r.QS[p, q] = stack_heads(dot(r.N1O[q], r.WA[p].reshape(DIM, HALF)[:, :128]))
+
+    def attend(p, q):
+        kv = r.KV.at[p, q]
+        stacked = r.QS[p, q]
+        mask = r.MASK[q]
+        scores = dot_tb(stacked, kv[:, :128]) + r.BIAS[p] + jnp.concatenate((mask, mask), axis=0)
+        weights = jnp.exp(scores - jnp.max(scores, axis=1, keepdims=True))
+        probs = (weights * (1.0 / jnp.sum(weights, axis=1, keepdims=True))).astype(BF16)
+        r.PS[p, q] = probs
+        r.ATT[c, q, :, 128 * p : 128 * p + 128] = unstack_heads(dot(probs, kv[:, 128:])).astype(BF16)
 
     def attended_send():
         put(r.ATT.at[c], r.ATT.at[c], to_core, k.att)
 
+    norm_block(c, z, x, own=True)
+    tokens_send()
+    cot_send()
+    bias_lines()
+    bias_pair(0)
+    shards()
+    weight_start(0)
+    gate_exchange()
+    weight_start(1)
+    weight_start(2)
+    gate_send(x)
     token_from_core(z, x)
-    bias_lines()
+    token_from_x(z)
+    masks()
+    token_from_z(0)
+    token_from_core(z, xo)
+    token_from_core(zord[0], x)
+    cot_from_x()
+    token_from_z(1)
+    weight_from_z(1, 0)
+    weight_from_z(0, 0)
+    weight_start(PAIRS)
+    bias_pair(2)
     gate_other()
+    token_from_x(zord[0])
+    gate_from_z(x, 0)
     weight_from_z(0, 1)
-    masks()
-    cot_send()
-    weight_from_z(1, 0)
-    bias_pair(2)
+    token_from_core(zord[1], x)
     bias_pair(1)
-    down_from_z(1)
-    token_from_z(0)
+    token_from_z(2)
+    weight_from_z(2, 1)
+    weight_from_z(0, 2)
     weight_from_z(2, 0)
-    token_from_x(z)
-    weight_from_z(0, 0)
-    bias_pair(0)
     weight_from_z(1, 1)
-    weight_from_z(2, 1)
-    token_from_core(zord[0], x)
+    token_from_x(zord[1])
+    weight_from_z(1, 2)
+    weight_from_z(PAIRS, 0)
+    down_send()
+    weight_from_z(2, 2)
+    token_from_core(zord[1], xo)
+    weight_relay(0)
+    weight_relay(2)
+    weight_relay(1)
+    token_from_x(zord[2])
+    weight_from_z(PAIRS, 1)
+    gate_from_z(xo, 0)
+    weight_from_z(PAIRS, 2)
+    token_from_core(zord[0], xo)
     down_from_z(0)
-    weight_from_z(1, 2)
-    token_from_core(z, xo)
-    down_from_z(2)
-    weight_from_z(0, 2)
-    token_from_x(zord[0])
-    weight_from_z(2, 2)
-    norm_block(c, z, x, own=True)
-    token_from_z(1)
-    weight_relay(0)
-    weight_relay(1)
-    weight_relay(2)
-    token_from_core(zord[0], xo)
-    token_from_z(2)
-    token_from_x(zord[1])
+    gate_from_z(xo, 1)
+    gate_from_z(x, 1)
     token_from_core(zord[2], x)
     weight_end(0)
-    token_from_x(zord[2])
-    weight_from_z(PAIRS, 2)
-    token_from_core(zord[1], x)
+    token_from_core(zord[2], xo)
+    gate_from_z(x, 2)
+    weight_end(2)
     weight_end(1)
-    gate_from_z(x, 0)
-    weight_from_z(PAIRS, 0)
-    weight_from_z(PAIRS, 1)
-    weight_end(2)
-    token_from_core(zord[2], xo)
-    token_from_core(zord[1], xo)
-    gate_from_z(xo, 0)
-    attention_pair(2)
+    keys_values(co, zord[0])
+    keys_values(c, zord[1])
+    keys_values(co, z)
+    keys_values(co, zord[2])
+    keys_values(c, z)
+    keys_values(co, zord[1])
+    queries(1)
+    keys_values(c, zord[0])
+    queries(0)
+    attend(0, co)
+    down_from_z(1)
     weight_relay(PAIRS)
-    attention_pair(0)
+    keys_values(c, zord[2])
+    attend(1, co)
+    down_from_z(2)
+    attend(0, c)
+    attend(1, c)
+    weight_end(PAIRS)
+    output_send()
+    attend(2, c)
+    attend(2, co)
+    attended_send()
     gate_from_z(xo, 2)
-    cot_from_x()
-    gate_from_z(xo, 1)
-    weight_end(PAIRS)
-    attention_pair(1)
-    output_send()
-    gate_from_z(x, 2)
-    attended_send()
-    gate_from_z(x, 1)
     take(r.WO.at[co], k.woc)
     take(r.ATT.at[co], k.att)
 
@@ -947,10 +988,6 @@
     put(r.N2.at[xo, c], r.N2.at[xo, c], to_core, k.n2c + 1)
     take(r.N2.at[xo, co], k.n2c + 1)
     feed_forward(xo)
-    take(r.E2C.at[xo], k.e2c + xo)
-    r.E2S[...] = (r.E2[xo, c].astype(F32) + r.E2C[xo].astype(F32)).astype(BF16)
-    put(r.E2S, r.E2X, to_x, k.e2x)
-
     far_first = [zord[2], zord[1], zord[0], z]
 
     def down_grad(zz):
@@ -999,7 +1036,8 @@
             put(r.GA.at[ch, :, xo, y], r.GA2.at[ch], to_x, k.ra2 + ch)
 
     def chip_scatter(ch):
-        return (lambda zz: r.GA.at[ch, zz, x, y]), r.GAZ.at[ch], r.GAC.at[ch], k.raz + 4 * ch, k.rac + ch
+        chain = None if FAR_DIRECT_CHIP[ch] else r.GAC.at[ch]
+        return (lambda zz: r.GA.at[ch, zz, x, y]), r.GAZ.at[ch], chain, k.raz + 4 * ch, k.rac + ch
 
     def chip_step2(ch):
         take(r.GA2.at[ch], k.ra2 + ch)
@@ -1008,10 +1046,11 @@
             z_scatter(*chip_scatter(ch), i)
 
     def chip_chain(ch):
-        z_chain(*chip_scatter(ch))
+        if not FAR_DIRECT_CHIP[ch]:
+            z_chain(*chip_scatter(ch))
 
     def chip_end(ch):
-        total = z_sum(r.GA[ch, z, x, y], r.GAZ.at[ch], k.raz + 4 * ch)
+        total = z_sum(r.GA[ch, z, x, y], r.GAZ.at[ch], k.raz + 4 * ch, FAR_DIRECT_CHIP[ch])
         r.FA[:, :, HALF * ch : HALF * ch + HALF] = total.reshape(CS, SHARD, HALF)
 
     reverse = (
@@ -1020,29 +1059,29 @@
     ).astype(BF16)
     reverse2 = jnp.concatenate((reverse, reverse), axis=1)
 
-    def attention_pair_back(p):
-        def one_sequence(q, carry):
-            d_out = stack_heads(r.DO[q, :, 128 * p : 128 * p + 128].astype(F32))
-            kv = r.KV.at[p, q]
-            probs = r.PS[p, q]
-            weighted = probs.astype(F32) * dot_tb(d_out, kv[:, 128:])
-            delta = jnp.sum(weighted, axis=1, keepdims=True)
-            d_scores = (weighted - probs.astype(F32) * delta).astype(BF16)
-            r.DS[q] = d_scores
-            r.DQ[p, q] = unstack_heads(dot(d_scores, kv[:, :128])).astype(BF16)
-            r.DKV[p, q, :128] = dot_ta(r.QS[p, q], d_scores).astype(BF16)
-            r.DKV[p, q, 128:] = dot_ta(d_out, probs).astype(BF16)
-            return carry
-
-        lax.fori_loop(0, CS, one_sequence, 0)
+    def attend_back(p, q):
+        d_out = stack_heads(r.DO[q, :, 128 * p : 128 * p + 128].astype(F32))
+        kv = r.KV.at[p, q]
+        probs = r.PS[p, q]
+        weighted = probs.astype(F32) * dot_tb(d_out, kv[:, 128:])
+        delta = jnp.sum(weighted, axis=1, keepdims=True)
+        d_scores = (weighted - probs.astype(F32) * delta).astype(BF16)
+        r.DS[p, q] = d_scores
+        r.DQ[p, q] = unstack_heads(dot(d_scores, kv[:, :128])).astype(BF16)
+        r.DKV[p, q, :128] = dot_ta(r.QS[p, q], d_scores).astype(BF16)
+        r.DKV[p, q, 128:] = dot_ta(d_out, probs).astype(BF16)
+
+    def grads_pair(p):
         kv_grad = dot(r.DKV[p, 0], r.N1[0].reshape(LENGTH, DIM)) + dot(
             r.DKV[p, 1], r.N1[1].reshape(LENGTH, DIM)
         )
         own_rows = r.N1O[...].reshape(CS * TOK, DIM)
         q_grad = dot_ta(r.DQ[p].reshape(CS * TOK, 128), own_rows)
         chip_grad(p, jnp.concatenate((q_grad, kv_grad), axis=0).astype(BF16).T)
+
+    def grads_bias(p):
         for hh in range(2):
-            both = r.DS[:, TOK * hh : TOK * hh + TOK, :].reshape(CS * TOK, LENGTH)
+            both = r.DS[p, :, TOK * hh : TOK * hh + TOK, :].reshape(CS * TOK, LENGTH)
             padded = jnp.concatenate((dot(reverse2, both), jnp.zeros((TOK, TOK), F32)), axis=1)
             placed = pltpu.roll(padded, 0, 1, stride=1, stride_axis=0)
             r.DG[2 * p + hh : 2 * p + hh + 1, :] = jnp.sum(placed, axis=0, keepdims=True)
@@ -1074,10 +1113,11 @@
     def token_part(zz):
         return r.DN.at[c, zz, x]
 
-    token_scatter = (r.DNZ, r.DNT, k.dnz, k.dnt)
+    token_scatter = (r.DNZ, None if FAR_DIRECT_TOKEN else r.DNT, k.dnz, k.dnt)
 
     def token_chain():
-        z_chain(token_part, *token_scatter)
+        if not FAR_DIRECT_TOKEN:
+            z_chain(token_part, *token_scatter)
 
     def token_to_z(i):
         zz = far_first[i]
@@ -1104,9 +1144,16 @@
     def zeros():
         z_zero(r.GDZ)
         z_zero(r.GGZ)
-        z_zero(r.DNZ)
+        if not FAR_DIRECT_TOKEN:
+            z_zero(r.DNZ)
         for ch in range(CHUNKS):
-            z_zero(r.GAZ.at[ch])
+            if not FAR_DIRECT_CHIP[ch]:
+                z_zero(r.GAZ.at[ch])
+
+    def hidden_send():
+        take(r.E2C.at[xo], k.e2c + xo)
+        r.E2S[...] = (r.E2[xo, c].astype(F32) + r.E2C[xo].astype(F32)).astype(BF16)
+        put(r.E2S, r.E2X, to_x, k.e2x)
 
     def hidden_back():
         take(r.E2C.at[x], k.e2c + x)
@@ -1208,7 +1255,7 @@
         )
 
     def token_end():
-        e1 = z_sum(r.DN[c, z, x], r.DNZ, k.dnz).T
+        e1 = z_sum(r.DN[c, z, x], r.DNZ, k.dnz, FAR_DIRECT_TOKEN).T
         n1_own, r1 = unit_rows(tok[...].astype(F32))
         r.tg[...] = (
             r.DH[...] + r1 * (e1 - n1_own * jnp.mean(e1 * n1_own, axis=1, keepdims=True))
@@ -1235,72 +1282,79 @@
             r.gwo[:, HALF * h : HALF * h + HALF] = r.F2[h, :, 3 * HALF :]
 
     grads_down()
+    hidden_send()
     grads_gate()
     mixed_send()
+    zeros()
+    down_from_y(0)
     hidden_back()
+    attended_back()
+    grads_output()
     down_from_y(1)
-    attended_back()
-    down_from_y(0)
-    grads_output()
-    attention_pair_back(2)
+    down_from_y(2)
+    attend_back(2, 1)
+    attend_back(1, 0)
+    mixed_end()
+    down_chain()
+    attend_back(2, 0)
+    grads_bias(2)
+    attend_back(1, 1)
+    grads_pair(2)
+    gate_from_y(0)
+    attend_back(0, 1)
+    attend_back(0, 0)
+    token_exchange(far_first[1])
+    down_from_y(3)
     chip_step1(PAIRS)
-    zeros()
-    gate_from_y(0)
+    token_exchange(far_first[3])
     gate_from_y(1)
-    down_chain()
-    attention_pair_back(0)
+    down_end()
+    token_exchange(far_first[2])
+    grads_pair(1)
+    token_to_x(far_first[1])
+    gate_chain()
+    grads_pair(0)
+    token_exchange(far_first[0])
+    chip_step1(2)
     gate_from_y(2)
-    down_from_y(2)
-    attention_pair_back(1)
-    token_exchange(far_first[3])
-    token_exchange(far_first[0])
+    token_to_x(far_first[0])
+    token_to_x(far_first[2])
+    grads_bias(0)
+    grads_bias(1)
     table_start()
-    chip_step1(2)
+    gate_from_y(3)
+    token_to_z(1)
+    token_to_z(0)
+    token_to_x(far_first[3])
     chip_step2(PAIRS)
+    token_to_z(2)
+    chip_step1(1)
+    gate_to_x()
+    chip_chain(PAIRS)
+    token_chain()
+    token_to_z(3)
     chip_step1(0)
-    gate_chain()
-    token_to_x(far_first[0])
-    token_exchange(far_first[1])
-    token_exchange(far_first[2])
+    chip_step2(1)
+    gate_to_core()
+    chip_chain(1)
+    chip_step2(2)
+    token_end()
+    gate_end()
+    chip_step2(0)
+    chip_end(PAIRS)
     table_to_x()
-    chip_step2(2)
-    chip_chain(PAIRS)
-    token_to_x(far_first[1])
-    chip_step2(0)
-    chip_step1(1)
-    down_from_y(3)
-    gate_from_y(3)
-    chip_step2(1)
-    mixed_end()
-    token_to_z(0)
-    down_end()
     chip_chain(2)
     chip_chain(0)
-    chip_end(PAIRS)
     table_to_z()
-    token_to_x(far_first[2])
-    gate_to_x()
-    token_to_z(1)
-    token_to_x(far_first[3])
-    chip_chain(1)
+    chip_end(1)
+    chip_end(2)
     chip_end(0)
-    token_to_z(2)
-    chip_end(2)
-    token_chain()
-    gate_to_core()
-    chip_end(1)
+    chips_to_core()
     table_to_core()
-    chips_to_core()
-    gate_end()
+    chips_end()
     table_end()
-    token_to_z(3)
-    chips_end()
-    token_end()
-    for copy, when in sent:
-        if when is None:
-            copy.wait_send()
-        else:
-            pl.when(when)(copy.wait_send)
+    for i in range(len(sent) - SEND_RING, len(sent)):
+        sent_wait(i)
 
 
 def finish_kernel(*refs):
@@ -1331,7 +1385,7 @@
         in_specs=[in_vmem] * len(operands),
         out_specs=[in_vmem] * len(out_shape),
         scratch_shapes=[pltpu.VMEM(shape, dtype) for shape, dtype in SCRATCH.values()]
-        + [pltpu.SemaphoreType.DMA((SEND_COUNT,)), pltpu.SemaphoreType.DMA((RECV_COUNT,))],
+        + [pltpu.SemaphoreType.DMA((SEND_RING,)), pltpu.SemaphoreType.DMA((RECV_COUNT,))],
         compiler_params=pltpu.CompilerParams(
             collective_id=0, has_side_effects=True, vmem_limit_bytes=63 * 2**20
         ),

time: 144 us -> 138 us (0.958)
  Pallas kernels: 143 us -> 137 us
    pallas_call x1, Pallas kernels: 140 us -> 135 us  [fused_device(): pl.pallas_call(layer_kernel, out_shape=out_shape, in_specs=[in_vmem] * le...]
where the time goes in v3:
time: 138 us
  Pallas kernels  137 us (99%)
    pallas_call x1, Pallas kernels, fused_device(): pl.pallas_call(layer_kernel, out_shape=out_shape, in_specs=[in_vmem] * le...  135 us

profile of v3, /device:TPU:0, one launch (start us, length us, event | category | flops | bytes accessed | tf_op | source)
XLA Modules:
  0.0 138.0 jit_solution(13760033982092162411)
XLA Ops:
  0.6 134.8 %layer.1 = (bf16[128,768]{1,0:T(8,128)(2,1)}, bf16[128,768]{1,0:T(8,128)(2,1)}, f32[1,24]{1,0:T(1,128)}, f32[24,768]{1,0:T(8,128)}, f32[24,768]{1,0:T(8,128)}, /...) custom-call(bf16[128,768]{1,0:T(8,128)(2,1)} %bitcast.12, ...), custom_call_target="tpu_custom_call" | custom-call | tf_op jit(solution)/shard_map/layer/pallas_call | solution.py:1382
  135.4 2.4 %finish.1 = (bf16[128,768]{1,0:T(8,128)(2,1)}, bf16[128,768]{1,0:T(8,128)(2,1)}, f32[1,24]{1,0:T(1,128)}, f32[24,768]{1,0:T(8,128)}, f32[24,768]{1,0:T(8,128)}, ...) custom-call(bf16[128,768]{1,0:T(8,128)(2,1)} %get-tuple-element.36.r, ...), custom_call_target="tpu_custom_call" | custom-call | tf_op jit(solution)/shard_map/finish/pallas_call | solution.py:1394

commit v4 on v3

--- a/solution.py
+++ b/solution.py
@@ -475,8 +475,8 @@
     SEG=((CS, 8, LENGTH), F32),
     BK=((1, 2 * LENGTH), jnp.int32),
     PH=((2 * CS * PAIRS, SPAN), F32),
-    BIAS=((PAIRS, 2 * TOK, LENGTH), F32),
-    MASK=((CS, TOK, LENGTH), F32),
+    BIAS=((PAIRS, 2 * TOK, LENGTH), BF16),
+    MASK=((CS, TOK, LENGTH), BF16),
     KV=((PAIRS, CS, LENGTH, 256), BF16),
     QS=((PAIRS, CS, 2 * TOK, 128), BF16),
     PS=((PAIRS, CS, 2 * TOK, LENGTH), BF16),
@@ -508,7 +508,6 @@
     DH=((TOK, DIM), F32),
     DB=((CS, TOK, DIM), BF16),
     DO=((CS, TOK, HALF), BF16),
-    DS=((PAIRS, CS, 2 * TOK, LENGTH), BF16),
     DQ=((PAIRS, CS, TOK, 128), BF16),
     DKV=((PAIRS, CS, 256, LENGTH), BF16),
     DG=((8, SPAN), F32),
@@ -517,8 +516,9 @@
     GA2=((CHUNKS, ZS, CHIP_ROWS, HALF), BF16),
     GAZ=((CHUNKS, ZS, CHIP_ROWS, HALF), BF16),
     GAC=((CHUNKS, CHIP_ROWS, HALF), BF16),
-    FA=((CS, SHARD, 4 * HALF), F32),
-    F2=((CS, SHARD, 4 * HALF), F32),
+    FA=((CHUNKS, CS, SHARD, HALF), F32),
+    F2=((CHUNKS, CS, SHARD, HALF), F32),
+    GT=((PAIRS, SHARD, 128), F32),
     DN=((CS, ZS, XS, DIM, TOK), BF16),
     DNC=((ZS, XS, DIM, TOK), BF16),
     DNX=((ZS, DIM, TOK), BF16),
@@ -535,9 +535,9 @@
 SEND_RING = 72
 SLOTS = dict(
     segc=1, wc=1, u=1, xz=4, xx=4, xc=8, wz=4 * CHUNKS, wx=4 * CHUNKS, wy=4 * CHUNKS, wr=CHUNKS, woc=1,
-    gz=8, gy=8, dz=4, dy=4, cotx=1, cotc=2, att=1, n2x=1, n2c=2, mxc=2, mxx=1, e2c=2, e2x=1,
+    gz=8, gy=8, dz=4, dy=4, cotx=1, cotc=2, att=2, n2x=1, n2c=2, mxc=2, mxx=1, e2c=2, e2x=1,
     rdy=4, rdz=4, rdc=1, rgy=4, rgz=4, rgc=1, f4x=1, f4=1, db=1,
-    ra1=CHUNKS, ra2=CHUNKS, raz=4 * CHUNKS, rac=CHUNKS, f2=1,
+    ra1=CHUNKS, ra2=CHUNKS, raz=4 * CHUNKS, rac=CHUNKS, f2=CHUNKS,
     dnc=4, dnx=4, dnz=4, dnt=1, ty=1, tx=1, tz=4, tc=1,
 )
 RECV_COUNT = sum(SLOTS.values())
@@ -744,13 +744,13 @@
             skewed = pltpu.roll(
                 jnp.broadcast_to(line, (TOK, SPAN)), SPAN - TOK + 1, 1, stride=1, stride_axis=0
             )
-            r.BIAS[p, TOK * hh : TOK * hh + TOK, :] = skewed[:, :LENGTH]
+            r.BIAS[p, TOK * hh : TOK * hh + TOK, :] = skewed[:, :LENGTH].astype(BF16)
 
     def masks():
         take(r.SEG.at[co], k.segc)
         for q in range(CS):
             col = to_column(r.SEG[q, 0:1, pl.ds(pl.multiple_of(TOK * s, 128), TOK)])
-            r.MASK[q] = jnp.where(col == r.SEG[q, 0:1, :], 0.0, NEGATIVE)
+            r.MASK[q] = jnp.where(col == r.SEG[q, 0:1, :], 0.0, NEGATIVE).astype(BF16)
 
     def weight_from_z(ch, i):
         w = weight(ch)
@@ -794,8 +794,9 @@
         z_take(lambda zz: r.WD.at[zz, y], k.dz, i, SPREAD_DOWN)
         put(r.WD.at[zord[i], y], r.WD.at[zord[i], y], to_y, k.dy + zord[i])
 
-    def tokens_send():
-        z_send(tok, r.X.at[c, z, x], k.xz, SPREAD_TOKEN)
+    def tokens_send(i):
+        far = beside if i == 2 and not SPREAD_TOKEN else None
+        put(tok, r.X.at[c, z, x], to_z[i], k.xz + z, when=far)
 
     def down_send():
         put(r.wd, r.WD.at[z, y], to_y, k.dy + z)
@@ -834,10 +835,10 @@
     zall = [z] + zord
 
     def keys_values(q, zz):
-        w = jnp.concatenate([r.WA[p].reshape(DIM, HALF)[:, 128:] for p in range(PAIRS)], axis=1)
-        kv = dot(r.N1[q, zz].reshape(XS * TOK, DIM), w).astype(BF16)
+        rows = r.N1[q, zz].reshape(XS * TOK, DIM)
         for p in range(PAIRS):
-            r.KV[p, q, pl.ds(pl.multiple_of(XS * TOK * zz, 128), XS * TOK), :] = kv[:, 256 * p : 256 * p + 256]
+            kv = dot(rows, r.WA[p].reshape(DIM, HALF)[:, 128:])
+            r.KV[p, q, pl.ds(pl.multiple_of(XS * TOK * zz, 128), XS * TOK), :] = kv.astype(BF16)
 
     def queries(q):
         for p in range(PAIRS):
@@ -846,98 +847,101 @@
     def attend(p, q):
         kv = r.KV.at[p, q]
         stacked = r.QS[p, q]
-        mask = r.MASK[q]
-        scores = dot_tb(stacked, kv[:, :128]) + r.BIAS[p] + jnp.concatenate((mask, mask), axis=0)
+        mask = r.MASK[q].astype(F32)
+        scores = dot_tb(stacked, kv[:, :128]) + r.BIAS[p].astype(F32) + jnp.concatenate((mask, mask), axis=0)
         weights = jnp.exp(scores - jnp.max(scores, axis=1, keepdims=True))
         probs = (weights * (1.0 / jnp.sum(weights, axis=1, keepdims=True))).astype(BF16)
         r.PS[p, q] = probs
         r.ATT[c, q, :, 128 * p : 128 * p + 128] = unstack_heads(dot(probs, kv[:, 128:])).astype(BF16)
 
-    def attended_send():
-        put(r.ATT.at[c], r.ATT.at[c], to_core, k.att)
-
+    def attended_send(q):
+        put(r.ATT.at[c, q], r.ATT.at[c, q], to_core, k.att + (1 if q is c else 0))
+
+    bias_lines()
+    tokens_send(0)
+    shards()
+    gate_exchange()
+    weight_start(PAIRS)
+    token_from_core(z, x)
+    weight_start(1)
+    bias_pair(0)
+    weight_start(2)
+    bias_pair(2)
+    masks()
+    weight_from_z(PAIRS, 0)
+    weight_start(0)
+    token_from_z(0)
+    tokens_send(1)
+    tokens_send(2)
+    gate_other()
+    down_send()
+    weight_from_z(PAIRS, 1)
+    token_from_x(z)
+    weight_from_z(2, 0)
+    weight_from_z(2, 1)
+    token_from_core(z, xo)
+    weight_from_z(1, 0)
+    weight_from_z(1, 1)
+    weight_from_z(PAIRS, 2)
+    weight_from_z(0, 1)
     norm_block(c, z, x, own=True)
-    tokens_send()
-    cot_send()
-    bias_lines()
-    bias_pair(0)
-    shards()
-    weight_start(0)
-    gate_exchange()
-    weight_start(1)
-    weight_start(2)
     gate_send(x)
-    token_from_core(z, x)
-    token_from_x(z)
-    masks()
-    token_from_z(0)
-    token_from_core(z, xo)
+    weight_from_z(0, 0)
+    bias_pair(1)
+    token_from_x(zord[0])
     token_from_core(zord[0], x)
-    cot_from_x()
+    token_from_core(zord[0], xo)
+    weight_from_z(0, 2)
+    weight_from_z(1, 2)
+    weight_from_z(2, 2)
     token_from_z(1)
-    weight_from_z(1, 0)
-    weight_from_z(0, 0)
-    weight_start(PAIRS)
-    bias_pair(2)
-    gate_other()
-    token_from_x(zord[0])
+    weight_relay(0)
+    weight_relay(1)
+    token_from_core(zord[1], x)
+    weight_relay(2)
     gate_from_z(x, 0)
-    weight_from_z(0, 1)
-    token_from_core(zord[1], x)
-    bias_pair(1)
     token_from_z(2)
-    weight_from_z(2, 1)
-    weight_from_z(0, 2)
-    weight_from_z(2, 0)
-    weight_from_z(1, 1)
+    down_from_z(0)
+    gate_from_z(xo, 0)
     token_from_x(zord[1])
-    weight_from_z(1, 2)
-    weight_from_z(PAIRS, 0)
-    down_send()
-    weight_from_z(2, 2)
-    token_from_core(zord[1], xo)
-    weight_relay(0)
-    weight_relay(2)
-    weight_relay(1)
-    token_from_x(zord[2])
-    weight_from_z(PAIRS, 1)
-    gate_from_z(xo, 0)
-    weight_from_z(PAIRS, 2)
-    token_from_core(zord[0], xo)
-    down_from_z(0)
+    weight_relay(PAIRS)
     gate_from_z(xo, 1)
-    gate_from_z(x, 1)
-    token_from_core(zord[2], x)
     weight_end(0)
-    token_from_core(zord[2], xo)
-    gate_from_z(x, 2)
+    weight_end(1)
     weight_end(2)
-    weight_end(1)
-    keys_values(co, zord[0])
-    keys_values(c, zord[1])
-    keys_values(co, z)
-    keys_values(co, zord[2])
-    keys_values(c, z)
-    keys_values(co, zord[1])
     queries(1)
     keys_values(c, zord[0])
+    keys_values(co, z)
+    token_from_core(zord[1], xo)
+    keys_values(c, zord[1])
+    keys_values(c, z)
+    down_from_z(1)
+    token_from_core(zord[2], x)
     queries(0)
+    token_from_x(zord[2])
+    keys_values(c, zord[2])
+    keys_values(co, zord[1])
+    cot_send()
+    keys_values(co, zord[0])
+    gate_from_z(xo, 2)
+    weight_end(PAIRS)
+    token_from_core(zord[2], xo)
+    keys_values(co, zord[2])
+    attend(1, co)
     attend(0, co)
-    down_from_z(1)
-    weight_relay(PAIRS)
-    keys_values(c, zord[2])
-    attend(1, co)
     down_from_z(2)
+    gate_from_z(x, 1)
+    output_send()
     attend(0, c)
+    attend(2, co)
+    attended_send(co)
+    gate_from_z(x, 2)
+    cot_from_x()
+    attend(2, c)
     attend(1, c)
-    weight_end(PAIRS)
-    output_send()
-    attend(2, c)
-    attend(2, co)
-    attended_send()
-    gate_from_z(xo, 2)
+    attended_send(c)
     take(r.WO.at[co], k.woc)
-    take(r.ATT.at[co], k.att)
+    take(r.ATT.at[co, c], k.att)
 
     att_own = jnp.concatenate((r.ATT[0, c], r.ATT[1, c]), axis=1)
     tokens_f = tok[...].astype(F32)
@@ -1051,7 +1055,9 @@
 
     def chip_end(ch):
         total = z_sum(r.GA[ch, z, x, y], r.GAZ.at[ch], k.raz + 4 * ch, FAR_DIRECT_CHIP[ch])
-        r.FA[:, :, HALF * ch : HALF * ch + HALF] = total.reshape(CS, SHARD, HALF)
+        r.FA[ch] = total.reshape(CS, SHARD, HALF)
+        put(r.FA.at[ch, co], r.F2.at[ch, c], to_core, k.f2 + ch)
+        r.F2[ch, c] = r.FA[ch, c]
 
     reverse = (
         lax.broadcasted_iota(jnp.int32, (TOK, TOK), 0) + lax.broadcasted_iota(jnp.int32, (TOK, TOK), 1)
@@ -1066,10 +1072,10 @@
         weighted = probs.astype(F32) * dot_tb(d_out, kv[:, 128:])
         delta = jnp.sum(weighted, axis=1, keepdims=True)
         d_scores = (weighted - probs.astype(F32) * delta).astype(BF16)
-        r.DS[p, q] = d_scores
         r.DQ[p, q] = unstack_heads(dot(d_scores, kv[:, :128])).astype(BF16)
         r.DKV[p, q, :128] = dot_ta(r.QS[p, q], d_scores).astype(BF16)
         r.DKV[p, q, 128:] = dot_ta(d_out, probs).astype(BF16)
+        r.PS[p, q] = d_scores
 
     def grads_pair(p):
         kv_grad = dot(r.DKV[p, 0], r.N1[0].reshape(LENGTH, DIM)) + dot(
@@ -1081,7 +1087,7 @@
 
     def grads_bias(p):
         for hh in range(2):
-            both = r.DS[p, :, TOK * hh : TOK * hh + TOK, :].reshape(CS * TOK, LENGTH)
+            both = r.PS[p, :, TOK * hh : TOK * hh + TOK, :].reshape(CS * TOK, LENGTH)
             padded = jnp.concatenate((dot(reverse2, both), jnp.zeros((TOK, TOK), F32)), axis=1)
             placed = pltpu.roll(padded, 0, 1, stride=1, stride_axis=0)
             r.DG[2 * p + hh : 2 * p + hh + 1, :] = jnp.sum(placed, axis=0, keepdims=True)
@@ -1178,14 +1184,15 @@
             r.H[...] + r.MX[x, c].astype(F32) + r.MXC[x].astype(F32) + r.MXX[...].astype(F32)
         ).astype(BF16)
 
-    def attended_back():
-        take(r.DB.at[co], k.db)
-        db_all = r.DB[...].reshape(CS * TOK, DIM)
+    def attended_back(q):
+        if q is co:
+            take(r.DB.at[co], k.db)
         rows = [r.WO[h, pl.ds(2 * c, 2)].reshape(HALF, HALF) for h in range(CS)]
-        d_att = dot_tb(db_all[:, :HALF], rows[0]) + dot_tb(db_all[:, HALF:], rows[1])
-        r.DO[...] = d_att.astype(BF16).reshape(CS, TOK, HALF)
+        d_att = dot_tb(r.DB[q, :, :HALF], rows[0]) + dot_tb(r.DB[q, :, HALF:], rows[1])
+        r.DO[q] = d_att.astype(BF16)
 
     def grads_output():
+        take(r.ATT.at[co, co], k.att + 1)
         att_all = jnp.concatenate(
             [jnp.concatenate((r.ATT[0, q], r.ATT[1, q]), axis=1) for q in range(CS)], axis=0
         )
@@ -1261,98 +1268,100 @@
             r.DH[...] + r1 * (e1 - n1_own * jnp.mean(e1 * n1_own, axis=1, keepdims=True))
         ).astype(BF16)
 
-    def chips_to_core():
-        put(r.FA.at[co], r.F2.at[c], to_core, k.f2)
-        r.F2[c] = r.FA[c]
-
-    def chips_end():
-        take(r.F2.at[co], k.f2)
-        gain_total = jnp.zeros((SHARD, 1), F32)
+    def chip_out(ch):
+        take(r.F2.at[ch, co], k.f2 + ch)
+        if ch == PAIRS:
+            for h in range(CS):
+                r.gwo[:, HALF * h : HALF * h + HALF] = r.F2[ch, h]
+            return
+        gain_part = jnp.zeros((SHARD, 128), F32)
         for j, (w_ref, out_ref) in enumerate(((r.wq, r.gwq), (r.wk, r.gwk), (r.wv, r.gwv))):
             for h in range(CS):
-                for p in range(PAIRS):
-                    lanes = slice(HALF * h + 128 * p, HALF * h + 128 * p + 128)
-                    grad = r.F2[h, :, HALF * p + 128 * j : HALF * p + 128 * j + 128]
-                    gain_total = gain_total + jnp.sum(
-                        grad * w_ref[:, lanes].astype(F32), axis=1, keepdims=True
-                    )
-                    out_ref[:, lanes] = grad * gain_a
-        r.gga[...] = to_row(gain_total)
-        for h in range(CS):
-            r.gwo[:, HALF * h : HALF * h + HALF] = r.F2[h, :, 3 * HALF :]
-
+                lanes = slice(HALF * h + 128 * ch, HALF * h + 128 * ch + 128)
+                grad = r.F2[ch, h, :, 128 * j : 128 * j + 128]
+                gain_part = gain_part + grad * w_ref[:, lanes].astype(F32)
+                out_ref[:, lanes] = grad * gain_a
+        r.GT[ch] = gain_part
+
+    def gain_end():
+        r.gga[...] = to_row(jnp.sum(r.GT[0] + r.GT[1] + r.GT[2], axis=1, keepdims=True))
+
+    zeros()
     grads_down()
     hidden_send()
+    down_from_y(0)
     grads_gate()
     mixed_send()
-    zeros()
-    down_from_y(0)
     hidden_back()
-    attended_back()
+    down_from_y(2)
+    attended_back(c)
+    down_from_y(1)
+    attend_back(2, c)
+    attended_back(co)
     grads_output()
-    down_from_y(1)
-    down_from_y(2)
-    attend_back(2, 1)
-    attend_back(1, 0)
+    attend_back(0, c)
     mixed_end()
+    attend_back(2, co)
+    down_from_y(3)
     down_chain()
-    attend_back(2, 0)
-    grads_bias(2)
-    attend_back(1, 1)
+    attend_back(1, co)
     grads_pair(2)
     gate_from_y(0)
-    attend_back(0, 1)
-    attend_back(0, 0)
+    attend_back(0, co)
+    grads_bias(2)
+    attend_back(1, c)
     token_exchange(far_first[1])
-    down_from_y(3)
+    gate_from_y(1)
     chip_step1(PAIRS)
-    token_exchange(far_first[3])
-    gate_from_y(1)
     down_end()
+    token_exchange(far_first[0])
+    grads_bias(1)
+    grads_bias(0)
+    table_start()
+    token_to_x(far_first[1])
+    gate_from_y(2)
     token_exchange(far_first[2])
-    grads_pair(1)
-    token_to_x(far_first[1])
     gate_chain()
     grads_pair(0)
-    token_exchange(far_first[0])
+    token_to_x(far_first[0])
+    token_exchange(far_first[3])
+    grads_pair(1)
+    token_to_x(far_first[2])
+    token_to_z(1)
+    table_to_x()
+    chip_step2(PAIRS)
     chip_step1(2)
-    gate_from_y(2)
-    token_to_x(far_first[0])
-    token_to_x(far_first[2])
-    grads_bias(0)
-    grads_bias(1)
-    table_start()
+    token_to_z(0)
     gate_from_y(3)
-    token_to_z(1)
-    token_to_z(0)
+    chip_step1(0)
+    chip_chain(PAIRS)
+    table_to_z()
     token_to_x(far_first[3])
-    chip_step2(PAIRS)
     token_to_z(2)
+    chip_step2(0)
+    token_chain()
+    chip_end(PAIRS)
     chip_step1(1)
+    chip_out(PAIRS)
+    table_to_core()
+    chip_step2(2)
+    table_end()
     gate_to_x()
-    chip_chain(PAIRS)
-    token_chain()
     token_to_z(3)
-    chip_step1(0)
     chip_step2(1)
+    chip_chain(0)
+    token_end()
+    chip_end(0)
+    chip_chain(2)
     gate_to_core()
+    chip_out(0)
     chip_chain(1)
-    chip_step2(2)
-    token_end()
     gate_end()
-    chip_step2(0)
-    chip_end(PAIRS)
-    table_to_x()
-    chip_chain(2)
-    chip_chain(0)
-    table_to_z()
+    chip_end(2)
     chip_end(1)
-    chip_end(2)
-    chip_end(0)
-    chips_to_core()
-    table_to_core()
-    chips_end()
-    table_end()
+    chip_out(2)
+    chip_out(1)
+    gain_end()
     for i in range(len(sent) - SEND_RING, len(sent)):
         sent_wait(i)
 

time: 138 us -> 136 us (0.986)
  Pallas kernels: 137 us -> 134 us
    pallas_call x1, Pallas kernels: 135 us -> 132 us  [fused_device(): pl.pallas_call(layer_kernel, out_shape=out_shape, in_specs=[in_vmem] * le...]
where the time goes in v4:
time: 136 us; the launch traced here: 135 us
  Pallas kernels  134 us (99%)
    pallas_call x1, Pallas kernels, fused_device(): pl.pallas_call(layer_kernel, out_shape=out_shape, in_specs=[in_vmem] * le...  132 us

profile of v4, /device:TPU:0, one launch (start us, length us, event | category | flops | bytes accessed | tf_op | source)
XLA Modules:
  0.0 135.3 jit_solution(12916919011662986102)
XLA Ops:
  0.6 132.0 %layer.1 = (bf16[128,768]{1,0:T(8,128)(2,1)}, bf16[128,768]{1,0:T(8,128)(2,1)}, f32[1,24]{1,0:T(1,128)}, f32[24,768]{1,0:T(8,128)}, f32[24,768]{1,0:T(8,128)}, /...) custom-call(bf16[128,768]{1,0:T(8,128)(2,1)} %bitcast.12, ...), custom_call_target="tpu_custom_call" | custom-call | tf_op jit(solution)/shard_map/layer/pallas_call | solution.py:1391
  132.7 2.4 %finish.1 = (bf16[128,768]{1,0:T(8,128)(2,1)}, bf16[128,768]{1,0:T(8,128)(2,1)}, f32[1,24]{1,0:T(1,128)}, f32[24,768]{1,0:T(8,128)}, f32[24,768]{1,0:T(8,128)}, ...) custom-call(bf16[128,768]{1,0:T(8,128)(2,1)} %get-tuple-element.36.r, ...), custom_call_target="tpu_custom_call" | custom-call | tf_op jit(solution)/shard_map/finish/pallas_call | solution.py:1403

commit v5 on v4

--- a/solution.py
+++ b/solution.py
@@ -537,7 +537,7 @@
     segc=1, wc=1, u=1, xz=4, xx=4, xc=8, wz=4 * CHUNKS, wx=4 * CHUNKS, wy=4 * CHUNKS, wr=CHUNKS, woc=1,
     gz=8, gy=8, dz=4, dy=4, cotx=1, cotc=2, att=2, n2x=1, n2c=2, mxc=2, mxx=1, e2c=2, e2x=1,
     rdy=4, rdz=4, rdc=1, rgy=4, rgz=4, rgc=1, f4x=1, f4=1, db=1,
-    ra1=CHUNKS, ra2=CHUNKS, raz=4 * CHUNKS, rac=CHUNKS, f2=CHUNKS,
+    ra1=2 * CHUNKS, ra2=CHUNKS, raz=4 * CHUNKS, rac=CHUNKS, f2=CHUNKS,
     dnc=4, dnx=4, dnz=4, dnt=1, ty=1, tx=1, tz=4, tc=1,
 )
 RECV_COUNT = sum(SLOTS.values())
@@ -857,89 +857,89 @@
     def attended_send(q):
         put(r.ATT.at[c, q], r.ATT.at[c, q], to_core, k.att + (1 if q is c else 0))
 
+    tokens_send(0)
+    norm_block(c, z, x, own=True)
     bias_lines()
-    tokens_send(0)
+    bias_pair(2)
     shards()
+    weight_start(PAIRS)
+    masks()
     gate_exchange()
-    weight_start(PAIRS)
+    bias_pair(0)
+    weight_start(1)
+    weight_start(2)
+    weight_start(0)
+    tokens_send(1)
     token_from_core(z, x)
-    weight_start(1)
-    bias_pair(0)
-    weight_start(2)
-    bias_pair(2)
-    masks()
+    tokens_send(2)
+    token_from_x(z)
+    bias_pair(1)
+    token_from_z(0)
     weight_from_z(PAIRS, 0)
-    weight_start(0)
-    token_from_z(0)
-    tokens_send(1)
-    tokens_send(2)
+    weight_from_z(1, 0)
+    weight_from_z(1, 1)
     gate_other()
     down_send()
+    weight_from_z(0, 0)
+    weight_from_z(2, 1)
+    token_from_core(zord[0], x)
+    weight_from_z(2, 0)
+    weight_from_z(1, 2)
+    token_from_core(z, xo)
+    gate_send(x)
     weight_from_z(PAIRS, 1)
-    token_from_x(z)
-    weight_from_z(2, 0)
-    weight_from_z(2, 1)
-    token_from_core(z, xo)
-    weight_from_z(1, 0)
-    weight_from_z(1, 1)
+    weight_from_z(0, 1)
+    token_from_x(zord[0])
+    token_from_core(zord[0], xo)
+    weight_from_z(2, 2)
+    weight_relay(1)
+    weight_from_z(0, 2)
     weight_from_z(PAIRS, 2)
-    weight_from_z(0, 1)
-    norm_block(c, z, x, own=True)
-    gate_send(x)
-    weight_from_z(0, 0)
-    bias_pair(1)
-    token_from_x(zord[0])
-    token_from_core(zord[0], x)
-    token_from_core(zord[0], xo)
-    weight_from_z(0, 2)
-    weight_from_z(1, 2)
-    weight_from_z(2, 2)
     token_from_z(1)
     weight_relay(0)
-    weight_relay(1)
+    down_from_z(0)
+    weight_relay(2)
+    gate_from_z(xo, 0)
+    token_from_z(2)
+    weight_relay(PAIRS)
+    cot_send()
+    gate_from_z(x, 0)
     token_from_core(zord[1], x)
-    weight_relay(2)
-    gate_from_z(x, 0)
-    token_from_z(2)
-    down_from_z(0)
-    gate_from_z(xo, 0)
+    weight_end(1)
+    gate_from_z(xo, 1)
     token_from_x(zord[1])
-    weight_relay(PAIRS)
-    gate_from_z(xo, 1)
+    weight_end(2)
     weight_end(0)
-    weight_end(1)
-    weight_end(2)
+    keys_values(co, zord[0])
+    keys_values(co, z)
+    queries(0)
+    keys_values(c, zord[1])
+    keys_values(c, zord[0])
+    token_from_core(zord[2], x)
+    gate_from_z(xo, 2)
+    keys_values(c, z)
+    token_from_core(zord[1], xo)
     queries(1)
-    keys_values(c, zord[0])
-    keys_values(co, z)
-    token_from_core(zord[1], xo)
-    keys_values(c, zord[1])
-    keys_values(c, z)
     down_from_z(1)
-    token_from_core(zord[2], x)
-    queries(0)
     token_from_x(zord[2])
     keys_values(c, zord[2])
     keys_values(co, zord[1])
-    cot_send()
-    keys_values(co, zord[0])
-    gate_from_z(xo, 2)
-    weight_end(PAIRS)
+    attend(2, c)
+    gate_from_z(x, 1)
     token_from_core(zord[2], xo)
     keys_values(co, zord[2])
-    attend(1, co)
+    weight_end(PAIRS)
     attend(0, co)
     down_from_z(2)
-    gate_from_z(x, 1)
     output_send()
-    attend(0, c)
+    attend(1, co)
     attend(2, co)
     attended_send(co)
+    attend(0, c)
+    attend(1, c)
+    attended_send(c)
     gate_from_z(x, 2)
     cot_from_x()
-    attend(2, c)
-    attend(1, c)
-    attended_send(c)
     take(r.WO.at[co], k.woc)
     take(r.ATT.at[co, c], k.att)
 
@@ -1026,17 +1026,20 @@
     def chip_grad(ch, value):
         r.GA[ch] = value.astype(BF16).reshape(ZS, XS, YS, CHIP_ROWS, HALF)
         if HEAVY_X[ch]:
-            put(r.GA.at[ch, :, xo], r.GA1.at[ch], to_x, k.ra1 + ch)
+            put(r.GA.at[ch, :, xo, yo], r.GA1.at[ch, :, yo], to_x, k.ra1 + 2 * ch)
+            put(r.GA.at[ch, :, xo, y], r.GA1.at[ch, :, y], to_x, k.ra1 + 2 * ch + 1)
         else:
-            put(r.GA.at[ch, :, :, yo], r.GA1.at[ch], to_y, k.ra1 + ch)
+            put(r.GA.at[ch, :, xo, yo], r.GA1.at[ch, :, xo], to_y, k.ra1 + 2 * ch)
+            put(r.GA.at[ch, :, x, yo], r.GA1.at[ch, :, x], to_y, k.ra1 + 2 * ch + 1)
 
     def chip_step1(ch):
-        take(r.GA1.at[ch], k.ra1 + ch)
         if HEAVY_X[ch]:
-            r.GA[ch, :, x] = (r.GA[ch, :, x].astype(F32) + r.GA1[ch].astype(F32)).astype(BF16)
+            take(r.GA1.at[ch, :, yo], k.ra1 + 2 * ch)
+            r.GA[ch, :, x, yo] = (r.GA[ch, :, x, yo].astype(F32) + r.GA1[ch, :, yo].astype(F32)).astype(BF16)
             put(r.GA.at[ch, :, x, yo], r.GA2.at[ch], to_y, k.ra2 + ch)
         else:
-            r.GA[ch, :, :, y] = (r.GA[ch, :, :, y].astype(F32) + r.GA1[ch].astype(F32)).astype(BF16)
+            take(r.GA1.at[ch, :, xo], k.ra1 + 2 * ch)
+            r.GA[ch, :, xo, y] = (r.GA[ch, :, xo, y].astype(F32) + r.GA1[ch, :, xo].astype(F32)).astype(BF16)
             put(r.GA.at[ch, :, xo, y], r.GA2.at[ch], to_x, k.ra2 + ch)
 
     def chip_scatter(ch):
@@ -1044,8 +1047,12 @@
         return (lambda zz: r.GA.at[ch, zz, x, y]), r.GAZ.at[ch], chain, k.raz + 4 * ch, k.rac + ch
 
     def chip_step2(ch):
+        here = y if HEAVY_X[ch] else x
+        take(r.GA1.at[ch, :, here], k.ra1 + 2 * ch + 1)
         take(r.GA2.at[ch], k.ra2 + ch)
-        r.GA[ch, :, x, y] = (r.GA[ch, :, x, y].astype(F32) + r.GA2[ch].astype(F32)).astype(BF16)
+        r.GA[ch, :, x, y] = (
+            r.GA[ch, :, x, y].astype(F32) + r.GA1[ch, :, here].astype(F32) + r.GA2[ch].astype(F32)
+        ).astype(BF16)
         for i in (2, 1, 0):
             z_scatter(*chip_scatter(ch), i)
 
@@ -1290,76 +1297,76 @@
     grads_down()
     hidden_send()
     down_from_y(0)
+    mixed_send()
     grads_gate()
-    mixed_send()
     hidden_back()
+    down_from_y(1)
+    attended_back(c)
+    attend_back(2, c)
     down_from_y(2)
-    attended_back(c)
-    down_from_y(1)
-    attend_back(2, c)
     attended_back(co)
+    down_chain()
     grads_output()
     attend_back(0, c)
-    mixed_end()
+    attend_back(1, co)
     attend_back(2, co)
     down_from_y(3)
-    down_chain()
-    attend_back(1, co)
+    grads_bias(2)
     grads_pair(2)
     gate_from_y(0)
     attend_back(0, co)
-    grads_bias(2)
+    down_end()
+    chip_step1(PAIRS)
     attend_back(1, c)
     token_exchange(far_first[1])
+    mixed_end()
+    grads_bias(1)
     gate_from_y(1)
-    chip_step1(PAIRS)
-    down_end()
-    token_exchange(far_first[0])
-    grads_bias(1)
     grads_bias(0)
-    table_start()
-    token_to_x(far_first[1])
-    gate_from_y(2)
     token_exchange(far_first[2])
     gate_chain()
+    token_to_x(far_first[1])
+    table_start()
+    token_exchange(far_first[0])
+    chip_step1(2)
+    gate_from_y(2)
     grads_pair(0)
+    grads_pair(1)
     token_to_x(far_first[0])
+    token_to_x(far_first[2])
     token_exchange(far_first[3])
-    grads_pair(1)
-    token_to_x(far_first[2])
     token_to_z(1)
+    gate_from_y(3)
     table_to_x()
     chip_step2(PAIRS)
-    chip_step1(2)
+    token_to_x(far_first[3])
+    chip_chain(PAIRS)
     token_to_z(0)
-    gate_from_y(3)
+    table_to_z()
+    token_to_z(2)
     chip_step1(0)
-    chip_chain(PAIRS)
-    table_to_z()
-    token_to_x(far_first[3])
-    token_to_z(2)
-    chip_step2(0)
+    chip_step1(1)
+    gate_to_x()
+    token_to_z(3)
+    chip_step2(2)
     token_chain()
     chip_end(PAIRS)
-    chip_step1(1)
+    chip_step2(0)
+    chip_chain(2)
+    table_to_core()
     chip_out(PAIRS)
-    table_to_core()
-    chip_step2(2)
+    chip_step2(1)
+    chip_end(2)
+    gate_to_core()
+    chip_chain(0)
+    chip_out(2)
     table_end()
-    gate_to_x()
-    token_to_z(3)
-    chip_step2(1)
-    chip_chain(0)
+    chip_chain(1)
     token_end()
+    gate_end()
     chip_end(0)
-    chip_chain(2)
-    gate_to_core()
+    chip_end(1)
     chip_out(0)
-    chip_chain(1)
-    gate_end()
-    chip_end(2)
-    chip_end(1)
-    chip_out(2)
     chip_out(1)
     gain_end()
     for i in range(len(sent) - SEND_RING, len(sent)):

time: 136 us -> 133 us (0.978)
  Pallas kernels: 134 us -> 132 us
    pallas_call x1, Pallas kernels: 132 us -> 130 us  [fused_device(): pl.pallas_call(layer_kernel, out_shape=out_shape, in_specs=[in_vmem] * le...]
where the time goes in v5:
time: 133 us
  Pallas kernels  132 us (99%)
    pallas_call x1, Pallas kernels, fused_device(): pl.pallas_call(layer_kernel, out_shape=out_shape, in_specs=[in_vmem] * le...  130 us

profile of v5, /device:TPU:0, one launch (start us, length us, event | category | flops | bytes accessed | tf_op | source)
XLA Modules:
  0.0 133.3 jit_solution(13318893285264355329)
XLA Ops:
  0.6 130.0 %layer.1 = (bf16[128,768]{1,0:T(8,128)(2,1)}, bf16[128,768]{1,0:T(8,128)(2,1)}, f32[1,24]{1,0:T(1,128)}, f32[24,768]{1,0:T(8,128)}, f32[24,768]{1,0:T(8,128)}, /...) custom-call(bf16[128,768]{1,0:T(8,128)(2,1)} %bitcast.12, ...), custom_call_target="tpu_custom_call" | custom-call | tf_op jit(solution)/shard_map/layer/pallas_call | solution.py:1398
  130.7 2.4 %finish.1 = (bf16[128,768]{1,0:T(8,128)(2,1)}, bf16[128,768]{1,0:T(8,128)(2,1)}, f32[1,24]{1,0:T(1,128)}, f32[24,768]{1,0:T(8,128)}, f32[24,768]{1,0:T(8,128)}, ...) custom-call(bf16[128,768]{1,0:T(8,128)(2,1)} %get-tuple-element.36.r, ...), custom_call_target="tpu_custom_call" | custom-call | tf_op jit(solution)/shard_map/finish/pallas_call | solution.py:1410

commit v6 on v5

--- a/solution.py
+++ b/solution.py
@@ -532,10 +532,10 @@
     TZ=((ZS, 8, 128), F32),
     TO=((CS, 8, 128), F32),
 )
-SEND_RING = 72
+SEND_RING = 64
 SLOTS = dict(
-    segc=1, wc=1, u=1, xz=4, xx=4, xc=8, wz=4 * CHUNKS, wx=4 * CHUNKS, wy=4 * CHUNKS, wr=CHUNKS, woc=1,
-    gz=8, gy=8, dz=4, dy=4, cotx=1, cotc=2, att=2, n2x=1, n2c=2, mxc=2, mxx=1, e2c=2, e2x=1,
+    segc=1, wc=1, u=1, xz=4, xx=4, xc=8, wz=4 * CHUNKS, wx=CHUNKS, wy=CHUNKS, wr=CHUNKS, woc=1,
+    gz=8, gy=1, dz=4, dy=1, cotx=1, cotc=2, att=2, n2x=1, n2c=2, mxc=2, mxx=1, e2c=2, e2x=1,
     rdy=4, rdz=4, rdc=1, rgy=4, rgz=4, rgc=1, f4x=1, f4=1, db=1,
     ra1=2 * CHUNKS, ra2=CHUNKS, raz=4 * CHUNKS, rac=CHUNKS, f2=CHUNKS,
     dnc=4, dnx=4, dnz=4, dnt=1, ty=1, tx=1, tz=4, tc=1,
@@ -704,8 +704,8 @@
     def weight_start(ch):
         own = weight(ch).at[z, x, y]
         z_send(own, own, k.wz + 4 * ch, SPREAD_CHIP[ch])
-        put(own, own, to_y, k.wy + 4 * ch + z)
-        put(own, own, to_x, k.wx + 4 * ch + z)
+        put(own, own, to_y, k.wy + ch)
+        put(own, own, to_x, k.wx + ch)
 
     def norm_block(q, zz, xx, own=False):
         value = unit_rows(r.X[q, zz, xx].astype(F32))[0].astype(BF16)
@@ -756,16 +756,15 @@
         w = weight(ch)
         z_take(lambda zz: w.at[zz, x, y], k.wz + 4 * ch, i, SPREAD_CHIP[ch])
         arrived = w.at[zord[i], x, y]
-        put(arrived, arrived, to_y, k.wy + 4 * ch + zord[i])
-        put(arrived, arrived, to_x, k.wx + 4 * ch + zord[i])
+        put(arrived, arrived, to_y, k.wy + ch)
+        put(arrived, arrived, to_x, k.wx + ch)
 
     def weight_relay(ch):
         w = weight(ch)
-        for zz in [z] + zord:
-            if RELAY_TO_Y[ch]:
-                take(w.at[zz, xo, y], k.wx + 4 * ch + zz)
-            else:
-                take(w.at[zz, x, yo], k.wy + 4 * ch + zz)
+        if RELAY_TO_Y[ch]:
+            take(w.at[:, xo, y], k.wx + ch)
+        else:
+            take(w.at[:, x, yo], k.wy + ch)
         if RELAY_TO_Y[ch]:
             put(w.at[:, xo, y], w.at[:, xo, y], to_y, k.wr + ch)
         else:
@@ -773,33 +772,32 @@
 
     def weight_end(ch):
         w = weight(ch)
-        for zz in [z] + zord:
-            if RELAY_TO_Y[ch]:
-                take(w.at[zz, x, yo], k.wy + 4 * ch + zz)
-            else:
-                take(w.at[zz, xo, y], k.wx + 4 * ch + zz)
+        if RELAY_TO_Y[ch]:
+            take(w.at[:, x, yo], k.wy + ch)
+        else:
+            take(w.at[:, xo, y], k.wx + ch)
         take(w.at[:, xo, yo], k.wr + ch)
 
     def gate_send(xx):
         own = r.WG.at[z, xx, y]
         z_send(own, own, k.gz + 4 * xx, SPREAD_GATE)
-        put(own, own, to_y, k.gy + 4 * xx + z)
+        put(own, own, to_y, k.gy)
 
     def gate_from_z(xx, i):
         z_take(lambda zz: r.WG.at[zz, xx, y], k.gz + 4 * xx, i, SPREAD_GATE)
         arrived = r.WG.at[zord[i], xx, y]
-        put(arrived, arrived, to_y, k.gy + 4 * xx + zord[i])
+        put(arrived, arrived, to_y, k.gy)
 
     def down_from_z(i):
         z_take(lambda zz: r.WD.at[zz, y], k.dz, i, SPREAD_DOWN)
-        put(r.WD.at[zord[i], y], r.WD.at[zord[i], y], to_y, k.dy + zord[i])
+        put(r.WD.at[zord[i], y], r.WD.at[zord[i], y], to_y, k.dy)
 
     def tokens_send(i):
         far = beside if i == 2 and not SPREAD_TOKEN else None
         put(tok, r.X.at[c, z, x], to_z[i], k.xz + z, when=far)
 
     def down_send():
-        put(r.wd, r.WD.at[z, y], to_y, k.dy + z)
+        put(r.wd, r.WD.at[z, y], to_y, k.dy)
         z_send(r.wd, r.WD.at[z, y], k.dz, SPREAD_DOWN)
 
     def shards():
@@ -952,10 +950,8 @@
     put(r.N2.at[x, c], r.N2.at[x, c], to_core, k.n2c + 0)
     put(r.N2.at[x, c], r.N2.at[x, c], to_x, k.n2x)
 
-    for zz in [z] + zord:
-        for xx in range(XS):
-            take(r.WG.at[zz, xx, yo], k.gy + 4 * xx + zz)
-        take(r.WD.at[zz, yo], k.dy + zz)
+    take(r.WG.at[:, :, yo], k.gy)
+    take(r.WD.at[:, yo], k.dy)
     take(r.COT.at[x, co], k.cotc + 0)
     take(r.COT.at[xo, co], k.cotc + 1)
     take(r.N2.at[x, co], k.n2c + 0)

time: 133 us -> 133 us (level)
  no operation moved by 1% of the time
where the time goes in v6:
time: 133 us
  Pallas kernels  132 us (99%)
    pallas_call x1, Pallas kernels, fused_device(): pl.pallas_call(layer_kernel, out_shape=out_shape, in_specs=[in_vmem] * le...  129 us

profile of v6, /device:TPU:0, one launch (start us, length us, event | category | flops | bytes accessed | tf_op | source)
XLA Modules:
  0.0 132.7 jit_solution(9672392810659342012)
XLA Ops:
  0.6 129.5 %layer.1 = (bf16[128,768]{1,0:T(8,128)(2,1)}, bf16[128,768]{1,0:T(8,128)(2,1)}, f32[1,24]{1,0:T(1,128)}, f32[24,768]{1,0:T(8,128)}, f32[24,768]{1,0:T(8,128)}, /...) custom-call(bf16[128,768]{1,0:T(8,128)(2,1)} %bitcast.12, ...), custom_call_target="tpu_custom_call" | custom-call | tf_op jit(solution)/shard_map/layer/pallas_call | solution.py:1394
  130.1 2.4 %finish.1 = (bf16[128,768]{1,0:T(8,128)(2,1)}, bf16[128,768]{1,0:T(8,128)(2,1)}, f32[1,24]{1,0:T(1,128)}, f32[24,768]{1,0:T(8,128)}, f32[24,768]{1,0:T(8,128)}, ...) custom-call(bf16[128,768]{1,0:T(8,128)(2,1)} %get-tuple-element.36.r, ...), custom_call_target="tpu_custom_call" | custom-call | tf_op jit(solution)/shard_map/finish/pallas_call | solution.py:1406
